TPU v7x, 256 devices: a whole 4x4x8 slice. The times are simulated.
256 devices in a mesh: rows: 64 (over z, x, core), proj: 4 (over y).
Axes of the slice: x: 4, y: 4, z: 8, core: 2. Of those that a mesh axis runs over, the one named last changes fastest.
Arguments:
- q_nope: bfloat16 [4096, 8192], P('rows', 'proj'), may hold values from -6 to 6
- q_rope: bfloat16 [4096, 4096], P('rows', 'proj')
- w_uk: bfloat16 [64, 128, 512], P(None, None, 'proj'), may hold values from -0.5 to 0.5
- w_uv: bfloat16 [64, 128, 512], P(None, None, 'proj'), may hold values from -0.25 to 0.25
- prefix_latent: bfloat16 [128, 128, 512], P('rows'), may hold values from -6 to 6
- prefix_rope: bfloat16 [128, 8192], P('rows'), may hold values from -6 to 6
- suffix_latent: bfloat16 [4096, 64, 512], P('rows'), may hold values from -6 to 6
- suffix_rope: bfloat16 [4096, 4096], P('rows')
- page_slot: int32 [128], replicated, may hold values from 0 to 127, each once
- page_pattern: int32 [4096, 2], P('rows'), may hold values from 0 to 127, all different within a row; in each aligned block of 64 rows (0 to 63, 64 to 127, ...) at most 2 rows name the same one
- suffix_len: int32 [4096], P('rows'), may hold values from 1 to 64, 131072 in all
Outputs:
- attended: bfloat16 [4096, 8192], P('rows', 'proj')
Inputs may be any that keep to these rules, and one draw needn't show every extreme that they name: Page p is stored at slot page_slot[p]; slots 2 * d to 2 * d + 1 lie on index d of rows. `page_pattern`: each row names 2 different pages. Among the rows of one device no page is named by more than 2 rows, and in some aligned blocks of 64 rows one page is named by exactly 2 rows. `suffix_len`: some row has all 64 slots live.
All inputs are finite; a program needn't handle non-finite values. No bound on the sum of `suffix_len` on one device may be relied on, other than what follows from the above.
Results may differ from a plain program's by a relative error of at most 0.011.
Values may be sent and summed in bfloat16 or wider, within the bound.
No kernel may reach another device: no remote copies, remote signals or barrier semaphores. Data moves between devices by JAX's collectives and lax.ppermute only.
A program may use at most 128 MiB of HBM per device.

v0:
```python
import jax
import jax.numpy as jnp
from jax import lax
from jax.sharding import PartitionSpec as P


def partial_attention(queries, query_rope, latents, rope_keys, visible, score_scale):
    scores = jnp.einsum("bgc,btc->bgt", queries, latents, preferred_element_type=jnp.float32)
    scores = scores + jnp.einsum(
        "bge,bte->bgt", query_rope, rope_keys, preferred_element_type=jnp.float32
    )
    scores = scores * score_scale
    scores = jnp.where(visible[:, None, :], scores, jnp.float32(-1e30))
    maxima = jnp.max(scores, axis=2, keepdims=True)
    raw_weights = jnp.exp(scores - maxima)
    totals = jnp.sum(raw_weights, axis=2)
    rounded = raw_weights.astype(jnp.bfloat16)
    summed = jnp.einsum("bgt,btc->bgc", rounded, latents, preferred_element_type=jnp.float32)
    result = (summed / totals[:, :, None]).astype(jnp.bfloat16)
    return (result, maxima[:, :, 0] + jnp.log(totals))


def combine_blocks(results, log_totals):
    stacked_logs = jnp.stack(log_totals)
    highest = jnp.max(stacked_logs, axis=0)
    factors = jnp.exp(stacked_logs - highest)
    summed = jnp.sum(factors[..., None] * jnp.stack(results).astype(jnp.float32), axis=0)
    return (summed / jnp.sum(factors, axis=0)[..., None]).astype(jnp.bfloat16)


def shards(
    q_nope,
    q_rope,
    w_uk,
    w_uv,
    prefix_latent,
    prefix_rope,
    suffix_latent,
    suffix_rope,
    page_slot,
    page_pattern,
    suffix_len,
):
    rows_here = q_nope.shape[0]
    head_total = w_uk.shape[0]
    nope_size = w_uk.shape[1]
    value_size = w_uv.shape[1]
    proj_count = lax.axis_size("proj")
    head_count = head_total // proj_count
    rope_size = q_rope.shape[1] // head_count
    suffix_slots = suffix_latent.shape[1]
    owned_pages = prefix_latent.shape[0]
    page_len = prefix_latent.shape[1]
    pages_read = page_pattern.shape[1]
    row_devices = lax.axis_size("rows")
    page_total = owned_pages * row_devices
    score_scale = (nope_size + rope_size) ** (-0.5)
    w_uk_mine, w_uv_mine = (
        lax.all_to_all(w_uk, "proj", split_axis=0, concat_axis=2, tiled=True),
        lax.all_to_all(w_uv, "proj", split_axis=0, concat_axis=2, tiled=True),
    )
    nope_rows = q_nope.reshape(rows_here, head_count, nope_size)
    rope_rows = q_rope.reshape(rows_here, head_count, rope_size)
    queries = jnp.einsum(
        "rhd,hdc->rhc", nope_rows, w_uk_mine, preferred_element_type=jnp.float32
    ).astype(jnp.bfloat16)
    visible = jnp.arange(suffix_slots, dtype=jnp.int32)[None, :] < suffix_len[:, None]
    own_rope = suffix_rope.reshape(rows_here, suffix_slots, rope_size)
    result, log_total = partial_attention(
        queries, rope_rows, suffix_latent, own_rope, visible, score_scale
    )
    results = [result]
    log_totals = [log_total]
    pattern_flat = page_pattern.reshape(-1)
    slot_match = pattern_flat[:, None] == jnp.arange(page_total, dtype=jnp.int32)[None, :]
    slots_flat = jnp.sum(jnp.where(slot_match, page_slot[None, :], 0), axis=1)
    all_latent, all_rope = (
        lax.all_gather(prefix_latent, "rows", axis=0, tiled=True),
        lax.all_gather(prefix_rope, "rows", axis=0, tiled=True),
    )
    all_rope = all_rope.reshape(page_total, page_len, rope_size)
    chosen_slots = slots_flat.reshape(rows_here, pages_read)
    everywhere = jnp.ones((rows_here, page_len), dtype=bool)
    for column in range(pages_read):
        picked = chosen_slots[:, column]
        result, log_total = partial_attention(
            queries, rope_rows, all_latent[picked], all_rope[picked], everywhere, score_scale
        )
        results.append(result)
        log_totals.append(log_total)
    mixed = combine_blocks(results, log_totals)
    final = jnp.einsum("rhc,hvc->rhv", mixed, w_uv_mine, preferred_element_type=jnp.float32).astype(
        jnp.bfloat16
    )
    return final.reshape(rows_here, head_count * value_size)


def solution(mesh):
    return jax.shard_map(
        shards,
        mesh=mesh,
        in_specs=(
            P("rows", "proj"),
            P("rows", "proj"),
            P(None, None, "proj"),
            P(None, None, "proj"),
            P("rows", None, None),
            P("rows", None),
            P("rows", None, None),
            P("rows", None),
            P(),
            P("rows", None),
            P("rows"),
        ),
        out_specs=P("rows", "proj"),
        check_vma=False,
    )
```

profile of v0, /device:TPU:1, one launch (start us, length us, event | category | flops | bytes accessed | tf_op | source)
XLA Modules:
  0.0 242.9 jit_solution(10257325399327589432)
XLA Ops:
  6.5 0.7 all-gather.6.cloned.1.call-update
  7.3 0.7 all-gather.4.cloned.1.call-update
  8.0 29.2 %all_to_all.36 = bf16[64,128,128]{2,1,0:T(8,128)(2,1)} all-to-all(bf16[64,128,128]{2,1,0:T(8,128)(2,1)} %param.14), channel_id=1, replica_groups=mesh['rows'=64,'proj'=4] {'proj'}, dimensions={0} | all-to-all | bytes 4194304 | tf_op jit(solution)/shard_map/all_to_all | solution.py:60
  37.2 3.8 %all-to-all-start = ((bf16[64,128,128]{2,1,0:T(8,128)(2,1)}), bf16[64,128,128]{2,1,0:T(8,128)(2,1)S(1)}, u32[]{:S(2)}, u32[]{:S(2)}) async-start(bf16[64,128,128]{2,1,0:T(8,128)(2,1)} %param.13), calls=%async_computation | async-start | bytes 4194304 | tf_op jit(solution)/shard_map/all_to_all | solution.py:59
  41.6 0.9 reshape.139
  42.5 2.1 reshape.140
  44.8 4.7 %copy.104 = bf16[4,16,128,128]{3,0,2,1:T(4,128)(2,1)} copy(bf16[4,16,128,128]{3,2,1,0:T(8,128)(2,1)} %bitcast.55) | data formatting | bytes 4194304 | tf_op jit(solution)/shard_map/all_to_all | solution.py:60
  49.5 4.1 %all_to_all.33 = bf16[16,128,512]{2,1,0:T(8,128)(2,1)} reshape(bf16[16,128,4,128]{3,2,1,0:T(4,128)(2,1)} %bitcast.56) | data formatting | bytes 4194304 | tf_op jit(solution)/shard_map/all_to_all | solution.py:60
  53.7 10.3 %all-to-all-done = bf16[64,128,128]{2,1,0:T(8,128)(2,1)S(1)} async-done(((bf16[64,128,128]{2,1,0:T(8,128)(2,1)}), bf16[64,128,128]{2,1,0:T(8,128)(2,1)S(1)}, u32[]{:S(2)}, u32[]{:S(2)}) %all-to-all-start) | async-done | bytes 2097184 | tf_op jit(solution)/shard_map/all_to_all | solution.py:59
  64.0 3.1 %copy.105 = bf16[4,16,128,128]{3,0,2,1:T(4,128)(2,1)} copy(bf16[4,16,128,128]{3,2,1,0:T(8,128)(2,1)S(1)} %bitcast.54) | data formatting | bytes 4194304 | tf_op jit(solution)/shard_map/all_to_all | solution.py:59
  67.1 2.8 %all_to_all.29 = bf16[16,128,512]{2,1,0:T(8,128)(2,1)S(1)} reshape(bf16[16,128,4,128]{3,2,1,0:T(4,128)(2,1)} %bitcast.57) | data formatting | bytes 4194304 | tf_op jit(solution)/shard_map/all_to_all | solution.py:59
  69.8 0.4 fusion
  70.3 3.6 %fusion.12 = f32[64,16,64]{2,1,0:T(8,128)S(1)} fusion(bf16[64,64,512]{2,1,0:T(8,128)(2,1)} %param.17, bf16[64,16,512]{2,0,1:T(8,128)(2,1)S(1)} %fusion), kind=kOutput, calls=%fused_computation.30 | convolution fusion | flops 67108864 | bytes 5505024 | tf_op jit(solution)/shard_map/bgc,btc->bgt/dot_general | solution.py:8
  73.9 0.7 fusion.38
  75.0 1.7 fusion.1
  76.7 14.8 %all-gather.6.cloned.1.call-done = bf16[64,2,8192]{2,1,0:T(2,128)(2,1)} async-done(((bf16[1,2,8192]{2,1,0:T(2,128)(2,1)}), bf16[64,2,8192]{2,1,0:T(2,128)(2,1)}) %all-gather.6.cloned.1.call-update) | async-done | bytes 2097168 | tf_op jit(solution)/shard_map/all_gather | solution.py:79
  91.6 7.9 %reshape.142 = bf16[128,128,64]{2,1,0:T(8,128)(2,1)} reshape(bf16[64,2,8192]{2,1,0:T(2,128)(2,1)} %all-gather.6.cloned.1.call-done) | data formatting | bytes 4194304 | tf_op jit(solution)/shard_map/reshape | solution.py:81
  99.5 3.7 %copy.70 = bf16[128,128,64]{1,2,0:T(8,128)(2,1)S(1)} copy(bf16[128,128,64]{2,1,0:T(8,128)(2,1)} %reshape.142) | data formatting | bytes 4194304 | tf_op jit(solution)/shard_map/reshape | solution.py:81
  103.2 1.7 gather_fusion.3
  104.9 1.7 gather_fusion.1
  106.6 1.6 convolution_bitcast_fusion
  108.2 1.6 convolution_bitcast_fusion.1
  109.8 82.0 %all-gather.4.cloned.1.call-done = bf16[128,128,512]{2,1,0:T(8,128)(2,1)} async-done(((bf16[2,128,512]{2,1,0:T(8,128)(2,1)}), bf16[128,128,512]{2,1,0:T(8,128)(2,1)}) %all-gather.4.cloned.1.call-update) | async-done | bytes 16777232 | tf_op jit(solution)/shard_map/all_gather | solution.py:78
  191.8 11.3 %gather_fusion.2 = bf16[64,128,512]{2,1,0:T(8,128)(2,1)} fusion(bf16[128,128,512]{2,1,0:T(8,128)(2,1)} %all-gather.4.cloned.1.call-done, s32[1024]{0:T(1024)S(1)} %get-tuple-element.19), kind=kCustom, calls=%fused_computation.2 | custom fusion | bytes 16777472 | tf_op jit(solution)/shard_map/gather | solution.py:87
  203.1 5.9 %fusion.36 = (f32[64,16]{1,0:T(8,128)S(1)}, f32[64,16,128]{2,1,0:T(8,128)S(1)}) fusion(f32[64,16,128]{2,1,0:T(8,128)S(1)} %convolution_bitcast_fusion, bf16[64,128,512]{2,1,0:T(8,128)(2,1)} %gather_fusion.2, bf16[64,16,512]{2,0,1:T(8,128)(2,1)S(1)} %fusion), kind=kOutput, calls=%fused_computation.66 | convolution fusion | flops 134609920 | bytes 10489856 | tf_op jit(solution)/shard_map/bgc,btc->bgt/dot_general | solution.py:8
  209.4 2.2 fusion.3
  211.6 11.3 %gather_fusion = bf16[64,128,512]{2,1,0:T(8,128)(2,1)} fusion(bf16[128,128,512]{2,1,0:T(8,128)(2,1)} %all-gather.4.cloned.1.call-done, s32[1024]{0:T(1024)S(1)} %get-tuple-element.20), kind=kCustom, calls=%fused_computation | custom fusion | bytes 16777472 | tf_op jit(solution)/shard_map/gather | solution.py:87
  222.9 5.9 %fusion.37 = (f32[64,16]{1,0:T(8,128)S(1)}, f32[64,16,128]{2,1,0:T(8,128)S(1)}) fusion(f32[64,16,128]{2,1,0:T(8,128)S(1)} %convolution_bitcast_fusion.1, bf16[64,128,512]{2,1,0:T(8,128)(2,1)} %gather_fusion, bf16[64,16,512]{2,0,1:T(8,128)(2,1)S(1)} %fusion), kind=kOutput, calls=%fused_computation.67 | convolution fusion | flops 134609920 | bytes 10489856 | tf_op jit(solution)/shard_map/bgc,btc->bgt/dot_general | solution.py:8
  229.2 2.3 fusion.2
  232.1 2.1 multiply_reduce_fusion
  234.4 0.8 fusion.8
  235.3 0.8 copy.106
  (51 shorter events, 2.8 us)
Async XLA Ops:
  6.5 63.3 %copy-start = (bf16[64,2048]{1,0:T(8,128)(2,1)S(1)}, bf16[64,2048]{1,0:T(8,128)(2,1)}, u32[]{:S(2)}) copy-start(bf16[64,2048]{1,0:T(8,128)(2,1)} %param.11) | copy-start | bytes 786436
  6.5 85.0 %all-gather.6.cloned.1.call-start = ((), (), s32[]{:S(2)}) async-start(), calls=%async_computation.3 | async-start | bytes 2129920 | tf_op jit(solution)/shard_map/all_gather | solution.py:79
  7.3 184.5 %all-gather.4.cloned.1.call-start = ((), (), s32[]{:S(2)}) async-start(), calls=%async_computation.2 | async-start | bytes 17039360 | tf_op jit(solution)/shard_map/all_gather | solution.py:78
  8.0 33.0 %copy-start.12 = (s32[64,2]{0,1:T(2,128)S(1)}, s32[64,2]{0,1:T(2,128)}, u32[]{:S(2)}) copy-start(s32[64,2]{0,1:T(2,128)} %param.20) | copy-start | bytes 1540
  37.2 4.0 %copy-start.14 = (s32[128]{0:T(128)S(1)}, s32[128]{0:T(128)}, u32[]{:S(2)}) copy-start(s32[128]{0:T(128)} %param.19) | copy-start | bytes 1540
  37.2 4.4 %copy-start.11 = (bf16[64,1024]{1,0:T(8,128)(2,1)S(1)}, bf16[64,1024]{1,0:T(8,128)(2,1)}, u32[]{:S(2)}) copy-start(bf16[64,1024]{1,0:T(8,128)(2,1)} %param.12) | copy-start | bytes 393220
  37.2 5.3 %copy-start.10 = (bf16[64,4096]{1,0:T(8,128)(2,1)S(1)}, bf16[64,4096]{1,0:T(8,128)(2,1)}, u32[]{:S(2)}) copy-start(bf16[64,4096]{1,0:T(8,128)(2,1)} %param.18) | copy-start | bytes 1572868
  37.2 7.5 %copy-start.13 = (s32[64]{0:T(128)S(1)}, s32[64]{0:T(128)}, u32[]{:S(2)}) copy-start(s32[64]{0:T(128)} %param.21) | copy-start | bytes 772
  37.2 26.7 %all-to-all-start = ((bf16[64,128,128]{2,1,0:T(8,128)(2,1)}), bf16[64,128,128]{2,1,0:T(8,128)(2,1)S(1)}, u32[]{:S(2)}, u32[]{:S(2)}) async-start(bf16[64,128,128]{2,1,0:T(8,128)(2,1)} %param.13), calls=%async_computation | async-start | bytes 4194304 | tf_op jit(solution)/shard_map/all_to_all | solution.py:59
  70.3 3.6 %copy-start.5 = (bf16[64,16,64]{2,1,0:T(8,128)(2,1)S(1)}, bf16[64,16,64]{2,1,0:T(8,128)(2,1)}, u32[]{:S(2)}) copy-start(bf16[64,16,64]{2,1,0:T(8,128)(2,1)} %reshape.139) | copy-start | bytes 393220
  70.3 3.6 %copy-start.6 = (bf16[64,64,64]{2,1,0:T(8,128)(2,1)S(1)}, bf16[64,64,64]{2,1,0:T(8,128)(2,1)}, u32[]{:S(2)}) copy-start(bf16[64,64,64]{2,1,0:T(8,128)(2,1)} %reshape.140) | copy-start | bytes 1572868
  70.3 4.7 %copy-start.7 = (bf16[64,64,512]{2,1,0:T(8,128)(2,1)S(1)}, bf16[64,64,512]{2,1,0:T(8,128)(2,1)}, u32[]{:S(2)}) copy-start(bf16[64,64,512]{2,1,0:T(8,128)(2,1)} %param.17) | copy-start | bytes 12582916
  203.1 6.3 %copy-start.3 = (bf16[64,128,512]{2,1,0:T(8,128)(2,1)S(1)}, bf16[64,128,512]{2,1,0:T(8,128)(2,1)}, u32[]{:S(2)}) copy-start(bf16[64,128,512]{2,1,0:T(8,128)(2,1)} %gather_fusion.2) | copy-start | bytes 25165828
  222.9 6.3 %copy-start.2 = (bf16[64,128,512]{2,1,0:T(8,128)(2,1)S(1)}, bf16[64,128,512]{2,1,0:T(8,128)(2,1)}, u32[]{:S(2)}) copy-start(bf16[64,128,512]{2,1,0:T(8,128)(2,1)} %gather_fusion) | copy-start | bytes 25165828
  229.2 2.8 %copy-start.8 = (bf16[1,64,16,512]{3,2,1,0:T(8,128)(2,1)S(1)}, bf16[1,64,16,512]{3,2,1,0:T(8,128)(2,1)}, u32[]{:S(2)}) copy-start(bf16[1,64,16,512]{3,2,1,0:T(8,128)(2,1)} %fusion.1) | copy-start | bytes 3145732
  229.2 2.8 %copy-start.9 = (bf16[1,64,16,512]{3,2,1,0:T(8,128)(2,1)S(1)}, bf16[1,64,16,512]{3,2,1,0:T(8,128)(2,1)}, u32[]{:S(2)}) copy-start(bf16[1,64,16,512]{3,2,1,0:T(8,128)(2,1)} %fusion.3) | copy-start | bytes 3145732
  232.0 2.4 copy-start.4
  232.0 4.0 %copy-start.1 = (bf16[64,2048]{1,0:T(8,128)(2,1)S(1)}, bf16[64,2048]{1,0:T(8,128)(2,1)}, u32[]{:S(2)}) copy-start(bf16[64,2048]{1,0:T(8,128)(2,1)} %param.11) | copy-start | bytes 786436
Sparse Core Ops, SparseCore 0:
  10.1 81.4 all-gather.5
  94.3 97.4 all-gather.3
where the time goes:
time: 244 us; the launch traced here: 243 us
  waiting for transfers between devices  109 us (45%)
  local copies, waits for them, and re-layouts  56.9 us (23%)
  blocking collectives  29.2 us (12%)
  matrix products  26.8 us (11%)
  between operations  13.7 us (6%)
  other arithmetic  4.01 us (2%)
  starting transfers between devices  3.79 us (2%)
    all_gather x1, waiting for transfers between devices, shards(): lax.all_gather(prefix_latent, 'rows', axis=0, tiled=True)  82 us
    all_to_all x1, blocking collectives, shards(): lax.all_to_all(w_uv, 'proj', split_axis=0, concat_axis=2, tiled=True)  29.2 us
    gather x2, local copies, waits for them, and re-layouts, shards(): all_latent[picked]  22.6 us
    dot_general x3, matrix products, partial_attention(): jnp.einsum('bgc,btc->bgt', queries, latents, preferred_element_type=jnp.f...  15.3 us
    all_gather x1, waiting for transfers between devices, shards(): lax.all_gather(prefix_rope, 'rows', axis=0, tiled=True)  14.8 us
    reshape x2, local copies, waits for them, and re-layouts, shards(): all_rope = all_rope.reshape(page_total, page_len, rope_size)  11.6 us
    all_to_all x1, waiting for transfers between devices, shards(): lax.all_to_all(w_uk, 'proj', split_axis=0, concat_axis=2, tiled=True)  10.3 us
    all_to_all x2, local copies, waits for them, and re-layouts, shards(): lax.all_to_all(w_uv, 'proj', split_axis=0, concat_axis=2, tiled=True)  8.81 us
  transfers between devices with their start and end apart: 3, of which 3 were waited for; matrix products, arithmetic and copies ran while one was open for 15% of the time, Pallas kernels for 0%

commit v1 on v0

v1 whole, which is shorter than its diff:
```python
import functools

import jax
import jax.numpy as jnp
from jax import lax
from jax.experimental import pallas as pl
from jax.experimental.pallas import tpu as pltpu
from jax.sharding import PartitionSpec as P

F32, BF16, I32 = jnp.float32, jnp.bfloat16, jnp.int32
LOW = -1e30

NZ, NX, NC, NY = 8, 4, 2, 4
HEADS = 16
ROWS = 64
NOPE = 128
VDIM = 128
ROPE = 64
KVL = 512
PAGE = 128
SUF = 64
UNIT = PAGE + PAGE * ROPE // KVL
QN = HEADS * NOPE
QR = HEADS * ROPE
PAY = QN + QR + 128
SLOTS = 256
PAIRS = 16
EARLY = 10
LATE = PAIRS - EARLY
SCALE = (NOPE + ROPE) ** -0.5
OUT = HEADS * VDIM
RET = OUT + 128
LAST = (((1,), (1,)), ((), ()))
FIRST = (((0,), (0,)), ((), ()))


def dot(a, b, dims=(((1,), (0,)), ((), ())), precision=None):
    return lax.dot_general(a, b, dims, preferred_element_type=F32, precision=precision)


def iota(shape, axis):
    return lax.broadcasted_iota(I32, shape, axis)


def params(mib):
    return pltpu.CompilerParams(vmem_limit_bytes=mib << 20)


VMEM = pl.BlockSpec(memory_space=pltpu.VMEM)
SMEM = pl.BlockSpec(memory_space=pltpu.SMEM)
ANY = pl.BlockSpec(memory_space=pl.ANY)


def prep_kernel(
    place, pattern, page_slot, latent, rope, q_nope, q_rope, w_uk, w_uv, pages, pay, ka, kb, va, vb, sems
):
    core, y = place[2], place[3]
    head_a = lax.rem(y + 1 + 2 * core, NY) * HEADS
    head_b = lax.rem(y + 2, NY) * HEADS + (HEADS // 2) * core
    copies = [
        pltpu.make_async_copy(w_uk.at[pl.ds(head_a, HEADS)], ka, sems.at[0]),
        pltpu.make_async_copy(w_uk.at[pl.ds(head_b, HEADS // 2)], kb, sems.at[1]),
        pltpu.make_async_copy(w_uv.at[pl.ds(head_a, HEADS)], va, sems.at[2]),
        pltpu.make_async_copy(w_uv.at[pl.ds(head_b, HEADS // 2)], vb, sems.at[3]),
    ]
    for copy in copies:
        copy.start()
    pages[:, :PAGE, :] = latent[...]
    flat = rope[...].astype(F32)
    half = PAGE // 2
    sub = iota((8, 128), 0)
    even = (iota((half, PAGE), 1) == 2 * iota((half, PAGE), 0)).astype(F32)
    odd = (iota((half, PAGE), 1) == 2 * iota((half, PAGE), 0) + 1).astype(F32)
    for page in range(2):
        tiles = []
        for tile in range(half // 8):
            piece = jnp.zeros((8, 128), F32)
            for row in range(8):
                at = (tile * 8 + row) * 128
                piece = jnp.where(sub == row, flat[page : page + 1, at : at + 128], piece)
            tiles.append(piece)
        two_tokens = jnp.concatenate(tiles, axis=0)
        turned = dot(two_tokens[:, :ROPE], even, FIRST) + dot(two_tokens[:, ROPE:], odd, FIRST)
        turned = jnp.concatenate([turned[16 * i : 16 * i + 16] for i in range(4)], axis=1)
        pages[page, PAGE:, :] = turned.astype(BF16)
    pay[:, :QN] = q_nope[...]
    pay[:, QN : QN + QR] = q_rope[...]
    lane = iota((ROWS, 128), 1)
    slot_row = page_slot[...].astype(F32)
    slots, owners = [], []
    for k in range(2):
        named = lane == pattern[:, k : k + 1]
        slot = jnp.sum(jnp.where(named, slot_row, 0.0), axis=1, keepdims=True)
        slots.append(slot)
        owners.append((lane == lax.shift_right_logical(slot.astype(I32), 1)).astype(F32))
    below = (iota((ROWS, ROWS), 0) > iota((ROWS, ROWS), 1)).astype(F32)
    before0 = dot(below, owners[0])
    before1 = dot(below, owners[1]) + jnp.sum(owners[0], axis=0, keepdims=True)
    rank0 = jnp.sum(owners[0] * before0, axis=1, keepdims=True)
    rank1 = jnp.sum(owners[1] * before1, axis=1, keepdims=True)
    code = jnp.zeros((ROWS, 128), F32)
    for at, value in enumerate((slots[0], slots[1], rank0, rank1)):
        code = jnp.where(lane == at, value, code)
    pay[:, QN + QR :] = code.astype(BF16)
    for copy in copies:
        copy.wait()


def gather_weights(place, full, a, a_swap, b, b_swap, whole, sems):
    core, y = place[2], place[3]

    def lanes(which):
        return pl.ds(pl.multiple_of(lax.rem(which, NY) * 128, 128), 128)

    half = HEADS // 2
    copies = [
        pltpu.make_async_copy(full.at[pl.ds(y * HEADS, HEADS)], whole.at[:, :, lanes(y)], sems.at[0]),
        pltpu.make_async_copy(a, whole.at[:, :, lanes(y + 3 - 2 * core)], sems.at[1]),
        pltpu.make_async_copy(a_swap, whole.at[:, :, lanes(y + 1 + 2 * core)], sems.at[2]),
        pltpu.make_async_copy(b, whole.at[pl.ds(half * core, half), :, lanes(y + 2)], sems.at[3]),
        pltpu.make_async_copy(b_swap, whole.at[pl.ds(half * (1 - core), half), :, lanes(y + 2)], sems.at[4]),
    ]
    for copy in copies:
        copy.start()
    return copies


def query_kernel(
    place, p0, p1, p2, p3, w_uk, ka, ka_swap, kb, kb_swap, q_lat, q_rot, own_lat, own_rot, page_bit, slot_of, whole, turned, sems
):
    copies = gather_weights(place, w_uk, ka, ka_swap, kb, kb_swap, whole, sems)
    z, x, core = place[0], place[1], place[2]
    pays = (p0, p1, p2, p3)
    lane = iota((ROWS, 128), 1)
    wide = iota((ROWS, SLOTS), 1)
    picks, bits, places = ([], []), ([], []), []
    for peer, pay in enumerate(pays):
        code = pay[:, QN + QR :].astype(F32)
        columns = [
            jnp.sum(jnp.where(lane == at, code, 0.0), axis=1, keepdims=True).astype(I32) for at in range(4)
        ]
        noted = jnp.zeros((ROWS, 128), F32)
        for k in range(2):
            slot, rank = columns[k], columns[2 + k]
            away = (z - lax.shift_right_logical(slot, 4)) * (1 - 2 * core)
            away = lax.bitwise_and(away, NZ - 1)
            order = jnp.where(away < 3, away, jnp.where(away >= 6, away - 3, away + 2))
            other = jnp.where(lax.bitwise_and(lax.shift_right_logical(slot, 1), 1) != core, 1, 0)
            here = lax.bitwise_and(lax.shift_right_logical(slot, 2), 3) == x
            at = jnp.where(here, (order * 2 + other) * 16 + peer * 4 + rank, -1)
            picks[k].append((wide == at).astype(F32))
            bits[k].append(lax.bitwise_and(slot, 1).astype(F32) * jnp.ones((1, 128), F32))
            noted = jnp.where(lane == k, at.astype(F32), noted)
        slot_of[peer * ROWS : (peer + 1) * ROWS, :] = noted
    pick = [jnp.concatenate(p, axis=0) for p in picks]
    bit = [jnp.concatenate(b, axis=0) for b in bits]
    page_bit[...] = dot(pick[0], bit[0], FIRST) + dot(pick[1], bit[1], FIRST)
    turned[...] = jnp.transpose(pick[0] + pick[1]).astype(BF16)
    for copy in copies:
        copy.wait()

    def two_heads(i, carry):
        rot = pl.ds(pl.multiple_of(QN + i * 128, 128), 128)
        gathered = dot(turned[...], jnp.concatenate([p[:, rot] for p in pays], axis=0))
        mine = p0[:, rot].astype(F32)
        for k in range(2):
            head = 2 * i + k
            q_rot[head] = gathered[:, k * ROPE : (k + 1) * ROPE].astype(BF16)
            own_rot[head] = mine[:, k * ROPE : (k + 1) * ROPE]
            at = pl.ds(pl.multiple_of(head * NOPE, 128), NOPE)
            left = dot(turned[...], jnp.concatenate([p[:, at] for p in pays], axis=0)).astype(BF16)
            left = jnp.concatenate([left, p0[:, at]], axis=0)
            latent = dot(left, whole[head]).astype(BF16)
            q_lat[head] = latent[:SLOTS]
            own_lat[head] = latent[SLOTS:].astype(F32)
        return carry

    lax.fori_loop(0, HEADS // 2, two_heads, 0)


def start_units(units, held, sems):
    copies = [pltpu.make_async_copy(unit, held.at[i], sems.at[i]) for i, unit in enumerate(units)]
    for copy in copies:
        copy.start()


def attend_units(count, base, unit0, q_lat, q_rot, page_bit, held, sems, result, logs):
    lane = iota((16, 128), 1)

    def body(i, carry):
        pltpu.make_async_copy(unit0, held.at[i], sems.at[i]).wait()
        unit = held.at[i]
        latent = unit[:, :PAGE, :].reshape(2 * PAGE, KVL)
        rot = unit[:, PAGE:, :]
        keys = jnp.concatenate(
            [
                jnp.concatenate([rot[page, :, 128 * j : 128 * j + 128] for j in range(4)], axis=0)
                for page in range(2)
            ],
            axis=1,
        )
        at = pl.ds(pl.multiple_of((base + i) * 16, 16), 16)
        query = q_lat[:, at, :].reshape(HEADS * 16, KVL)
        query_rot = q_rot[:, at, :].reshape(HEADS * 16, ROPE)
        scores = dot(query, latent, LAST) + dot(query_rot, keys)
        bit = page_bit[at, :]
        bias = jnp.concatenate(
            [jnp.where(bit < 0.5, 0.0, LOW), jnp.where(bit < 0.5, LOW, 0.0)], axis=1
        )
        scores = (scores * SCALE).reshape(HEADS, 16, 2 * PAGE) + bias[None]
        scores = scores.reshape(HEADS * 16, 2 * PAGE)
        top = jnp.max(scores, axis=1, keepdims=True)
        raw = jnp.exp(scores - top)
        total = jnp.sum(raw, axis=1, keepdims=True)
        summed = dot(raw.astype(BF16), latent) * (1.0 / total)
        out_at = pl.ds(pl.multiple_of(i * 16, 16), 16)
        result[:, out_at, :] = summed.astype(BF16).reshape(HEADS, 16, KVL)
        log = (top + jnp.log(total)).reshape(HEADS, 16, 1)
        spread = jnp.zeros((16, 128), F32)
        for head in range(HEADS):
            mine = (lax.bitwise_and(lane, 15) == head) & (lane < 48)
            spread = jnp.where(mine, log[head], spread)
        logs[out_at, :] = spread
        return carry

    lax.fori_loop(0, count, body, 0)


def early_kernel(*refs):
    units = refs[:EARLY]
    q_lat, q_rot, page_bit, result, logs, held, sems = refs[EARLY:]
    start_units(units, held, sems)
    attend_units(EARLY, 0, units[0], q_lat, q_rot, page_bit, held, sems, result, logs)


def late_kernel(*refs):
    units = refs[:LATE]
    (
        place, q_lat, q_rot, page_bit, slot_of, early, early_logs, w_uv, va, va_swap, vb, vb_swap,
        r0, r1, r2, r3, held, result, logs, whole, parts, sems, w_sems,
    ) = refs[LATE:]
    start_units(units, held, sems)
    copies = gather_weights(place, w_uv, va, va_swap, vb, vb_swap, whole, w_sems)
    attend_units(LATE, EARLY, units[0], q_lat, q_rot, page_bit, held, sems, result, logs)
    highest = lax.Precision.HIGHEST
    wide = iota((SLOTS, SLOTS), 1).astype(F32)
    at0, at1 = slot_of[:, 0:1], slot_of[:, 1:2]
    pick0, pick1 = (wide == at0).astype(F32), (wide == at1).astype(F32)
    partner = dot(pick0, pick1, FIRST) + dot(pick1, pick0, FIRST)
    has = jnp.sum(partner, axis=1, keepdims=True)
    log = jnp.concatenate([early_logs[...], logs[...]], axis=0)
    other = dot(partner, log, precision=highest) + (has - 1.0) * (-LOW)
    top = jnp.maximum(log, other)
    mine = jnp.exp(log - top)
    both = mine + jnp.exp(other - top)
    weight = mine / both
    merged = top + jnp.log(both)
    for copy in copies:
        copy.wait()
    for head in range(HEADS):
        mixed = jnp.concatenate([early[head], result[head]], axis=0)
        part = dot(mixed, whole[head], LAST) * weight[:, head : head + 1]
        parts[:, head * VDIM : (head + 1) * VDIM] = part.astype(BF16)
    first = jnp.where(at0 >= 0.0, 1.0, 0.0)
    row_log = dot(pick0 + pick1 * (1.0 - first), merged, precision=highest)
    none = (at0 < 0.0) & (at1 < 0.0)
    row_log = jnp.where(none, LOW, row_log)
    lane = iota((SLOTS, 128), 1)
    high = row_log.astype(BF16).astype(F32)
    rest = row_log - high
    middle = rest.astype(BF16).astype(F32)
    packed = jnp.where(lane < 16, high, jnp.where(lane < 32, middle, rest - middle))
    packed = jnp.where(lane < 48, packed, 0.0).astype(BF16)
    pick = (pick0 + pick1).astype(BF16)
    for peer, out in enumerate((r0, r1, r2, r3)):
        rows = slice(peer * ROWS, (peer + 1) * ROWS)
        out[:, :OUT] = dot(pick[rows], parts[...]).astype(BF16)
        out[:, OUT:] = packed[rows]


def suffix_kernel(
    place, own_lat, own_rot, latent, rope, live, w_uv, va, va_swap, vb, vb_swap, out, out_logs, rope32, result, whole, sems
):
    copies = gather_weights(place, w_uv, va, va_swap, vb, vb_swap, whole, sems)
    rope32[...] = rope[...].astype(F32)
    keys, pairs = 8 * SUF, 8 * SUF // 2
    key, pair = iota((keys, pairs), 0), iota((keys, pairs), 1)
    same = lax.shift_right_logical(key, 6) == lax.bitwise_and(pair, 7)
    first = 2 * lax.shift_right_logical(pair, 3)
    even = (same & (lax.bitwise_and(key, SUF - 1) == first)).astype(BF16)
    odd = (same & (lax.bitwise_and(key, SUF - 1) == first + 1)).astype(BF16)
    lane = iota((8, 128), 1)
    col, row = iota((8, keys), 1), iota((8, keys), 0)

    def body(i, carry):
        rows = pl.ds(pl.multiple_of(i * 8, 8), 8)
        query = own_lat[:, rows, :].reshape(HEADS * 8, KVL).astype(BF16)
        query_rot = own_rot[:, rows, :].reshape(HEADS * 8, ROPE).astype(BF16)
        lat = latent[rows].reshape(keys, KVL)
        rot = rope32[rows, :]
        rot = jnp.concatenate([rot[:, 128 * j : 128 * j + 128] for j in range(SUF // 2)], axis=0).astype(BF16)
        rot_keys = (dot(even, rot[:, :ROPE]) + dot(odd, rot[:, ROPE:])).astype(BF16)
        scores = dot(query, lat, LAST) + dot(query_rot, rot_keys, LAST)
        seen = (lax.shift_right_logical(col, 6) == row) & (lax.bitwise_and(col, SUF - 1) < live[rows, :])
        bias = jnp.where(seen, 0.0, LOW)
        scores = ((scores * SCALE).reshape(HEADS, 8, keys) + bias[None]).reshape(HEADS * 8, keys)
        top = jnp.max(scores, axis=1, keepdims=True)
        raw = jnp.exp(scores - top)
        total = jnp.sum(raw, axis=1, keepdims=True)
        summed = dot(raw.astype(BF16), lat) * (1.0 / total)
        result[:, rows, :] = summed.reshape(HEADS, 8, KVL)
        log = (top + jnp.log(total)).reshape(HEADS, 8, 1)
        spread = jnp.zeros((8, 128), F32)
        for head in range(HEADS):
            spread = jnp.where(lane == head, log[head], spread)
        out_logs[rows, :] = spread
        return carry

    lax.fori_loop(0, ROWS // 8, body, 0)
    for copy in copies:
        copy.wait()
    for head in range(HEADS):
        out[:, head * VDIM : (head + 1) * VDIM] = dot(result[head].astype(BF16), whole[head], LAST)


def final_kernel(own, own_logs, r0, r1, r2, r3, out):
    gather = (
        (lax.bitwise_and(iota((128, 128), 0), 15) == iota((128, 128), 1)) & (iota((128, 128), 0) < 48)
    ).astype(BF16)
    logs = [own_logs[...]] + [dot(r[:, OUT:], gather) for r in (r0, r1, r2, r3)]
    top = functools.reduce(jnp.maximum, logs)
    weights = [jnp.exp(log - top) for log in logs]
    total = 1.0 / functools.reduce(jnp.add, weights)
    weights = [w * total for w in weights]
    for head in range(HEADS):
        at = slice(head * VDIM, (head + 1) * VDIM)
        mixed = own[:, at] * weights[0][:, head : head + 1]
        for part, weight in zip((r0, r1, r2, r3), weights[1:]):
            mixed = mixed + part[:, at].astype(F32) * weight[:, head : head + 1]
        out[:, at] = mixed.astype(BF16)


def row_of(z, x, c):
    return ((z % NZ) * NX + x % NX) * NC + c


CHIPS = [(z, x, c) for z in range(NZ) for x in range(NX) for c in range(NC)]


def ring_z(a):
    return lax.ppermute(a, "rows", [(row_of(z, x, c), row_of(z + 1 - 2 * c, x, c)) for z, x, c in CHIPS])


def shift_x(a, by):
    return lax.ppermute(a, "rows", [(row_of(z, x, c), row_of(z, x + by, c)) for z, x, c in CHIPS])


def swap(a):
    return lax.ppermute(a, "rows", [(row_of(z, x, c), row_of(z, x, 1 - c)) for z, x, c in CHIPS])


def move_y(a, by):
    pairs = []
    for z, x, c in CHIPS:
        r = row_of(z, x, c)
        pairs += [(r * NY + y, r * NY + (y + by[c]) % NY) for y in range(NY)]
    return lax.ppermute(a, ("rows", "proj"), pairs)


def cost(us):
    return pl.CostEstimate(flops=int(us * 1e6), bytes_accessed=int(us * 3.0e6), transcendentals=0)


def struct(*shape, dtype=BF16):
    return jax.ShapeDtypeStruct(shape, dtype)


def shards(
    q_nope, q_rope, w_uk, w_uv, prefix_latent, prefix_rope, suffix_latent, suffix_rope, page_slot, page_pattern, suffix_len
):
    row, y = lax.axis_index("rows"), lax.axis_index("proj")
    place = jnp.stack([row // (NX * NC), row // NC % NX, row % NC, y]).astype(I32)
    half = HEADS // 2
    pages, pay, ka, kb, va, vb = pl.pallas_call(
        prep_kernel,
        out_shape=(
            struct(2, UNIT, KVL), struct(ROWS, PAY),
            struct(HEADS, NOPE, 128), struct(half, NOPE, 128), struct(HEADS, VDIM, 128), struct(half, VDIM, 128),
        ),
        in_specs=[SMEM] + [VMEM] * 6 + [ANY] * 2,
        out_specs=(VMEM, VMEM, ANY, ANY, ANY, ANY),
        scratch_shapes=[pltpu.SemaphoreType.DMA((4,))],
        compiler_params=params(16),
        cost_estimate=cost(2),
        name="prep",
    )(place, page_pattern, page_slot.reshape(1, -1), prefix_latent, prefix_rope, q_nope, q_rope, w_uk, w_uv)

    a, b = [pages], [swap(pages)]
    pays = [pay] + [shift_x(pay, by) for by in (1, 2, 3)]
    for step in range(1, 5):
        a.append(ring_z(a[-1]))
        if step < 4:
            b.append(ring_z(b[-1]))
    ka_y, kb_y = move_y(ka, (1, -1)), move_y(kb, (2, 2))
    va_y, vb_y = move_y(va, (1, -1)), move_y(vb, (2, 2))
    k_parts = (ka_y, swap(ka_y), kb_y, swap(kb_y))
    v_parts = (va_y, swap(va_y), vb_y, swap(vb_y))
    a_swap = [None] + [swap(u) for u in a[1:]]
    b_swap = [None] + [swap(u) for u in b[1:]]
    early_units = [a[0], b[0], a[1], b[1], a[2], b[2], b_swap[2], a_swap[2], b_swap[1], a_swap[1]]
    late_units = [a[3], b[3], a[4], a_swap[4], b_swap[3], a_swap[3]]

    q_lat, q_rot, own_lat, own_rot, page_bit, slot_of = pl.pallas_call(
        query_kernel,
        out_shape=(
            struct(HEADS, SLOTS, KVL), struct(HEADS, SLOTS, ROPE),
            struct(HEADS, ROWS, KVL, dtype=F32), struct(HEADS, ROWS, ROPE, dtype=F32),
            struct(SLOTS, 128, dtype=F32), struct(4 * ROWS, 128, dtype=F32),
        ),
        in_specs=[SMEM] + [VMEM] * 4 + [ANY] * 5,
        out_specs=(VMEM,) * 6,
        scratch_shapes=[
            pltpu.VMEM((HEADS, NOPE, KVL), BF16), pltpu.VMEM((SLOTS, 4 * ROWS), BF16), pltpu.SemaphoreType.DMA((5,)),
        ],
        compiler_params=params(32),
        cost_estimate=cost(4),
        name="queries",
    )(place, *pays, w_uk, *k_parts)

    early, early_logs = pl.pallas_call(
        early_kernel,
        out_shape=(struct(HEADS, EARLY * 16, KVL), struct(EARLY * 16, 128, dtype=F32)),
        in_specs=[ANY] * EARLY + [VMEM] * 3,
        out_specs=(VMEM, VMEM),
        scratch_shapes=[pltpu.VMEM((EARLY, 2, UNIT, KVL), BF16), pltpu.SemaphoreType.DMA((EARLY,))],
        compiler_params=params(32),
        cost_estimate=cost(6),
        name="early_pages",
    )(*early_units, q_lat, q_rot, page_bit)

    returns = pl.pallas_call(
        late_kernel,
        out_shape=(struct(ROWS, RET),) * 4,
        in_specs=[ANY] * LATE + [SMEM] + [VMEM] * 6 + [ANY] * 5,
        out_specs=(VMEM,) * 4,
        scratch_shapes=[
            pltpu.VMEM((LATE, 2, UNIT, KVL), BF16), pltpu.VMEM((HEADS, LATE * 16, KVL), BF16),
            pltpu.VMEM((LATE * 16, 128), F32), pltpu.VMEM((HEADS, VDIM, KVL), BF16), pltpu.VMEM((SLOTS, OUT), BF16),
            pltpu.SemaphoreType.DMA((LATE,)), pltpu.SemaphoreType.DMA((5,)),
        ],
        compiler_params=params(32),
        cost_estimate=cost(7),
        name="late_pages",
    )(*late_units, place, q_lat, q_rot, page_bit, slot_of, early, early_logs, w_uv, *v_parts)

    backs = [returns[0]] + [shift_x(returns[by], -by) for by in (1, 2, 3)]
    own_lat, returns = lax.optimization_barrier((own_lat, returns))
    own, own_logs = pl.pallas_call(
        suffix_kernel,
        out_shape=(struct(ROWS, OUT, dtype=F32), struct(ROWS, 128, dtype=F32)),
        in_specs=[SMEM] + [VMEM] * 5 + [ANY] * 5,
        out_specs=(VMEM, VMEM),
        scratch_shapes=[
            pltpu.VMEM((ROWS, SUF * ROPE), F32), pltpu.VMEM((HEADS, ROWS, KVL), F32),
            pltpu.VMEM((HEADS, VDIM, KVL), BF16), pltpu.SemaphoreType.DMA((5,)),
        ],
        compiler_params=params(32),
        cost_estimate=cost(8),
        name="suffix",
    )(place, own_lat, own_rot, suffix_latent, suffix_rope, suffix_len.reshape(-1, 1), w_uv, *v_parts)

    return pl.pallas_call(
        final_kernel,
        out_shape=struct(ROWS, OUT),
        in_specs=[VMEM] * 6,
        out_specs=VMEM,
        compiler_params=params(16),
        cost_estimate=cost(2),
        name="combine",
    )(own, own_logs, *backs)


def solution(mesh):
    return jax.shard_map(
        shards,
        mesh=mesh,
        in_specs=(
            P("rows", "proj"), P("rows", "proj"), P(None, None, "proj"), P(None, None, "proj"),
            P("rows", None, None), P("rows", None), P("rows", None, None), P("rows", None),
            P(), P("rows", None), P("rows"),
        ),
        out_specs=P("rows", "proj"),
        check_vma=False,
    )
```

time: 244 us -> 120 us (0.49)
  waiting for transfers between devices: 109 us -> 14.8 us
  starting transfers between devices: 3.79 us -> 47.9 us
  local copies, waits for them, and re-layouts: 56.9 us -> 17.9 us
  Pallas kernels: 0 us -> 38 us
  blocking collectives: 29.2 us -> 0 us
  matrix products: 26.8 us -> 0 us
  between operations: 13.7 us -> 0.21 us
  other arithmetic: 4.01 us -> 0.08 us
    all_gather x2 -> x0, waiting for transfers between devices: 96.8 us -> none  [the longest x1 82 us: shards(): lax.all_gather(prefix_latent, 'rows', axis=0, tiled=True)]
    ppermute x0 -> x29, starting transfers between devices: none -> 47.9 us  [the longest x7 18.6 us: ring_z(): lax.ppermute(a, 'rows', [(row_of(z, x, c), row_of(z + 1 - 2 * c, x, c)) f...]
    pallas_call x0 -> x6, Pallas kernels: none -> 38 us  [the longest x1 11.6 us: shards(): pl.pallas_call(suffix_kernel, out_shape=(struct(ROWS, OUT, dtype=F32), st...]
    all_to_all x1 -> x0, blocking collectives: 29.2 us -> none  [shards(): lax.all_to_all(w_uv, 'proj', split_axis=0, concat_axis=2, tiled=True)]
    dot_general x11 -> x0, matrix products: 26.8 us -> none  [the longest x3 15.3 us: partial_attention(): jnp.einsum('bgc,btc->bgt', queries, latents, preferred_element_type=jnp.f...]
    gather x4 -> x0, local copies, waits for them, and re-layouts: 26 us -> none  [the longest x2 22.6 us: shards(): all_latent[picked]]
    unnamed x32 -> x41, local copies, waits for them, and re-layouts: 0.25 us -> 17.8 us
    reshape x6 -> x1, local copies, waits for them, and re-layouts: 15.5 us -> 0.1 us  [shards(): suffix_len.reshape(-1, 1)]
  transfers between devices with their start and end apart: 3 -> 29, of which waited for: 3 -> 5; matrix products, arithmetic and copies ran while one was open for 15% -> 0% of each run, Pallas kernels for 0% -> 21%
where the time goes in v1:
time: 120 us; the launch traced here: 119 us
  starting transfers between devices  47.9 us (40%)
  Pallas kernels  38 us (32%)
  local copies, waits for them, and re-layouts  17.9 us (15%)
  waiting for transfers between devices  14.8 us (12%)
    ppermute x7, starting transfers between devices, ring_z(): lax.ppermute(a, 'rows', [(row_of(z, x, c), row_of(z + 1 - 2 * c, x, c)) f...  18.6 us
    unnamed x41, local copies, waits for them, and re-layouts  17.8 us
    ppermute x6, waiting for transfers between devices, shift_x(): lax.ppermute(a, 'rows', [(row_of(z, x, c), row_of(z, x + by, c)) for z, x...  12.3 us
    pallas_call x1, Pallas kernels, shards(): pl.pallas_call(suffix_kernel, out_shape=(struct(ROWS, OUT, dtype=F32), st...  11.6 us
    ppermute x12, starting transfers between devices, swap(): lax.ppermute(a, 'rows', [(row_of(z, x, c), row_of(z, x, 1 - c)) for z, x,...  11.5 us
    ppermute x4, starting transfers between devices, move_y(): return lax.ppermute(a, ('rows', 'proj'), pairs)  9.36 us
    pallas_call x1, Pallas kernels, shards(): pl.pallas_call(late_kernel, out_shape=(struct(ROWS, RET),) * 4, in_specs=...  8.98 us
    ppermute x6, starting transfers between devices, shift_x(): lax.ppermute(a, 'rows', [(row_of(z, x, c), row_of(z, x + by, c)) for z, x...  8.34 us
  transfers between devices with their start and end apart: 29, of which 5 were waited for; matrix products, arithmetic and copies ran while one was open for 0% of the time, Pallas kernels for 21%

profile of v1, /device:TPU:1, one launch (start us, length us, event | category | flops | bytes accessed | tf_op | source)
XLA Modules:
  0.0 118.8 jit_solution(12882695641261486344)
XLA Ops:
  0.8 1.6 %copy-done = bf16[64,128,128]{2,1,0:T(8,128)(2,1)S(1)} copy-done((bf16[64,128,128]{2,1,0:T(8,128)(2,1)S(1)}, bf16[64,128,128]{2,1,0:T(8,128)(2,1)}, u32[]{:S(2)}) %copy-start) | copy-done | bytes 2097176
  2.4 1.6 %copy-done.2 = bf16[64,128,128]{2,1,0:T(8,128)(2,1)S(1)} copy-done((bf16[64,128,128]{2,1,0:T(8,128)(2,1)S(1)}, bf16[64,128,128]{2,1,0:T(8,128)(2,1)}, u32[]{:S(2)}) %copy-start.2) | copy-done | bytes 2097176
  8.3 1.1 prep.1
  9.4 3.8 %collective-permute-start.5 = (bf16[8,128,128]{2,1,0:T(8,128)(2,1)S(1)}, bf16[8,128,128]{2,1,0:T(8,128)(2,1)S(1)}, u32[]{:S(2)}, u32[]{:S(2)}) collective-permute-start(bf16[8,128,128]{2,1,0:T(8,128)(2,1)S(1)} %get-tuple-element.28), channel_id=1, source_target_pairs={{0,2},{1,3},{2,0},{3,1},{4,6},{5,7},{6,4},{7,5},{8,10},{9,11},{10,... | collective-permute-start | bytes 786440 | tf_op jit(solution)/shard_map/ppermute | solution.py:367
  13.3 2.9 %collective-permute-start.10 = (bf16[2,144,512]{2,1,0:T(8,128)(2,1)S(1)}, bf16[2,144,512]{2,1,0:T(8,128)(2,1)S(1)}, u32[]{:S(2)}, u32[]{:S(2)}) collective-permute-start(bf16[2,144,512]{2,1,0:T(8,128)(2,1)S(1)} %get-tuple-element.30.refs_0_), channel_id=1, source_target_pairs={{0,4},{4,0},{8,12},{12,8},{16,20},{20,16},{24,28},{28,24},{32,36},... | collective-permute-start | bytes 884744 | tf_op jit(solution)/shard_map/ppermute | solution.py:359
  16.2 3.8 %collective-permute-start.7 = (bf16[2,144,512]{2,1,0:T(8,128)(2,1)S(1)}, bf16[2,144,512]{2,1,0:T(8,128)(2,1)S(1)}, u32[]{:S(2)}, u32[]{:S(2)}) collective-permute-start(bf16[2,144,512]{2,1,0:T(8,128)(2,1)S(1)} %get-tuple-element.30.refs_0_), channel_id=1, source_target_pairs={{0,32},{4,228},{8,40},{12,236},{16,48},{20,244},{24,56},{28,252},{... | collective-permute-start | bytes 884744 | tf_op jit(solution)/shard_map/ppermute | solution.py:351
  20.1 2.7 %collective-permute-start.3 = (bf16[16,128,128]{2,1,0:T(8,128)(2,1)S(1)}, bf16[16,128,128]{2,1,0:T(8,128)(2,1)S(1)}, u32[]{:S(2)}, u32[]{:S(2)}) collective-permute-start(bf16[16,128,128]{2,1,0:T(8,128)(2,1)S(1)} %get-tuple-element.27), channel_id=1, source_target_pairs={{0,1},{1,2},{2,3},{3,0},{4,7},{5,4},{6,5},{7,6},{8,9},{9,10},{10,1... | collective-permute-start | bytes 1572872 | tf_op jit(solution)/shard_map/ppermute | solution.py:367
  22.8 1.2 %collective-permute-start = (bf16[64,3200]{1,0:T(8,128)(2,1)S(1)}, bf16[64,3200]{1,0:T(8,128)(2,1)S(1)}, u32[]{:S(2)}, u32[]{:S(2)}) collective-permute-start(bf16[64,3200]{1,0:T(8,128)(2,1)S(1)} %get-tuple-element.26.p0), channel_id=1, source_target_pairs={{0,8},{4,12},{8,16},{12,20},{16,24},{20,28},{24,0},{28,4},{32,40},... | collective-permute-start | bytes 1228808 | tf_op jit(solution)/shard_map/ppermute | solution.py:355
  24.0 3.3 %collective-permute-start.1 = (bf16[64,3200]{1,0:T(8,128)(2,1)S(1)}, bf16[64,3200]{1,0:T(8,128)(2,1)S(1)}, u32[]{:S(2)}, u32[]{:S(2)}) collective-permute-start(bf16[64,3200]{1,0:T(8,128)(2,1)S(1)} %get-tuple-element.26.p0), channel_id=1, source_target_pairs={{0,16},{4,20},{8,24},{12,28},{16,0},{20,4},{24,8},{28,12},{32,48},... | collective-permute-start | bytes 1228808 | tf_op jit(solution)/shard_map/ppermute | solution.py:355
  28.3 2.7 %collective-permute-start.22 = (bf16[16,128,128]{2,1,0:T(8,128)(2,1)S(1)}, bf16[16,128,128]{2,1,0:T(8,128)(2,1)S(1)}, u32[]{:S(2)}, u32[]{:S(2)}) collective-permute-start(bf16[16,128,128]{2,1,0:T(8,128)(2,1)S(1)} %get-tuple-element.37), channel_id=1, source_target_pairs={{0,1},{1,2},{2,3},{3,0},{4,7},{5,4},{6,5},{7,6},{8,9},{9,10},{10,1... | collective-permute-start | bytes 1572872 | tf_op jit(solution)/shard_map/ppermute | solution.py:367
  30.9 3.5 %collective-permute-done.p1 = bf16[64,3200]{1,0:T(8,128)(2,1)S(1)} collective-permute-done((bf16[64,3200]{1,0:T(8,128)(2,1)S(1)}, bf16[64,3200]{1,0:T(8,128)(2,1)S(1)}, u32[]{:S(2)}, u32[]{:S(2)}) %collective-permute-start) | collective-permute-done | bytes 409632 | tf_op jit(solution)/shard_map/ppermute | solution.py:355
  34.4 2.1 %collective-permute-start.8 = (bf16[2,144,512]{2,1,0:T(8,128)(2,1)S(1)}, bf16[2,144,512]{2,1,0:T(8,128)(2,1)S(1)}, u32[]{:S(2)}, u32[]{:S(2)}) collective-permute-start(bf16[2,144,512]{2,1,0:T(8,128)(2,1)S(1)} %collective-permute-done.7.refs_2_), channel_id=1, source_target_pairs={{0,32},{4,228},{8,40},{12,236},{16,48},{20,244},{24,56},{28,252},{... | collective-permute-start | bytes 884744 | tf_op jit(solution)/shard_map/ppermute | solution.py:351
  36.6 7.8 %collective-permute-done.1.p2 = bf16[64,3200]{1,0:T(8,128)(2,1)S(1)} collective-permute-done((bf16[64,3200]{1,0:T(8,128)(2,1)S(1)}, bf16[64,3200]{1,0:T(8,128)(2,1)S(1)}, u32[]{:S(2)}, u32[]{:S(2)}) %collective-permute-start.1) | collective-permute-done | bytes 409632 | tf_op jit(solution)/shard_map/ppermute | solution.py:355
  44.3 1.0 collective-permute-done.2.p3
  45.4 1.6 %collective-permute-start.6 = (bf16[8,128,128]{2,1,0:T(8,128)(2,1)S(1)}, bf16[8,128,128]{2,1,0:T(8,128)(2,1)S(1)}, u32[]{:S(2)}, u32[]{:S(2)}) collective-permute-start(bf16[8,128,128]{2,1,0:T(8,128)(2,1)S(1)} %collective-permute-done.5.kb), channel_id=1, source_target_pairs={{0,4},{4,0},{8,12},{12,8},{16,20},{20,16},{24,28},{28,24},{32,36},... | collective-permute-start | bytes 786440 | tf_op jit(solution)/shard_map/ppermute | solution.py:359
  46.9 5.7 %collective-permute-start.9 = (bf16[2,144,512]{2,1,0:T(8,128)(2,1)S(1)}, bf16[2,144,512]{2,1,0:T(8,128)(2,1)S(1)}, u32[]{:S(2)}, u32[]{:S(2)}) collective-permute-start(bf16[2,144,512]{2,1,0:T(8,128)(2,1)S(1)} %collective-permute-done.8.refs_4_), channel_id=1, source_target_pairs={{0,32},{4,228},{8,40},{12,236},{16,48},{20,244},{24,56},{28,252},{... | collective-permute-start | bytes 884744 | tf_op jit(solution)/shard_map/ppermute | solution.py:351
  54.1 2.1 %collective-permute-done.9.refs_0_ = bf16[2,144,512]{2,1,0:T(8,128)(2,1)S(1)} collective-permute-done((bf16[2,144,512]{2,1,0:T(8,128)(2,1)S(1)}, bf16[2,144,512]{2,1,0:T(8,128)(2,1)S(1)}, u32[]{:S(2)}, u32[]{:S(2)}) %collective-permute-start.9) | collective-permute-done | bytes 294944 | tf_op jit(solution)/shard_map/ppermute | solution.py:351
  56.3 3.1 %collective-permute-start.14 = (bf16[2,144,512]{2,1,0:T(8,128)(2,1)S(1)}, bf16[2,144,512]{2,1,0:T(8,128)(2,1)S(1)}, u32[]{:S(2)}, u32[]{:S(2)}) collective-permute-start(bf16[2,144,512]{2,1,0:T(8,128)(2,1)S(1)} %collective-permute-done.9.refs_0_), channel_id=1, source_target_pairs={{0,32},{4,228},{8,40},{12,236},{16,48},{20,244},{24,56},{28,252},{... | collective-permute-start | bytes 884744 | tf_op jit(solution)/shard_map/ppermute | solution.py:351
  59.4 3.1 %collective-permute-start.13 = (bf16[2,144,512]{2,1,0:T(8,128)(2,1)S(1)}, bf16[2,144,512]{2,1,0:T(8,128)(2,1)S(1)}, u32[]{:S(2)}, u32[]{:S(2)}) collective-permute-start(bf16[2,144,512]{2,1,0:T(8,128)(2,1)S(1)} %collective-permute-done.12.refs_5_), channel_id=1, source_target_pairs={{0,32},{4,228},{8,40},{12,236},{16,48},{20,244},{24,56},{28,252},{... | collective-permute-start | bytes 884744 | tf_op jit(solution)/shard_map/ppermute | solution.py:351
  63.2 2.8 %collective-permute-start.15 = (bf16[2,144,512]{2,1,0:T(8,128)(2,1)S(1)}, bf16[2,144,512]{2,1,0:T(8,128)(2,1)S(1)}, u32[]{:S(2)}, u32[]{:S(2)}) collective-permute-start(bf16[2,144,512]{2,1,0:T(8,128)(2,1)S(1)} %collective-permute-done.14.refs_2_), channel_id=1, source_target_pairs={{0,4},{4,0},{8,12},{12,8},{16,20},{20,16},{24,28},{28,24},{32,36},... | collective-permute-start | bytes 884744 | tf_op jit(solution)/shard_map/ppermute | solution.py:359
  66.2 2.9 %collective-permute-start.16 = (bf16[2,144,512]{2,1,0:T(8,128)(2,1)S(1)}, bf16[2,144,512]{2,1,0:T(8,128)(2,1)S(1)}, u32[]{:S(2)}, u32[]{:S(2)}) collective-permute-start(bf16[2,144,512]{2,1,0:T(8,128)(2,1)S(1)} %collective-permute-done.13.refs_1_), channel_id=1, source_target_pairs={{0,4},{4,0},{8,12},{12,8},{16,20},{20,16},{24,28},{28,24},{32,36},... | collective-permute-start | bytes 884744 | tf_op jit(solution)/shard_map/ppermute | solution.py:359
  69.1 6.8 %queries.1 = (bf16[16,256,512]{2,1,0:T(8,128)(2,1)S(1)}, bf16[16,256,64]{2,1,0:T(8,128)(2,1)S(1)}, f32[16,64,512]{2,1,0:T(8,128)S(1)}, f32[16,64,64]{2,1,0:T(8,1...) custom-call(s32[4]{0:T(128)S(1)} %pad_add_fusion.place.refs_6_, bf16[64,3200]{1,0:T(8,128)(2,1)S(1)} %get-tuple-element.26.p0, ...), custom_call_target="tpu_custom_call" | custom-call | flops 4000000 | bytes 12000000 | tf_op jit(solution)/shard_map/queries/pallas_call | solution.py:413
  75.9 1.3 %copy-done.5 = f32[16,64,512]{2,1,0:T(8,128)} copy-done((f32[16,64,512]{2,1,0:T(8,128)}, f32[16,64,512]{2,1,0:T(8,128)S(1)}, u32[]{:S(2)}) %copy-start.5) | copy-done | bytes 2097176
  78.0 6.8 %early_pages.1 = (bf16[16,160,512]{2,1,0:T(8,128)(2,1)S(1)}, f32[160,128]{1,0:T(8,128)S(1)}) custom-call(bf16[2,144,512]{2,1,0:T(8,128)(2,1)S(1)} %get-tuple-element.30.refs_0_, bf16[2,144,512]{2,1,0:T(8,128)(2,1)S(1)} %collective-permute-done.10.refs_1_, bf16[2,144,512]{2,1,0:T(8,128)(2,1)S(1)} %collective-permute-done.7.refs_2_, ...), custom_call_target="tpu_custom_call" | custom-call | flops 6000000 | bytes 18000000 | tf_op jit(solution)/shard_map/early_pages/pallas_call | solution.py:430
  84.9 9.0 %late_pages.1 = (bf16[64,2176]{1,0:T(8,128)(2,1)S(1)}, bf16[64,2176]{1,0:T(8,128)(2,1)}, bf16[64,2176]{1,0:T(8,128)(2,1)}, bf16[64,2176]{1,0:T(8,128)(2,1)}) custom-call(bf16[2,144,512]{2,1,0:T(8,128)(2,1)S(1)} %collective-permute-done.9.refs_0_, bf16[2,144,512]{2,1,0:T(8,128)(2,1)S(1)} %collective-permute-done.13.refs_1_, ...), custom_call_target="tpu_custom_call" | custom-call | flops 7000000 | bytes 21000000 | tf_op jit(solution)/shard_map/late_pages/pallas_call | solution.py:441
  94.6 2.3 %collective-permute-start.26 = (bf16[64,2176]{1,0:T(8,128)(2,1)}, bf16[64,2176]{1,0:T(8,128)(2,1)}, u32[]{:S(2)}, u32[]{:S(2)}) collective-permute-start(bf16[64,2176]{1,0:T(8,128)(2,1)} %get-tuple-element.40), channel_id=1, source_target_pairs={{0,24},{4,28},{8,0},{12,4},{16,8},{20,12},{24,16},{28,20},{32,56},... | collective-permute-start | bytes 835592 | tf_op jit(solution)/shard_map/ppermute | solution.py:355
  97.6 2.2 %copy-done.4 = bf16[64,64,512]{2,1,0:T(8,128)(2,1)S(1)} copy-done((bf16[64,64,512]{2,1,0:T(8,128)(2,1)S(1)}, bf16[64,64,512]{2,1,0:T(8,128)(2,1)}, u32[]{:S(2)}) %copy-start.4) | copy-done | bytes 4194328
  99.8 1.6 %copy-done.6 = f32[16,64,512]{2,1,0:T(8,128)S(1)} copy-done((f32[16,64,512]{2,1,0:T(8,128)S(1)}, f32[16,64,512]{2,1,0:T(8,128)}, u32[]{:S(2)}) %copy-start.6) | copy-done | bytes 2097176
  102.3 1.0 copy-done.9
  103.4 1.0 copy-done.11
  104.4 11.6 %suffix.1 = (f32[64,2048]{1,0:T(8,128)S(1)}, f32[64,128]{1,0:T(8,128)S(1)}) custom-call(s32[4]{0:T(128)S(1)} %pad_add_fusion.place.refs_6_, f32[16,64,512]{2,1,0:T(8,128)S(1)} %copy-done.6, f32[16,64,64]{2,1,0:T(8,128)S(1)} %copy-done.11, bf16[64,64,512]{2,1,0:T(8,128)(2,1)S(1)} %copy-done.4, bf16[64,4096]{1,0:T(8,128)(2,1)S(1)} %copy-done.9, ...), custom_call_target="tpu_custom_call" | custom-call | flops 8000000 | bytes 24000000 | tf_op jit(solution)/shard_map/suffix/pallas_call | solution.py:458
  116.1 2.8 %combine.1 = bf16[64,2048]{1,0:T(8,128)(2,1)} custom-call(f32[64,2048]{1,0:T(8,128)S(1)} %get-tuple-element.45.own, f32[64,128]{1,0:T(8,128)S(1)} %get-tuple-element.46.own_logs, bf16[64,2176]{1,0:T(8,128)(2,1)S(1)} %copy-done.13, bf16[64,2176]{1,0:T(8,128)(2,1)} %collective-permute-done.26.r1, bf16[64,2176]{1,0:T(8,128)(2,1)} %collective-permute-done.27.r2, ...), custom_call_target="tpu_custom_call" | custom-call | flops 2000000 | bytes 6000000 | tf_op jit(solution)/shard_map/combine/pallas_call | solution.py:472
  (75 shorter events, 11.7 us)
Async XLA Ops:
  8.2 60.9 %copy-start.3 = (bf16[64,128,128]{2,1,0:T(8,128)(2,1)S(1)}, bf16[64,128,128]{2,1,0:T(8,128)(2,1)}, u32[]{:S(2)}) copy-start(bf16[64,128,128]{2,1,0:T(8,128)(2,1)} %w_uk.3) | copy-start | bytes 6291460
  9.4 13.4 %collective-permute-start.5 = (bf16[8,128,128]{2,1,0:T(8,128)(2,1)S(1)}, bf16[8,128,128]{2,1,0:T(8,128)(2,1)S(1)}, u32[]{:S(2)}, u32[]{:S(2)}) collective-permute-start(bf16[8,128,128]{2,1,0:T(8,128)(2,1)S(1)} %get-tuple-element.28), channel_id=1, source_target_pairs={{0,2},{1,3},{2,0},{3,1},{4,6},{5,7},{6,4},{7,5},{8,10},{9,11},{10,... | collective-permute-start | bytes 786440 | tf_op jit(solution)/shard_map/ppermute | solution.py:367
  13.2 10.8 %collective-permute-start.24 = (bf16[8,128,128]{2,1,0:T(8,128)(2,1)S(1)}, bf16[8,128,128]{2,1,0:T(8,128)(2,1)S(1)}, u32[]{:S(2)}, u32[]{:S(2)}) collective-permute-start(bf16[8,128,128]{2,1,0:T(8,128)(2,1)S(1)} %get-tuple-element.38), channel_id=1, source_target_pairs={{0,2},{1,3},{2,0},{3,1},{4,6},{5,7},{6,4},{7,5},{8,10},{9,11},{10,... | collective-permute-start | bytes 786440 | tf_op jit(solution)/shard_map/ppermute | solution.py:367
  13.3 14.1 %collective-permute-start.10 = (bf16[2,144,512]{2,1,0:T(8,128)(2,1)S(1)}, bf16[2,144,512]{2,1,0:T(8,128)(2,1)S(1)}, u32[]{:S(2)}, u32[]{:S(2)}) collective-permute-start(bf16[2,144,512]{2,1,0:T(8,128)(2,1)S(1)} %get-tuple-element.30.refs_0_), channel_id=1, source_target_pairs={{0,4},{4,0},{8,12},{12,8},{16,20},{20,16},{24,28},{28,24},{32,36},... | collective-permute-start | bytes 884744 | tf_op jit(solution)/shard_map/ppermute | solution.py:359
  16.2 12.0 %collective-permute-start.7 = (bf16[2,144,512]{2,1,0:T(8,128)(2,1)S(1)}, bf16[2,144,512]{2,1,0:T(8,128)(2,1)S(1)}, u32[]{:S(2)}, u32[]{:S(2)}) collective-permute-start(bf16[2,144,512]{2,1,0:T(8,128)(2,1)S(1)} %get-tuple-element.30.refs_0_), channel_id=1, source_target_pairs={{0,32},{4,228},{8,40},{12,236},{16,48},{20,244},{24,56},{28,252},{... | collective-permute-start | bytes 884744 | tf_op jit(solution)/shard_map/ppermute | solution.py:351
  20.1 26.9 %collective-permute-start.3 = (bf16[16,128,128]{2,1,0:T(8,128)(2,1)S(1)}, bf16[16,128,128]{2,1,0:T(8,128)(2,1)S(1)}, u32[]{:S(2)}, u32[]{:S(2)}) collective-permute-start(bf16[16,128,128]{2,1,0:T(8,128)(2,1)S(1)} %get-tuple-element.27), channel_id=1, source_target_pairs={{0,1},{1,2},{2,3},{3,0},{4,7},{5,4},{6,5},{7,6},{8,9},{9,10},{10,1... | collective-permute-start | bytes 1572872 | tf_op jit(solution)/shard_map/ppermute | solution.py:367
  22.8 11.6 %collective-permute-start = (bf16[64,3200]{1,0:T(8,128)(2,1)S(1)}, bf16[64,3200]{1,0:T(8,128)(2,1)S(1)}, u32[]{:S(2)}, u32[]{:S(2)}) collective-permute-start(bf16[64,3200]{1,0:T(8,128)(2,1)S(1)} %get-tuple-element.26.p0), channel_id=1, source_target_pairs={{0,8},{4,12},{8,16},{12,20},{16,24},{20,28},{24,0},{28,4},{32,40},... | collective-permute-start | bytes 1228808 | tf_op jit(solution)/shard_map/ppermute | solution.py:355
  24.0 20.3 %collective-permute-start.1 = (bf16[64,3200]{1,0:T(8,128)(2,1)S(1)}, bf16[64,3200]{1,0:T(8,128)(2,1)S(1)}, u32[]{:S(2)}, u32[]{:S(2)}) collective-permute-start(bf16[64,3200]{1,0:T(8,128)(2,1)S(1)} %get-tuple-element.26.p0), channel_id=1, source_target_pairs={{0,16},{4,20},{8,24},{12,28},{16,0},{20,4},{24,8},{28,12},{32,48},... | collective-permute-start | bytes 1228808 | tf_op jit(solution)/shard_map/ppermute | solution.py:355
  27.4 18.0 %collective-permute-start.2 = (bf16[64,3200]{1,0:T(8,128)(2,1)S(1)}, bf16[64,3200]{1,0:T(8,128)(2,1)S(1)}, u32[]{:S(2)}, u32[]{:S(2)}) collective-permute-start(bf16[64,3200]{1,0:T(8,128)(2,1)S(1)} %get-tuple-element.26.p0), channel_id=1, source_target_pairs={{0,24},{4,28},{8,0},{12,4},{16,8},{20,12},{24,16},{28,20},{32,56},... | collective-permute-start | bytes 1228808 | tf_op jit(solution)/shard_map/ppermute | solution.py:355
  28.3 25.1 %collective-permute-start.22 = (bf16[16,128,128]{2,1,0:T(8,128)(2,1)S(1)}, bf16[16,128,128]{2,1,0:T(8,128)(2,1)S(1)}, u32[]{:S(2)}, u32[]{:S(2)}) collective-permute-start(bf16[16,128,128]{2,1,0:T(8,128)(2,1)S(1)} %get-tuple-element.37), channel_id=1, source_target_pairs={{0,1},{1,2},{2,3},{3,0},{4,7},{5,4},{6,5},{7,6},{8,9},{9,10},{10,1... | collective-permute-start | bytes 1572872 | tf_op jit(solution)/shard_map/ppermute | solution.py:367
  34.4 12.5 %collective-permute-start.8 = (bf16[2,144,512]{2,1,0:T(8,128)(2,1)S(1)}, bf16[2,144,512]{2,1,0:T(8,128)(2,1)S(1)}, u32[]{:S(2)}, u32[]{:S(2)}) collective-permute-start(bf16[2,144,512]{2,1,0:T(8,128)(2,1)S(1)} %collective-permute-done.7.refs_2_), channel_id=1, source_target_pairs={{0,32},{4,228},{8,40},{12,236},{16,48},{20,244},{24,56},{28,252},{... | collective-permute-start | bytes 884744 | tf_op jit(solution)/shard_map/ppermute | solution.py:351
  44.3 8.3 %collective-permute-start.11 = (bf16[2,144,512]{2,1,0:T(8,128)(2,1)S(1)}, bf16[2,144,512]{2,1,0:T(8,128)(2,1)S(1)}, u32[]{:S(2)}, u32[]{:S(2)}) collective-permute-start(bf16[2,144,512]{2,1,0:T(8,128)(2,1)S(1)} %collective-permute-done.10.refs_1_), channel_id=1, source_target_pairs={{0,32},{4,228},{8,40},{12,236},{16,48},{20,244},{24,56},{28,252},{... | collective-permute-start | bytes 884744 | tf_op jit(solution)/shard_map/ppermute | solution.py:351
  45.4 8.0 %collective-permute-start.6 = (bf16[8,128,128]{2,1,0:T(8,128)(2,1)S(1)}, bf16[8,128,128]{2,1,0:T(8,128)(2,1)S(1)}, u32[]{:S(2)}, u32[]{:S(2)}) collective-permute-start(bf16[8,128,128]{2,1,0:T(8,128)(2,1)S(1)} %collective-permute-done.5.kb), channel_id=1, source_target_pairs={{0,4},{4,0},{8,12},{12,8},{16,20},{20,16},{24,28},{28,24},{32,36},... | collective-permute-start | bytes 786440 | tf_op jit(solution)/shard_map/ppermute | solution.py:359
  46.9 6.9 %collective-permute-start.21 = (bf16[2,144,512]{2,1,0:T(8,128)(2,1)S(1)}, bf16[2,144,512]{2,1,0:T(8,128)(2,1)S(1)}, u32[]{:S(2)}, u32[]{:S(2)}) collective-permute-start(bf16[2,144,512]{2,1,0:T(8,128)(2,1)S(1)} %collective-permute-done.7.refs_2_), channel_id=1, source_target_pairs={{0,4},{4,0},{8,12},{12,8},{16,20},{20,16},{24,28},{28,24},{32,36},... | collective-permute-start | bytes 884744 | tf_op jit(solution)/shard_map/ppermute | solution.py:359
  46.9 9.3 %collective-permute-start.9 = (bf16[2,144,512]{2,1,0:T(8,128)(2,1)S(1)}, bf16[2,144,512]{2,1,0:T(8,128)(2,1)S(1)}, u32[]{:S(2)}, u32[]{:S(2)}) collective-permute-start(bf16[2,144,512]{2,1,0:T(8,128)(2,1)S(1)} %collective-permute-done.8.refs_4_), channel_id=1, source_target_pairs={{0,32},{4,228},{8,40},{12,236},{16,48},{20,244},{24,56},{28,252},{... | collective-permute-start | bytes 884744 | tf_op jit(solution)/shard_map/ppermute | solution.py:351
  52.6 6.8 %collective-permute-start.12 = (bf16[2,144,512]{2,1,0:T(8,128)(2,1)S(1)}, bf16[2,144,512]{2,1,0:T(8,128)(2,1)S(1)}, u32[]{:S(2)}, u32[]{:S(2)}) collective-permute-start(bf16[2,144,512]{2,1,0:T(8,128)(2,1)S(1)} %collective-permute-done.11.refs_3_), channel_id=1, source_target_pairs={{0,32},{4,228},{8,40},{12,236},{16,48},{20,244},{24,56},{28,252},{... | collective-permute-start | bytes 884744 | tf_op jit(solution)/shard_map/ppermute | solution.py:351
  53.3 9.2 %collective-permute-start.19 = (bf16[2,144,512]{2,1,0:T(8,128)(2,1)S(1)}, bf16[2,144,512]{2,1,0:T(8,128)(2,1)S(1)}, u32[]{:S(2)}, u32[]{:S(2)}) collective-permute-start(bf16[2,144,512]{2,1,0:T(8,128)(2,1)S(1)} %collective-permute-done.8.refs_4_), channel_id=1, source_target_pairs={{0,4},{4,0},{8,12},{12,8},{16,20},{20,16},{24,28},{28,24},{32,36},... | collective-permute-start | bytes 884744 | tf_op jit(solution)/shard_map/ppermute | solution.py:359
  53.3 9.7 %collective-permute-start.4 = (bf16[16,128,128]{2,1,0:T(8,128)(2,1)S(1)}, bf16[16,128,128]{2,1,0:T(8,128)(2,1)S(1)}, u32[]{:S(2)}, u32[]{:S(2)}) collective-permute-start(bf16[16,128,128]{2,1,0:T(8,128)(2,1)S(1)} %collective-permute-done.3.ka), channel_id=1, source_target_pairs={{0,4},{4,0},{8,12},{12,8},{16,20},{20,16},{24,28},{28,24},{32,36},... | collective-permute-start | bytes 1572872 | tf_op jit(solution)/shard_map/ppermute | solution.py:359
  53.9 8.7 %collective-permute-start.20 = (bf16[2,144,512]{2,1,0:T(8,128)(2,1)S(1)}, bf16[2,144,512]{2,1,0:T(8,128)(2,1)S(1)}, u32[]{:S(2)}, u32[]{:S(2)}) collective-permute-start(bf16[2,144,512]{2,1,0:T(8,128)(2,1)S(1)} %collective-permute-done.11.refs_3_), channel_id=1, source_target_pairs={{0,4},{4,0},{8,12},{12,8},{16,20},{20,16},{24,28},{28,24},{32,36},... | collective-permute-start | bytes 884744 | tf_op jit(solution)/shard_map/ppermute | solution.py:359
  56.3 6.9 %collective-permute-start.14 = (bf16[2,144,512]{2,1,0:T(8,128)(2,1)S(1)}, bf16[2,144,512]{2,1,0:T(8,128)(2,1)S(1)}, u32[]{:S(2)}, u32[]{:S(2)}) collective-permute-start(bf16[2,144,512]{2,1,0:T(8,128)(2,1)S(1)} %collective-permute-done.9.refs_0_), channel_id=1, source_target_pairs={{0,32},{4,228},{8,40},{12,236},{16,48},{20,244},{24,56},{28,252},{... | collective-permute-start | bytes 884744 | tf_op jit(solution)/shard_map/ppermute | solution.py:351
  59.4 6.8 %collective-permute-start.13 = (bf16[2,144,512]{2,1,0:T(8,128)(2,1)S(1)}, bf16[2,144,512]{2,1,0:T(8,128)(2,1)S(1)}, u32[]{:S(2)}, u32[]{:S(2)}) collective-permute-start(bf16[2,144,512]{2,1,0:T(8,128)(2,1)S(1)} %collective-permute-done.12.refs_5_), channel_id=1, source_target_pairs={{0,32},{4,228},{8,40},{12,236},{16,48},{20,244},{24,56},{28,252},{... | collective-permute-start | bytes 884744 | tf_op jit(solution)/shard_map/ppermute | solution.py:351
  62.5 6.6 %collective-permute-start.18 = (bf16[2,144,512]{2,1,0:T(8,128)(2,1)S(1)}, bf16[2,144,512]{2,1,0:T(8,128)(2,1)S(1)}, u32[]{:S(2)}, u32[]{:S(2)}) collective-permute-start(bf16[2,144,512]{2,1,0:T(8,128)(2,1)S(1)} %collective-permute-done.12.refs_5_), channel_id=1, source_target_pairs={{0,4},{4,0},{8,12},{12,8},{16,20},{20,16},{24,28},{28,24},{32,36},... | collective-permute-start | bytes 884744 | tf_op jit(solution)/shard_map/ppermute | solution.py:359
  62.6 22.3 %collective-permute-start.23 = (bf16[16,128,128]{2,1,0:T(8,128)(2,1)S(1)}, bf16[16,128,128]{2,1,0:T(8,128)(2,1)S(1)}, u32[]{:S(2)}, u32[]{:S(2)}) collective-permute-start(bf16[16,128,128]{2,1,0:T(8,128)(2,1)S(1)} %collective-permute-done.22.refs_14_.va), channel_id=1, source_target_pairs={{0,4},{4,0},{8,12},{12,8},{16,20},{20,16},{24,28},{28,24},{32,36},... | collective-permute-start | bytes 1572872 | tf_op jit(solution)/shard_map/ppermute | solution.py:359
  63.1 21.8 %collective-permute-start.17 = (bf16[2,144,512]{2,1,0:T(8,128)(2,1)S(1)}, bf16[2,144,512]{2,1,0:T(8,128)(2,1)S(1)}, u32[]{:S(2)}, u32[]{:S(2)}) collective-permute-start(bf16[2,144,512]{2,1,0:T(8,128)(2,1)S(1)} %collective-permute-done.9.refs_0_), channel_id=1, source_target_pairs={{0,4},{4,0},{8,12},{12,8},{16,20},{20,16},{24,28},{28,24},{32,36},... | collective-permute-start | bytes 884744 | tf_op jit(solution)/shard_map/ppermute | solution.py:359
  63.2 21.7 %collective-permute-start.15 = (bf16[2,144,512]{2,1,0:T(8,128)(2,1)S(1)}, bf16[2,144,512]{2,1,0:T(8,128)(2,1)S(1)}, u32[]{:S(2)}, u32[]{:S(2)}) collective-permute-start(bf16[2,144,512]{2,1,0:T(8,128)(2,1)S(1)} %collective-permute-done.14.refs_2_), channel_id=1, source_target_pairs={{0,4},{4,0},{8,12},{12,8},{16,20},{20,16},{24,28},{28,24},{32,36},... | collective-permute-start | bytes 884744 | tf_op jit(solution)/shard_map/ppermute | solution.py:359
  66.2 18.6 %collective-permute-start.16 = (bf16[2,144,512]{2,1,0:T(8,128)(2,1)S(1)}, bf16[2,144,512]{2,1,0:T(8,128)(2,1)S(1)}, u32[]{:S(2)}, u32[]{:S(2)}) collective-permute-start(bf16[2,144,512]{2,1,0:T(8,128)(2,1)S(1)} %collective-permute-done.13.refs_1_), channel_id=1, source_target_pairs={{0,4},{4,0},{8,12},{12,8},{16,20},{20,16},{24,28},{28,24},{32,36},... | collective-permute-start | bytes 884744 | tf_op jit(solution)/shard_map/ppermute | solution.py:359
  69.1 15.7 %collective-permute-start.25 = (bf16[8,128,128]{2,1,0:T(8,128)(2,1)S(1)}, bf16[8,128,128]{2,1,0:T(8,128)(2,1)S(1)}, u32[]{:S(2)}, u32[]{:S(2)}) collective-permute-start(bf16[8,128,128]{2,1,0:T(8,128)(2,1)S(1)} %collective-permute-done.24.refs_16_.vb), channel_id=1, source_target_pairs={{0,4},{4,0},{8,12},{12,8},{16,20},{20,16},{24,28},{28,24},{32,36},... | collective-permute-start | bytes 786440 | tf_op jit(solution)/shard_map/ppermute | solution.py:359
  84.9 12.6 %copy-start.19 = (s32[64]{0:T(128)S(1)}, s32[64]{0:T(128)}, u32[]{:S(2)}) copy-start(s32[64]{0:T(128)} %param.21) | copy-start | bytes 772
  94.6 21.5 %collective-permute-start.26 = (bf16[64,2176]{1,0:T(8,128)(2,1)}, bf16[64,2176]{1,0:T(8,128)(2,1)}, u32[]{:S(2)}, u32[]{:S(2)}) collective-permute-start(bf16[64,2176]{1,0:T(8,128)(2,1)} %get-tuple-element.40), channel_id=1, source_target_pairs={{0,24},{4,28},{8,0},{12,4},{16,8},{20,12},{24,16},{28,20},{32,56},... | collective-permute-start | bytes 835592 | tf_op jit(solution)/shard_map/ppermute | solution.py:355
  96.9 19.1 %collective-permute-start.27 = (bf16[64,2176]{1,0:T(8,128)(2,1)}, bf16[64,2176]{1,0:T(8,128)(2,1)}, u32[]{:S(2)}, u32[]{:S(2)}) collective-permute-start(bf16[64,2176]{1,0:T(8,128)(2,1)} %get-tuple-element.41), channel_id=1, source_target_pairs={{0,16},{4,20},{8,24},{12,28},{16,0},{20,4},{24,8},{28,12},{32,48},... | collective-permute-start | bytes 835592 | tf_op jit(solution)/shard_map/ppermute | solution.py:355
  97.4 18.6 %collective-permute-start.28 = (bf16[64,2176]{1,0:T(8,128)(2,1)}, bf16[64,2176]{1,0:T(8,128)(2,1)}, u32[]{:S(2)}, u32[]{:S(2)}) collective-permute-start(bf16[64,2176]{1,0:T(8,128)(2,1)} %get-tuple-element.42), channel_id=1, source_target_pairs={{0,8},{4,12},{8,16},{12,20},{16,24},{20,28},{24,0},{28,4},{32,40},... | collective-permute-start | bytes 835592 | tf_op jit(solution)/shard_map/ppermute | solution.py:355
  104.4 11.6 %copy-start.13 = (bf16[64,2176]{1,0:T(8,128)(2,1)S(1)}, bf16[64,2176]{1,0:T(8,128)(2,1)}, u32[]{:S(2)}) copy-start(bf16[64,2176]{1,0:T(8,128)(2,1)} %copy-done.12) | copy-start | bytes 835588
  (17 other events, 32.9 us)

commit v2 on v1

v2 whole, which is shorter than its diff:
```python
import functools

import jax
import jax.numpy as jnp
from jax import lax
from jax.experimental import pallas as pl
from jax.experimental.pallas import tpu as pltpu
from jax.sharding import PartitionSpec as P

F32, BF16, I32 = jnp.float32, jnp.bfloat16, jnp.int32
LOW = -1e30

NZ, NX, NC, NY = 8, 4, 2, 4
HEADS = 16
ROWS = 64
NOPE = 128
VDIM = 128
ROPE = 64
KVL = 512
PAGE = 128
SUF = 64
UNIT = PAGE + PAGE * ROPE // KVL
QN = HEADS * NOPE
QR = HEADS * ROPE
PAY = QN + QR + 128
SLOTS = 256
PAIRS = 16
EARLY = 10
LATE = PAIRS - EARLY
SCALE = (NOPE + ROPE) ** -0.5
OUT = HEADS * VDIM
RET = OUT + 128
LOG2E = 1.4426950408889634
LAST = (((1,), (1,)), ((), ()))
FIRST = (((0,), (0,)), ((), ()))


def dot(a, b, dims=(((1,), (0,)), ((), ())), precision=None):
    return lax.dot_general(a, b, dims, preferred_element_type=F32, precision=precision)


def iota(shape, axis):
    return lax.broadcasted_iota(I32, shape, axis)


def params(mib):
    return pltpu.CompilerParams(vmem_limit_bytes=mib << 20)


VMEM = pl.BlockSpec(memory_space=pltpu.VMEM)
SMEM = pl.BlockSpec(memory_space=pltpu.SMEM)
ANY = pl.BlockSpec(memory_space=pl.ANY)
HBM = pl.BlockSpec(memory_space=pltpu.HBM)


def load_all(pairs, sems):
    copies = [pltpu.make_async_copy(src, dst, sems.at[i]) for i, (src, dst) in enumerate(pairs)]
    for copy in copies:
        copy.start()
    return copies


def pack_kernel(pattern, page_slot, rope_in, latent_in, q_nope, q_rope, pages, pay, rope, sems):
    copies = load_all(
        [
            (rope_in, rope),
            (latent_in, pages.at[:, :PAGE, :]),
            (q_nope, pay.at[:, :QN]),
            (q_rope, pay.at[:, QN : QN + QR]),
        ],
        sems,
    )
    copies[0].wait()
    flat = rope[...].astype(F32)
    half = PAGE // 2
    sub = iota((8, 128), 0)
    even = (iota((half, PAGE), 1) == 2 * iota((half, PAGE), 0)).astype(F32)
    odd = (iota((half, PAGE), 1) == 2 * iota((half, PAGE), 0) + 1).astype(F32)
    for page in range(2):
        tiles = []
        for tile in range(half // 8):
            piece = jnp.zeros((8, 128), F32)
            for row in range(8):
                at = (tile * 8 + row) * 128
                piece = jnp.where(sub == row, flat[page : page + 1, at : at + 128], piece)
            tiles.append(piece)
        two_tokens = jnp.concatenate(tiles, axis=0)
        turned = dot(two_tokens[:, :ROPE], even, FIRST) + dot(two_tokens[:, ROPE:], odd, FIRST)
        turned = jnp.concatenate([turned[16 * i : 16 * i + 16] for i in range(4)], axis=1)
        pages[page, PAGE:, :] = turned.astype(BF16)
    lane = iota((ROWS, 128), 1)
    across = iota((ROWS, ROWS), 0) == iota((ROWS, ROWS), 1)
    slot_row = page_slot[...].astype(F32)
    slots, owners = [], []
    for k in range(2):
        names = pattern[k : k + 1, :].astype(F32)
        names = jnp.sum(jnp.where(across, names, 0.0), axis=1, keepdims=True).astype(I32)
        named = lane == names
        slot = jnp.sum(jnp.where(named, slot_row, 0.0), axis=1, keepdims=True)
        slots.append(slot)
        owners.append((lane == lax.shift_right_logical(slot.astype(I32), 1)).astype(F32))
    below = (iota((ROWS, ROWS), 0) > iota((ROWS, ROWS), 1)).astype(F32)
    before0 = dot(below, owners[0])
    before1 = dot(below, owners[1]) + jnp.sum(owners[0], axis=0, keepdims=True)
    rank0 = jnp.sum(owners[0] * before0, axis=1, keepdims=True)
    rank1 = jnp.sum(owners[1] * before1, axis=1, keepdims=True)
    code = jnp.zeros((ROWS, 128), F32)
    for at, value in enumerate((slots[0], slots[1], rank0, rank1)):
        code = jnp.where(lane == at, value, code)
    pay[:, QN + QR :] = code.astype(BF16)
    for copy in copies[1:]:
        copy.wait()


def gather_weights(place, both, half_swap, second, whole, sems):
    core, heads = place[2], HEADS // 2
    pairs = []
    for which, part in ((core, both), (1 - core, half_swap)):
        for y in range(NY):
            to = whole.at[pl.ds(which * heads, heads), :, y * 128 : (y + 1) * 128]
            at = (2 * y + second) * heads if part is both else y * heads
            pairs.append((part.at[pl.ds(at, heads)], to))
    return load_all(pairs, sems)


def query_kernel(
    place, p0_in, p1_in, p2_in, p3_in, both, k_swap, q_lat, q_rot, page_bit, slot_of,
    p0, p1, p2, p3, whole, turned, p_sems, sems,
):
    p_copies = load_all(list(zip((p0_in, p1_in, p2_in, p3_in), (p0, p1, p2, p3))), p_sems)
    copies = gather_weights(place, both, k_swap, 0, whole, sems)
    for copy in p_copies:
        copy.wait()
    z, x, core = place[0], place[1], place[2]
    pays = (p0, p1, p2, p3)
    lane = iota((ROWS, 128), 1)
    wide = iota((ROWS, SLOTS), 1)
    picks, bits, places = ([], []), ([], []), []
    for peer, part in enumerate(pays):
        code = part[:, QN + QR :].astype(F32)
        columns = [
            jnp.sum(jnp.where(lane == at, code, 0.0), axis=1, keepdims=True).astype(I32) for at in range(4)
        ]
        noted = jnp.zeros((ROWS, 128), F32)
        for k in range(2):
            slot, rank = columns[k], columns[2 + k]
            away = (z - lax.shift_right_logical(slot, 4)) * (1 - 2 * core)
            away = lax.bitwise_and(away, NZ - 1)
            order = jnp.where(away < 3, away, jnp.where(away >= 6, away - 3, away + 2))
            other = jnp.where(lax.bitwise_and(lax.shift_right_logical(slot, 1), 1) != core, 1, 0)
            here = lax.bitwise_and(lax.shift_right_logical(slot, 2), 3) == x
            at = jnp.where(here, (order * 2 + other) * 16 + peer * 4 + rank, -1)
            picks[k].append((wide == at).astype(F32))
            bits[k].append(lax.bitwise_and(slot, 1).astype(F32) * jnp.ones((1, 128), F32))
            noted = jnp.where(lane == k, at.astype(F32), noted)
        slot_of[peer * ROWS : (peer + 1) * ROWS, :] = noted
    pick = [jnp.concatenate(p, axis=0) for p in picks]
    bit = [jnp.concatenate(b, axis=0) for b in bits]
    page_bit[...] = dot(pick[0], bit[0], FIRST) + dot(pick[1], bit[1], FIRST)
    turned[...] = jnp.transpose(pick[0] + pick[1]).astype(BF16)
    for copy in copies:
        copy.wait()

    def two_heads(i, carry):
        rot = pl.ds(pl.multiple_of(QN + i * 128, 128), 128)
        gathered = dot(turned[...], jnp.concatenate([p[:, rot] for p in pays], axis=0)).astype(BF16)
        at = pl.ds(pl.multiple_of(i * 2 * NOPE, 128), 2 * NOPE)
        left = dot(turned[...], jnp.concatenate([p[:, at] for p in pays], axis=0)).astype(BF16)
        for k in range(2):
            q_rot[2 * i + k] = gathered[:, k * ROPE : (k + 1) * ROPE]
            q_lat[2 * i + k] = dot(left[:, k * NOPE : (k + 1) * NOPE], whole[2 * i + k]).astype(BF16)
        return carry

    lax.fori_loop(0, HEADS // 2, two_heads, 0)


def start_units(units, held, sems):
    copies = [pltpu.make_async_copy(unit, held.at[i], sems.at[i]) for i, unit in enumerate(units)]
    for copy in copies:
        copy.start()


def attend_units(count, base, unit0, q_lat, q_rot, page_bit, held, sems, result, logs):
    lane = iota((16, 128), 1)

    def block(i):
        unit = held.at[i]
        latent = unit[:, :PAGE, :].reshape(2 * PAGE, KVL)
        rot = unit[:, PAGE:, :]
        keys = jnp.concatenate(
            [
                jnp.concatenate([rot[page, :, 128 * j : 128 * j + 128] for j in range(4)], axis=0)
                for page in range(2)
            ],
            axis=1,
        )
        at = pl.ds(pl.multiple_of((base + i) * 16, 16), 16)
        query = q_lat[:, at, :].reshape(HEADS * 16, KVL)
        query_rot = q_rot[:, at, :].reshape(HEADS * 16, ROPE)
        scores = dot(query, latent, LAST) + dot(query_rot, keys)
        bit = page_bit[at, :]
        bias = jnp.concatenate(
            [jnp.where(bit < 0.5, 0.0, LOW), jnp.where(bit < 0.5, LOW, 0.0)], axis=1
        )
        scores = (scores.reshape(HEADS, 16, 2 * PAGE) + bias[None]).reshape(HEADS * 16, 2 * PAGE)
        top = jnp.max(scores, axis=1, keepdims=True)
        raw = jnp.exp2((scores - top) * (SCALE * LOG2E))
        total = jnp.sum(raw, axis=1, keepdims=True)
        summed = dot(raw.astype(BF16), latent) * (1.0 / total)
        out_at = pl.ds(pl.multiple_of(i * 16, 16), 16)
        result[:, out_at, :] = summed.astype(BF16).reshape(HEADS, 16, KVL)
        log = (top * SCALE + jnp.log(total)).reshape(HEADS, 16, 1)
        spread = jnp.zeros((16, 128), F32)
        for head in range(HEADS):
            mine = (lax.bitwise_and(lane, 15) == head) & (lane < 48)
            spread = jnp.where(mine, log[head], spread)
        logs[out_at, :] = spread

    def body(i, carry):
        for k in range(2):
            pltpu.make_async_copy(unit0, held.at[2 * i + k], sems.at[2 * i + k]).wait()
        for k in range(2):
            block(2 * i + k)
        return carry

    lax.fori_loop(0, count // 2, body, 0)


def early_kernel(*refs):
    units = refs[:EARLY]
    q_lat, q_rot, page_bit, result, logs, held, sems = refs[EARLY:]
    start_units(units, held, sems)
    attend_units(EARLY, 0, units[0], q_lat, q_rot, page_bit, held, sems, result, logs)


def pack_log(log):
    lane = iota(log.shape, 1)
    high = log.astype(BF16).astype(F32)
    rest = log - high
    middle = rest.astype(BF16).astype(F32)
    packed = jnp.where(lane < 16, high, jnp.where(lane < 32, middle, rest - middle))
    return jnp.where(lane < 48, packed, 0.0).astype(BF16)


def late_kernel(*refs):
    units = refs[:LATE]
    (
        place, q_lat, q_rot, page_bit, slot_of, early, early_logs, weights, v_swap,
        r0, r1, r2, r3, held, result, logs, whole, parts, sems, w_sems,
    ) = refs[LATE:]
    start_units(units, held, sems)
    copies = gather_weights(place, weights, v_swap, 1, whole, w_sems)
    attend_units(LATE, EARLY, units[0], q_lat, q_rot, page_bit, held, sems, result, logs)
    highest = lax.Precision.HIGHEST
    wide = iota((SLOTS, SLOTS), 1).astype(F32)
    at0, at1 = slot_of[:, 0:1], slot_of[:, 1:2]
    pick0, pick1 = (wide == at0).astype(F32), (wide == at1).astype(F32)
    partner = dot(pick0, pick1, FIRST) + dot(pick1, pick0, FIRST)
    has = jnp.sum(partner, axis=1, keepdims=True)
    log = jnp.concatenate([early_logs[...], logs[...]], axis=0)
    other = dot(partner, log, precision=highest) + (has - 1.0) * (-LOW)
    top = jnp.maximum(log, other)
    mine = jnp.exp(log - top)
    both = mine + jnp.exp(other - top)
    weight = mine / both
    merged = top + jnp.log(both)
    for copy in copies:
        copy.wait()
    for head in range(HEADS):
        mixed = jnp.concatenate([early[head], result[head]], axis=0)
        part = dot(mixed, whole[head], LAST) * weight[:, head : head + 1]
        parts[:, head * VDIM : (head + 1) * VDIM] = part.astype(BF16)
    first = jnp.where(at0 >= 0.0, 1.0, 0.0)
    row_log = dot(pick0 + pick1 * (1.0 - first), merged, precision=highest)
    none = (at0 < 0.0) & (at1 < 0.0)
    row_log = jnp.where(none, LOW, row_log)
    packed = pack_log(row_log)
    pick = (pick0 + pick1).astype(BF16)
    for peer, out in enumerate((r0, r1, r2, r3)):
        rows = slice(peer * ROWS, (peer + 1) * ROWS)
        out[:, :OUT] = dot(pick[rows], parts[...]).astype(BF16)
        out[:, OUT:] = packed[rows]


def suffix_kernel(
    place, live, q_nope_in, q_rope_in, latent_in, rope_in, both, k_swap, v_swap,
    out, q_nope, q_rope, latent, rope, rope32, query32, rot32, result, logs, whole_k, whole_v,
    k_sems, v_sems, q_sems, lat_sems,
):
    q_copies = load_all([(q_nope_in, q_nope), (q_rope_in, q_rope), (rope_in, rope)], q_sems)
    k_copies = gather_weights(place, both, k_swap, 0, whole_k, k_sems)
    for i in range(ROWS // 8):
        pltpu.make_async_copy(latent_in.at[pl.ds(8 * i, 8)], latent.at[pl.ds(8 * i, 8)], lat_sems.at[i]).start()
    v_copies = gather_weights(place, both, v_swap, 1, whole_v, v_sems)
    for copy in q_copies:
        copy.wait()
    rope32[...] = rope[...].astype(F32)
    across = iota((ROWS, ROWS), 0) == iota((ROWS, ROWS), 1)
    length = jnp.sum(jnp.where(across, live[...].astype(F32), 0.0), axis=1, keepdims=True)
    for copy in k_copies:
        copy.wait()
    for head in range(HEADS):
        projected = dot(q_nope[:, head * NOPE : (head + 1) * NOPE], whole_k[head])
        query32[head] = projected.astype(BF16).astype(F32)
        rot32[head] = q_rope[:, head * ROPE : (head + 1) * ROPE].astype(F32)
    keys, pairs = 8 * SUF, 8 * SUF // 2
    key, pair = iota((keys, pairs), 0), iota((keys, pairs), 1)
    same = lax.shift_right_logical(key, 6) == lax.bitwise_and(pair, 7)
    first = 2 * lax.shift_right_logical(pair, 3)
    even = (same & (lax.bitwise_and(key, SUF - 1) == first)).astype(BF16)
    odd = (same & (lax.bitwise_and(key, SUF - 1) == first + 1)).astype(BF16)
    lane = iota((8, 128), 1)
    col, row = iota((8, keys), 1), iota((8, keys), 0)

    def block(i, live_rows):
        rows = pl.ds(pl.multiple_of(i * 8, 8), 8)
        query = query32[:, rows, :].reshape(HEADS * 8, KVL).astype(BF16)
        query_rot = rot32[:, rows, :].reshape(HEADS * 8, ROPE).astype(BF16)
        lat = latent[rows].reshape(keys, KVL)
        rot = rope32[rows, :]
        rot = jnp.concatenate([rot[:, 128 * j : 128 * j + 128] for j in range(SUF // 2)], axis=0).astype(BF16)
        rot_keys = (dot(even, rot[:, :ROPE]) + dot(odd, rot[:, ROPE:])).astype(BF16)
        scores = dot(query, lat, LAST) + dot(query_rot, rot_keys, LAST)
        seen = (lax.shift_right_logical(col, 6) == row) & (lax.bitwise_and(col, SUF - 1).astype(F32) < live_rows)
        bias = jnp.where(seen, 0.0, LOW)
        scores = (scores.reshape(HEADS, 8, keys) + bias[None]).reshape(HEADS * 8, keys)
        top = jnp.max(scores, axis=1, keepdims=True)
        raw = jnp.exp2((scores - top) * (SCALE * LOG2E))
        total = jnp.sum(raw, axis=1, keepdims=True)
        summed = dot(raw.astype(BF16), lat) * (1.0 / total)
        result[:, rows, :] = summed.reshape(HEADS, 8, KVL)
        log = (top * SCALE + jnp.log(total)).reshape(HEADS, 8, 1)
        spread = jnp.zeros((8, 128), F32)
        for head in range(HEADS):
            spread = jnp.where(lax.bitwise_and(lane, 15) == head, log[head], spread)
        logs[rows, :] = spread

    for i in range(0, ROWS // 8, 2):
        for k in range(2):
            at = latent.at[pl.ds(8 * (i + k), 8)]
            pltpu.make_async_copy(latent_in.at[pl.ds(8 * (i + k), 8)], at, lat_sems.at[i + k]).wait()
        for k in range(2):
            block(i + k, length[8 * (i + k) : 8 * (i + k) + 8])
    for copy in v_copies:
        copy.wait()
    for head in range(HEADS):
        part = dot(result[head].astype(BF16), whole_v[head], LAST)
        out[:, head * VDIM : (head + 1) * VDIM] = part.astype(BF16)
    out[:, OUT:] = pack_log(logs[...])


def final_kernel(own, r0, r1, r2, r3, out):
    gather = (
        (lax.bitwise_and(iota((128, 128), 0), 15) == iota((128, 128), 1)) & (iota((128, 128), 0) < 48)
    ).astype(BF16)
    parts = (own, r0, r1, r2, r3)
    logs = [dot(part[:, OUT:], gather) for part in parts]
    top = functools.reduce(jnp.maximum, logs)
    weights = [jnp.exp(log - top) for log in logs]
    total = 1.0 / functools.reduce(jnp.add, weights)
    weights = [w * total for w in weights]
    for head in range(HEADS):
        at = slice(head * VDIM, (head + 1) * VDIM)
        scaled = [part[:, at].astype(F32) * weight[:, head : head + 1] for part, weight in zip(parts, weights)]
        out[:, at] = functools.reduce(jnp.add, scaled).astype(BF16)


def row_of(z, x, c):
    return ((z % NZ) * NX + x % NX) * NC + c


CHIPS = [(z, x, c) for z in range(NZ) for x in range(NX) for c in range(NC)]


def ring_z(a):
    return lax.ppermute(a, "rows", [(row_of(z, x, c), row_of(z + 1 - 2 * c, x, c)) for z, x, c in CHIPS])


def ring_x(a, steps=1):
    return lax.ppermute(a, "rows", [(row_of(z, x, c), row_of(z, x + steps * (1 - 2 * c), c)) for z, x, c in CHIPS])


def back_x(a, steps=1):
    return ring_x(a, -steps)


def swap(a):
    return lax.ppermute(a, "rows", [(row_of(z, x, c), row_of(z, x, 1 - c)) for z, x, c in CHIPS])


def cost(us):
    return pl.CostEstimate(flops=int(us * 1e6), bytes_accessed=int(us * 3.0e6), transcendentals=0)


def struct(*shape, dtype=BF16):
    return jax.ShapeDtypeStruct(shape, dtype)


def shards(
    q_nope, q_rope, w_uk, w_uv, prefix_latent, prefix_rope, suffix_latent, suffix_rope, page_slot, page_pattern, suffix_len
):
    row, y = lax.axis_index("rows"), lax.axis_index("proj")
    place = jnp.stack([row // (NX * NC), row // NC % NX, row % NC, y]).astype(I32)

    def exchange(a):
        return lax.all_to_all(a, "proj", split_axis=0, concat_axis=0, tiled=True)

    def after(a, *others):
        return lax.optimization_barrier((a, *others))[0]

    def halve(full):
        whole = full.reshape(NY, HEADS, *full.shape[1:])
        half = lax.dynamic_slice_in_dim(whole, (row % NC) * (HEADS // 2), HEADS // 2, 1)
        return half.reshape(NY * HEADS // 2, *full.shape[1:])

    half = (NY, HEADS // 2, NOPE, 128)
    both = jnp.concatenate([halve(w).reshape(half) for w in (w_uk, w_uv)], axis=1).reshape(NY * HEADS, NOPE, 128)
    page_pattern = after(page_pattern, both)
    both = exchange(both)
    pages, pay = pl.pallas_call(
        pack_kernel,
        out_shape=(struct(2, UNIT, KVL), struct(ROWS, PAY)),
        in_specs=[VMEM] * 2 + [HBM] * 4,
        out_specs=(VMEM,) * 2,
        scratch_shapes=[pltpu.VMEM((2, PAGE * ROPE), BF16), pltpu.SemaphoreType.DMA((4,))],
        compiler_params=params(60),
        cost_estimate=cost(2),
        name="pack",
    )(page_pattern.T, page_slot.reshape(1, -1), prefix_rope, prefix_latent, q_nope, q_rope)

    a, b = [pages], [swap(pages)]
    a_pay, b_pay = [pay], [swap(pay)]
    a.append(ring_z(a[0]))
    a_pay.append(ring_x(pay))
    b.append(ring_z(b[0]))
    b_pay.append(ring_x(b_pay[0]))
    a.append(ring_z(after(a[1], a_pay[1])))
    a_pay.append(ring_x(after(a_pay[1], a[1])))
    b.append(ring_z(after(b[1], b_pay[1])))
    pays = [pay, a_pay[1], a_pay[2], swap(b_pay[1])]
    a.append(ring_z(after(a[2], b[1], b_pay[1])))
    b.append(ring_z(b[2]))
    split = both.reshape(NY, HEADS, NOPE, 128)
    k_part, v_part = split[:, : HEADS // 2], split[:, HEADS // 2 :]
    k_swap = swap(after(k_part.reshape(NY * HEADS // 2, NOPE, 128), a[3], b[2], a_pay[2]))
    v_swap = swap(v_part.reshape(NY * HEADS // 2, NOPE, 128))

    q_lat, q_rot, page_bit, slot_of = pl.pallas_call(
        query_kernel,
        out_shape=(
            struct(HEADS, SLOTS, KVL), struct(HEADS, SLOTS, ROPE),
            struct(SLOTS, 128, dtype=F32), struct(4 * ROWS, 128, dtype=F32),
        ),
        in_specs=[SMEM] + [ANY] * 6,
        out_specs=(VMEM,) * 4,
        scratch_shapes=[
            *[pltpu.VMEM((ROWS, PAY), BF16)] * 4,
            pltpu.VMEM((HEADS, NOPE, KVL), BF16), pltpu.VMEM((SLOTS, 4 * ROWS), BF16),
            pltpu.SemaphoreType.DMA((4,)), pltpu.SemaphoreType.DMA((8,)),
        ],
        compiler_params=params(32),
        cost_estimate=cost(4),
        name="queries",
    )(place, *pays, both, k_swap)

    a.append(ring_z(after(a[3], b[2], a_pay[2])))
    a_swap = [None] + [swap(u) for u in a[1:4]]
    b_swap = [None] + [swap(u) for u in b[1:3]]
    early_units = [a[0], b[0], a[1], b[1], a[2], b[2], b_swap[2], a_swap[2], b_swap[1], a_swap[1]]

    early, early_logs = pl.pallas_call(
        early_kernel,
        out_shape=(struct(HEADS, EARLY * 16, KVL), struct(EARLY * 16, 128, dtype=F32)),
        in_specs=[ANY] * EARLY + [VMEM] * 3,
        out_specs=(VMEM, VMEM),
        scratch_shapes=[pltpu.VMEM((EARLY, 2, UNIT, KVL), BF16), pltpu.SemaphoreType.DMA((EARLY,))],
        compiler_params=params(32),
        cost_estimate=cost(1),
        name="early_pages",
    )(*early_units, q_lat, q_rot, page_bit)

    a_swap.append(swap(after(a[4], early_logs)))
    b_swap.append(swap(after(b[3], early_logs)))
    late_units = [a[3], b[3], a[4], a_swap[4], b_swap[3], a_swap[3]]
    returns = pl.pallas_call(
        late_kernel,
        out_shape=(struct(ROWS, RET),) * 4,
        in_specs=[ANY] * LATE + [SMEM] + [VMEM] * 6 + [ANY] * 2,
        out_specs=(VMEM,) * 4,
        scratch_shapes=[
            pltpu.VMEM((LATE, 2, UNIT, KVL), BF16), pltpu.VMEM((HEADS, LATE * 16, KVL), BF16),
            pltpu.VMEM((LATE * 16, 128), F32), pltpu.VMEM((HEADS, VDIM, KVL), BF16), pltpu.VMEM((SLOTS, OUT), BF16),
            pltpu.SemaphoreType.DMA((LATE,)), pltpu.SemaphoreType.DMA((8,)),
        ],
        compiler_params=params(32),
        cost_estimate=cost(7),
        name="late_pages",
    )(*late_units, place, q_lat, q_rot, page_bit, slot_of, early, early_logs, both, v_swap)

    backs = [returns[0], back_x(returns[1]), back_x(returns[2], 2), ring_x(returns[3])]
    k_swap, returns = lax.optimization_barrier((k_swap, returns))
    own = pl.pallas_call(
        suffix_kernel,
        out_shape=struct(ROWS, RET),
        in_specs=[SMEM, VMEM] + [HBM] * 4 + [ANY] * 3,
        out_specs=VMEM,
        scratch_shapes=[
            pltpu.VMEM((ROWS, QN), BF16), pltpu.VMEM((ROWS, QR), BF16),
            pltpu.VMEM((ROWS, SUF, KVL), BF16), pltpu.VMEM((ROWS, SUF * ROPE), BF16),
            pltpu.VMEM((ROWS, SUF * ROPE), F32), pltpu.VMEM((HEADS, ROWS, KVL), F32),
            pltpu.VMEM((HEADS, ROWS, ROPE), F32), pltpu.VMEM((HEADS, ROWS, KVL), F32), pltpu.VMEM((ROWS, 128), F32),
            pltpu.VMEM((HEADS, NOPE, KVL), BF16), pltpu.VMEM((HEADS, VDIM, KVL), BF16),
            pltpu.SemaphoreType.DMA((8,)), pltpu.SemaphoreType.DMA((8,)),
            pltpu.SemaphoreType.DMA((3,)), pltpu.SemaphoreType.DMA((8,)),
        ],
        compiler_params=params(60),
        cost_estimate=cost(8),
        name="suffix",
    )(place, suffix_len.reshape(1, -1), q_nope, q_rope, suffix_latent, suffix_rope, both, k_swap, v_swap)

    return pl.pallas_call(
        final_kernel,
        out_shape=struct(ROWS, OUT),
        in_specs=[VMEM] * 5,
        out_specs=VMEM,
        compiler_params=params(16),
        cost_estimate=cost(2),
        name="combine",
    )(own, *backs)


def solution(mesh):
    return jax.shard_map(
        shards,
        mesh=mesh,
        in_specs=(
            P("rows", "proj"), P("rows", "proj"), P(None, None, "proj"), P(None, None, "proj"),
            P("rows", None, None), P("rows", None), P("rows", None, None), P("rows", None),
            P(), P("rows", None), P("rows"),
        ),
        out_specs=P("rows", "proj"),
        check_vma=False,
    )
```

time: 120 us -> 99.9 us (0.83)
  starting transfers between devices: 47.9 us -> 38.1 us
  local copies, waits for them, and re-layouts: 17.9 us -> 10.6 us
  waiting for transfers between devices: 14.8 us -> 10.1 us
  other arithmetic: 0.08 us -> 1.6 us
    ppermute x10 -> x6, waiting for transfers between devices: 12.3 us -> 0.02 us  [ring_x(): lax.ppermute(a, 'rows', [(row_of(z, x, c), row_of(z, x + steps * (1 - 2 *...]
    unnamed x41 -> x46, local copies, waits for them, and re-layouts: 17.8 us -> 7.69 us
    ppermute x10 -> x6, starting transfers between devices: 17.7 us -> 8.2 us  [ring_x(): lax.ppermute(a, 'rows', [(row_of(z, x, c), row_of(z, x + steps * (1 - 2 *...]
    ppermute x12, waiting for transfers between devices: 0.03 us -> 5.94 us  [swap(): lax.ppermute(a, 'rows', [(row_of(z, x, c), row_of(z, x, 1 - c)) for z, x,...]
    all_to_all x0 -> x1, starting transfers between devices: none -> 5.01 us  [exchange(): return lax.all_to_all(a, 'proj', split_axis=0, concat_axis=0, tiled=True)]
    pallas_call x2, Pallas kernels: 12.7 us -> 17 us  [the longest x1 14.2 us: shards(): pl.pallas_call(suffix_kernel, out_shape=struct(ROWS, RET), in_specs=[SMEM...]
    ppermute x12, starting transfers between devices: 11.5 us -> 7.87 us  [swap(): lax.ppermute(a, 'rows', [(row_of(z, x, c), row_of(z, x, 1 - c)) for z, x,...]
    dynamic_slice x0 -> x1, local copies, waits for them, and re-layouts: none -> 1.78 us  [halve(): lax.dynamic_slice_in_dim(whole, row % NC * (HEADS // 2), HEADS // 2, 1)]
  transfers between devices with their start and end apart: 29 -> 26, of which waited for: 5 -> 6; matrix products, arithmetic and copies ran while one was open for 0% -> 1% of each run, Pallas kernels for 21% -> 29%
where the time goes in v2:
time: 99.9 us; the launch traced here: 99.5 us
  Pallas kernels  38.9 us (39%)
  starting transfers between devices  38.1 us (38%)
  local copies, waits for them, and re-layouts  10.6 us (11%)
  waiting for transfers between devices  10.1 us (10%)
  other arithmetic  1.6 us (2%)
    ppermute x7, starting transfers between devices, ring_z(): lax.ppermute(a, 'rows', [(row_of(z, x, c), row_of(z + 1 - 2 * c, x, c)) f...  17 us
    pallas_call x1, Pallas kernels, shards(): pl.pallas_call(suffix_kernel, out_shape=struct(ROWS, RET), in_specs=[SMEM...  14.2 us
    pallas_call x1, Pallas kernels, shards(): pl.pallas_call(late_kernel, out_shape=(struct(ROWS, RET),) * 4, in_specs=...  8.22 us
    ppermute x6, starting transfers between devices, ring_x(): lax.ppermute(a, 'rows', [(row_of(z, x, c), row_of(z, x + steps * (1 - 2 *...  8.2 us
    ppermute x12, starting transfers between devices, swap(): lax.ppermute(a, 'rows', [(row_of(z, x, c), row_of(z, x, 1 - c)) for z, x,...  7.87 us
    unnamed x46, local copies, waits for them, and re-layouts  7.69 us
    pallas_call x1, Pallas kernels, shards(): pl.pallas_call(query_kernel, out_shape=(struct(HEADS, SLOTS, KVL), struct...  6.17 us
    ppermute x12, waiting for transfers between devices, swap(): lax.ppermute(a, 'rows', [(row_of(z, x, c), row_of(z, x, 1 - c)) for z, x,...  5.94 us
  transfers between devices with their start and end apart: 26, of which 6 were waited for; matrix products, arithmetic and copies ran while one was open for 1% of the time, Pallas kernels for 29%

profile of v2, /device:TPU:1, one launch (start us, length us, event | category | flops | bytes accessed | tf_op | source)
XLA Modules:
  0.0 99.5 jit_solution(16625243400649432259)
XLA Ops:
  0.0 1.8 %constant_dynamic-slice_fusion = (bf16[4,8,128,128]{3,2,1,0:T(8,128)(2,1)S(1)}, bf16[4,8,128,128]{3,2,1,0:T(8,128)(2,1)S(1)}) fusion(bf16[4,16,128,128]{3,2,1,0:T(8,128)(2,1)} %bitcast.16, s32[]{:T(128)S(6)} %select_n.30, bf16[4,16,128,128]{3,2,1,0:T(8,128)(2,1)} %bitcast.17), kind=kLoop, calls=%fused_computation.2 | loop fusion | bytes 4194308 | tf_op jit(solution)/shard_map/dynamic_slice | solution.py:413
  1.8 1.5 %pad_maximum_fusion = bf16[4,16,128,128]{3,2,1,0:T(8,128)(2,1)} fusion(bf16[4,8,128,128]{3,2,1,0:T(8,128)(2,1)S(1)} %get-tuple-element.51, bf16[4,8,128,128]{3,2,1,0:T(8,128)(2,1)S(1)} %get-tuple-element.52), kind=kLoop, calls=%fused_computation | loop fusion | flops 1048576 | bytes 4194304 | tf_op jit(solution)/shard_map/concatenate | solution.py:417
  3.3 5.0 %all-to-all-start = ((bf16[64,128,128]{2,1,0:T(8,128)(2,1)}), bf16[64,128,128]{2,1,0:T(8,128)(2,1)S(1)}, u32[]{:S(2)}, u32[]{:S(2)}) async-start(bf16[64,128,128]{2,1,0:T(8,128)(2,1)} %bitcast.14), calls=%async_computation | async-start | bytes 4194304 | tf_op jit(solution)/shard_map/all_to_all | solution.py:406
  8.3 2.8 %pack.1 = (bf16[2,144,512]{2,1,0:T(8,128)(2,1)}, bf16[64,3200]{1,0:T(8,128)(2,1)}) custom-call(s32[2,64]{1,0:T(2,128)} %bitcast.18, s32[1,128]{1,0:T(1,128)} %bitcast.19, bf16[2,8192]{1,0:T(2,128)(2,1)} %rope_in.2, bf16[2,128,512]{2,1,0:T(8,128)(2,1)} %latent_in.2, bf16[64,2048]{1,0:T(8,128)(2,1)} %q_nope_in.1, bf16[64,1024]{1,0:T(8,128)(2,1)} %q_rope_in.1), custom_call_target="tpu_custom_call" | custom-call | flops 2000000 | bytes 6000000 | tf_op jit(solution)/shard_map/pack/pallas_call | solution.py:420
  11.1 1.9 %collective-permute-start.5 = (bf16[64,3200]{1,0:T(8,128)(2,1)}, bf16[64,3200]{1,0:T(8,128)(2,1)S(1)}, u32[]{:S(2)}, u32[]{:S(2)}) collective-permute-start(bf16[64,3200]{1,0:T(8,128)(2,1)} %get-tuple-element.29.p0_in), channel_id=1, source_target_pairs={{0,4},{4,0},{8,12},{12,8},{16,20},{20,16},{24,28},{28,24},{32,36},... | collective-permute-start | bytes 1228808 | tf_op jit(solution)/shard_map/ppermute | solution.py:388
  13.1 1.6 %collective-permute-start.1 = (bf16[64,3200]{1,0:T(8,128)(2,1)}, bf16[64,3200]{1,0:T(8,128)(2,1)S(1)}, u32[]{:S(2)}, u32[]{:S(2)}) collective-permute-start(bf16[64,3200]{1,0:T(8,128)(2,1)} %get-tuple-element.29.p0_in), channel_id=1, source_target_pairs={{0,8},{4,28},{8,16},{12,4},{16,24},{20,12},{24,0},{28,20},{32,40},... | collective-permute-start | bytes 1228808 | tf_op jit(solution)/shard_map/ppermute | solution.py:380
  14.6 5.6 %collective-permute-start = (bf16[2,144,512]{2,1,0:T(8,128)(2,1)}, bf16[2,144,512]{2,1,0:T(8,128)(2,1)S(1)}, u32[]{:S(2)}, u32[]{:S(2)}) collective-permute-start(bf16[2,144,512]{2,1,0:T(8,128)(2,1)} %get-tuple-element.28.refs_0_), channel_id=1, source_target_pairs={{0,32},{4,228},{8,40},{12,236},{16,48},{20,244},{24,56},{28,252},{... | collective-permute-start | bytes 884744 | tf_op jit(solution)/shard_map/ppermute | solution.py:376
  20.8 1.2 %collective-permute-start.4 = (bf16[2,144,512]{2,1,0:T(8,128)(2,1)S(1)}, bf16[2,144,512]{2,1,0:T(8,128)(2,1)}, u32[]{:S(2)}, u32[]{:S(2)}) collective-permute-start(bf16[2,144,512]{2,1,0:T(8,128)(2,1)S(1)} %collective-permute-done.3.refs_1_), channel_id=1, source_target_pairs={{0,32},{4,228},{8,40},{12,236},{16,48},{20,244},{24,56},{28,252},{... | collective-permute-start | bytes 884744 | tf_op jit(solution)/shard_map/ppermute | solution.py:376
  22.8 1.4 %collective-permute-done.refs_2_ = bf16[2,144,512]{2,1,0:T(8,128)(2,1)S(1)} collective-permute-done((bf16[2,144,512]{2,1,0:T(8,128)(2,1)}, bf16[2,144,512]{2,1,0:T(8,128)(2,1)S(1)}, u32[]{:S(2)}, u32[]{:S(2)}) %collective-permute-start) | collective-permute-done | bytes 294944 | tf_op jit(solution)/shard_map/ppermute | solution.py:376
  24.2 3.4 %collective-permute-start.2 = (bf16[2,144,512]{2,1,0:T(8,128)(2,1)S(1)}, bf16[2,144,512]{2,1,0:T(8,128)(2,1)}, u32[]{:S(2)}, u32[]{:S(2)}) collective-permute-start(bf16[2,144,512]{2,1,0:T(8,128)(2,1)S(1)} %collective-permute-done.refs_2_), channel_id=1, source_target_pairs={{0,32},{4,228},{8,40},{12,236},{16,48},{20,244},{24,56},{28,252},{... | collective-permute-start | bytes 884744 | tf_op jit(solution)/shard_map/ppermute | solution.py:376
  27.6 1.1 %collective-permute-start.9 = (bf16[64,3200]{1,0:T(8,128)(2,1)S(1)}, bf16[64,3200]{1,0:T(8,128)(2,1)S(1)}, u32[]{:S(2)}, u32[]{:S(2)}) collective-permute-start(bf16[64,3200]{1,0:T(8,128)(2,1)S(1)} %collective-permute-done.1.p1_in), channel_id=1, source_target_pairs={{0,8},{4,28},{8,16},{12,4},{16,24},{20,12},{24,0},{28,20},{32,40},... | collective-permute-start | bytes 1228808 | tf_op jit(solution)/shard_map/ppermute | solution.py:380
  28.8 1.9 %collective-permute-start.8 = (bf16[2,144,512]{2,1,0:T(8,128)(2,1)}, bf16[2,144,512]{2,1,0:T(8,128)(2,1)}, u32[]{:S(2)}, u32[]{:S(2)}) collective-permute-start(bf16[2,144,512]{2,1,0:T(8,128)(2,1)} %collective-permute-done.4.refs_3_), channel_id=1, source_target_pairs={{0,32},{4,228},{8,40},{12,236},{16,48},{20,244},{24,56},{28,252},{... | collective-permute-start | bytes 884744 | tf_op jit(solution)/shard_map/ppermute | solution.py:376
  31.3 3.4 %collective-permute-start.7 = (bf16[2,144,512]{2,1,0:T(8,128)(2,1)}, bf16[2,144,512]{2,1,0:T(8,128)(2,1)}, u32[]{:S(2)}, u32[]{:S(2)}) collective-permute-start(bf16[2,144,512]{2,1,0:T(8,128)(2,1)} %collective-permute-done.2.refs_4_), channel_id=1, source_target_pairs={{0,32},{4,228},{8,40},{12,236},{16,48},{20,244},{24,56},{28,252},{... | collective-permute-start | bytes 884744 | tf_op jit(solution)/shard_map/ppermute | solution.py:376
  34.7 1.1 %fusion = (bf16[4,8,128,128]{3,2,1,0:T(8,128)(2,1)}, bf16[4,8,128,128]{3,2,1,0:T(8,128)(2,1)S(1)}) fusion(bf16[4,16,128,128]{3,2,1,0:T(8,128)(2,1)S(1)} %bitcast.13), kind=kLoop, calls=%fused_computation.4 | loop fusion | bytes 4194304 | tf_op jit(solution)/shard_map/slice | solution.py:444
  35.8 0.8 copy-done.6
  36.6 2.1 %collective-permute-done.7.refs_0_ = bf16[2,144,512]{2,1,0:T(8,128)(2,1)} collective-permute-done((bf16[2,144,512]{2,1,0:T(8,128)(2,1)}, bf16[2,144,512]{2,1,0:T(8,128)(2,1)}, u32[]{:S(2)}, u32[]{:S(2)}) %collective-permute-start.7) | collective-permute-done | bytes 294944 | tf_op jit(solution)/shard_map/ppermute | solution.py:376
  38.7 3.6 %collective-permute-start.10 = (bf16[32,128,128]{2,1,0:T(8,128)(2,1)S(1)}, bf16[32,128,128]{2,1,0:T(8,128)(2,1)S(1)}, u32[]{:S(2)}, u32[]{:S(2)}) collective-permute-start(bf16[32,128,128]{2,1,0:T(8,128)(2,1)S(1)} %bitcast.15), channel_id=1, source_target_pairs={{0,4},{4,0},{8,12},{12,8},{16,20},{20,16},{24,28},{28,24},{32,36},... | collective-permute-start | bytes 3145736 | tf_op jit(solution)/shard_map/ppermute | solution.py:388
  43.3 4.2 %collective-permute-done.16.refs_9_ = bf16[2,144,512]{2,1,0:T(8,128)(2,1)S(1)} collective-permute-done((bf16[2,144,512]{2,1,0:T(8,128)(2,1)S(1)}, bf16[2,144,512]{2,1,0:T(8,128)(2,1)S(1)}, u32[]{:S(2)}, u32[]{:S(2)}) %collective-permute-start.16) | collective-permute-done | bytes 294944 | tf_op jit(solution)/shard_map/ppermute | solution.py:388
  50.2 0.8 collective-permute-start.11
  51.8 1.0 %copy-done.5 = bf16[64,3200]{1,0:T(8,128)(2,1)S(1)} copy-done((bf16[64,3200]{1,0:T(8,128)(2,1)S(1)}, bf16[64,3200]{1,0:T(8,128)(2,1)}, u32[]{:S(2)}) %copy-start.5) | copy-done | bytes 409624
  52.8 1.0 %copy-done.7 = bf16[64,3200]{1,0:T(8,128)(2,1)S(1)} copy-done((bf16[64,3200]{1,0:T(8,128)(2,1)S(1)}, bf16[64,3200]{1,0:T(8,128)(2,1)}, u32[]{:S(2)}) %copy-start.7) | copy-done | bytes 409624
  53.8 1.0 %copy-done.9 = bf16[64,3200]{1,0:T(8,128)(2,1)S(1)} copy-done((bf16[64,3200]{1,0:T(8,128)(2,1)S(1)}, bf16[64,3200]{1,0:T(8,128)(2,1)}, u32[]{:S(2)}) %copy-start.9) | copy-done | bytes 409624
  54.9 6.2 %queries.1 = (bf16[16,256,512]{2,1,0:T(8,128)(2,1)S(1)}, bf16[16,256,64]{2,1,0:T(8,128)(2,1)S(1)}, f32[256,128]{1,0:T(8,128)S(1)}, f32[256,128]{1,0:T(8,128)S(1)}) custom-call(s32[4]{0:T(128)S(1)} %pad_add_fusion.place.refs_6_, bf16[64,3200]{1,0:T(8,128)(2,1)S(1)} %copy-done.3, bf16[64,3200]{1,0:T(8,128)(2,1)S(1)} %copy-done.5, ...), custom_call_target="tpu_custom_call" | custom-call | flops 4000000 | bytes 12000000 | tf_op jit(solution)/shard_map/queries/pallas_call | solution.py:448
  61.2 5.8 %early_pages.1 = (bf16[16,160,512]{2,1,0:T(8,128)(2,1)S(1)}, f32[160,128]{1,0:T(8,128)S(1)}) custom-call(bf16[2,144,512]{2,1,0:T(8,128)(2,1)S(1)} %copy-done.10, bf16[2,144,512]{2,1,0:T(8,128)(2,1)S(1)} %copy-done.12, bf16[2,144,512]{2,1,0:T(8,128)(2,1)S(1)} %copy-done.15, bf16[2,144,512]{2,1,0:T(8,128)(2,1)} %collective-permute-done.4.refs_3_, ...), custom_call_target="tpu_custom_call" | custom-call | flops 1000000 | bytes 3000000 | tf_op jit(solution)/shard_map/early_pages/pallas_call | solution.py:471
  67.8 1.3 %collective-permute-done.19.refs_4_ = bf16[2,144,512]{2,1,0:T(8,128)(2,1)S(1)} collective-permute-done((bf16[2,144,512]{2,1,0:T(8,128)(2,1)}, bf16[2,144,512]{2,1,0:T(8,128)(2,1)S(1)}, u32[]{:S(2)}, u32[]{:S(2)}) %collective-permute-start.19) | collective-permute-done | bytes 294944 | tf_op jit(solution)/shard_map/ppermute | solution.py:388
  69.5 8.2 %late_pages.1 = (bf16[64,2176]{1,0:T(8,128)(2,1)S(1)}, bf16[64,2176]{1,0:T(8,128)(2,1)S(1)}, bf16[64,2176]{1,0:T(8,128)(2,1)S(1)}, bf16[64,2176]{1,0:T(8,128)(2,1)S(1)}) custom-call(bf16[2,144,512]{2,1,0:T(8,128)(2,1)} %collective-permute-done.7.refs_0_, bf16[2,144,512]{2,1,0:T(8,128)(2,1)} %collective-permute-done.11.refs_1_, ...), custom_call_target="tpu_custom_call" | custom-call | flops 7000000 | bytes 21000000 | tf_op jit(solution)/shard_map/late_pages/pallas_call | solution.py:485
  77.7 1.3 %collective-permute-start.22 = (bf16[64,2176]{1,0:T(8,128)(2,1)S(1)}, bf16[64,2176]{1,0:T(8,128)(2,1)S(1)}, u32[]{:S(2)}, u32[]{:S(2)}) collective-permute-start(bf16[64,2176]{1,0:T(8,128)(2,1)S(1)} %get-tuple-element.45), channel_id=1, source_target_pairs={{0,24},{4,12},{8,0},{12,20},{16,8},{20,28},{24,16},{28,4},{32,56},... | collective-permute-start | bytes 835592 | tf_op jit(solution)/shard_map/ppermute | solution.py:380
  79.0 2.4 %collective-permute-start.23 = (bf16[64,2176]{1,0:T(8,128)(2,1)S(1)}, bf16[64,2176]{1,0:T(8,128)(2,1)S(1)}, u32[]{:S(2)}, u32[]{:S(2)}) collective-permute-start(bf16[64,2176]{1,0:T(8,128)(2,1)S(1)} %get-tuple-element.46), channel_id=1, source_target_pairs={{0,16},{4,20},{8,24},{12,28},{16,0},{20,4},{24,8},{28,12},{32,48},... | collective-permute-start | bytes 835592 | tf_op jit(solution)/shard_map/ppermute | solution.py:380
  81.5 1.1 %collective-permute-start.24 = (bf16[64,2176]{1,0:T(8,128)(2,1)S(1)}, bf16[64,2176]{1,0:T(8,128)(2,1)S(1)}, u32[]{:S(2)}, u32[]{:S(2)}) collective-permute-start(bf16[64,2176]{1,0:T(8,128)(2,1)S(1)} %get-tuple-element.47), channel_id=1, source_target_pairs={{0,8},{4,28},{8,16},{12,4},{16,24},{20,12},{24,0},{28,20},{32,40},... | collective-permute-start | bytes 835592 | tf_op jit(solution)/shard_map/ppermute | solution.py:380
  82.6 14.2 %suffix.1.own = bf16[64,2176]{1,0:T(8,128)(2,1)} custom-call(s32[4]{0:T(128)} %copy-done.20, s32[1,64]{1,0:T(1,128)} %bitcast.20, bf16[64,2048]{1,0:T(8,128)(2,1)} %q_nope_in.1, bf16[64,1024]{1,0:T(8,128)(2,1)} %q_rope_in.1, bf16[64,64,512]{2,1,0:T(8,128)(2,1)} %latent_in.3, bf16[64,4096]{1,0:T(8,128)(2,1)} %rope_in.3, bf16[64,128,128]{2,1,0:T(8,128)(2,1)} %copy-done, ...), custom_call_target="tpu_custom_call" | custom-call | flops 8000000 | bytes 24000000 | tf_op jit(solution)/shard_map/suffix/pallas_call | solution.py:502
  96.9 0.9 copy-done.2
  97.8 1.6 %combine.1 = bf16[64,2048]{1,0:T(8,128)(2,1)} custom-call(bf16[64,2176]{1,0:T(8,128)(2,1)S(1)} %copy-done.2, bf16[64,2176]{1,0:T(8,128)(2,1)S(1)} %get-tuple-element.44.r0, bf16[64,2176]{1,0:T(8,128)(2,1)S(1)} %collective-permute-done.22.r1, bf16[64,2176]{1,0:T(8,128)(2,1)S(1)} %collective-permute-done.23.r2, bf16[64,2176]{1,0:T(8,128)(2,1)S(1)} %collective-permute-done.24.r3), custom_call_target="tpu_custom_call" | custom-call | flops 2000000 | bytes 6000000 | tf_op jit(solution)/shard_map/combine/pallas_call | solution.py:521
  (76 shorter events, 7.7 us)
Async XLA Ops:
  3.3 31.4 %all-to-all-start = ((bf16[64,128,128]{2,1,0:T(8,128)(2,1)}), bf16[64,128,128]{2,1,0:T(8,128)(2,1)S(1)}, u32[]{:S(2)}, u32[]{:S(2)}) async-start(bf16[64,128,128]{2,1,0:T(8,128)(2,1)} %bitcast.14), calls=%async_computation | async-start | bytes 4194304 | tf_op jit(solution)/shard_map/all_to_all | solution.py:406
  11.1 9.1 %collective-permute-start.5 = (bf16[64,3200]{1,0:T(8,128)(2,1)}, bf16[64,3200]{1,0:T(8,128)(2,1)S(1)}, u32[]{:S(2)}, u32[]{:S(2)}) collective-permute-start(bf16[64,3200]{1,0:T(8,128)(2,1)} %get-tuple-element.29.p0_in), channel_id=1, source_target_pairs={{0,4},{4,0},{8,12},{12,8},{16,20},{20,16},{24,28},{28,24},{32,36},... | collective-permute-start | bytes 1228808 | tf_op jit(solution)/shard_map/ppermute | solution.py:388
  13.1 11.2 %collective-permute-start.1 = (bf16[64,3200]{1,0:T(8,128)(2,1)}, bf16[64,3200]{1,0:T(8,128)(2,1)S(1)}, u32[]{:S(2)}, u32[]{:S(2)}) collective-permute-start(bf16[64,3200]{1,0:T(8,128)(2,1)} %get-tuple-element.29.p0_in), channel_id=1, source_target_pairs={{0,8},{4,28},{8,16},{12,4},{16,24},{20,12},{24,0},{28,20},{32,40},... | collective-permute-start | bytes 1228808 | tf_op jit(solution)/shard_map/ppermute | solution.py:380
  14.6 6.2 %collective-permute-start.3 = (bf16[2,144,512]{2,1,0:T(8,128)(2,1)}, bf16[2,144,512]{2,1,0:T(8,128)(2,1)S(1)}, u32[]{:S(2)}, u32[]{:S(2)}) collective-permute-start(bf16[2,144,512]{2,1,0:T(8,128)(2,1)} %get-tuple-element.28.refs_0_), channel_id=1, source_target_pairs={{0,4},{4,0},{8,12},{12,8},{16,20},{20,16},{24,28},{28,24},{32,36},... | collective-permute-start | bytes 884744 | tf_op jit(solution)/shard_map/ppermute | solution.py:388
  14.6 9.6 %collective-permute-start = (bf16[2,144,512]{2,1,0:T(8,128)(2,1)}, bf16[2,144,512]{2,1,0:T(8,128)(2,1)S(1)}, u32[]{:S(2)}, u32[]{:S(2)}) collective-permute-start(bf16[2,144,512]{2,1,0:T(8,128)(2,1)} %get-tuple-element.28.refs_0_), channel_id=1, source_target_pairs={{0,32},{4,228},{8,40},{12,236},{16,48},{20,244},{24,56},{28,252},{... | collective-permute-start | bytes 884744 | tf_op jit(solution)/shard_map/ppermute | solution.py:376
  20.2 8.5 %collective-permute-start.6 = (bf16[64,3200]{1,0:T(8,128)(2,1)S(1)}, bf16[64,3200]{1,0:T(8,128)(2,1)S(1)}, u32[]{:S(2)}, u32[]{:S(2)}) collective-permute-start(bf16[64,3200]{1,0:T(8,128)(2,1)S(1)} %collective-permute-done.5), channel_id=1, source_target_pairs={{0,8},{4,28},{8,16},{12,4},{16,24},{20,12},{24,0},{28,20},{32,40},... | collective-permute-start | bytes 1228808 | tf_op jit(solution)/shard_map/ppermute | solution.py:380
  20.8 7.9 %collective-permute-start.4 = (bf16[2,144,512]{2,1,0:T(8,128)(2,1)S(1)}, bf16[2,144,512]{2,1,0:T(8,128)(2,1)}, u32[]{:S(2)}, u32[]{:S(2)}) collective-permute-start(bf16[2,144,512]{2,1,0:T(8,128)(2,1)S(1)} %collective-permute-done.3.refs_1_), channel_id=1, source_target_pairs={{0,32},{4,228},{8,40},{12,236},{16,48},{20,244},{24,56},{28,252},{... | collective-permute-start | bytes 884744 | tf_op jit(solution)/shard_map/ppermute | solution.py:376
  24.2 11.6 %copy-start.4 = (bf16[64,3200]{1,0:T(8,128)(2,1)}, bf16[64,3200]{1,0:T(8,128)(2,1)S(1)}, u32[]{:S(2)}) copy-start(bf16[64,3200]{1,0:T(8,128)(2,1)S(1)} %collective-permute-done.1.p1_in) | copy-start | bytes 1228804
  24.2 7.0 %collective-permute-start.2 = (bf16[2,144,512]{2,1,0:T(8,128)(2,1)S(1)}, bf16[2,144,512]{2,1,0:T(8,128)(2,1)}, u32[]{:S(2)}, u32[]{:S(2)}) collective-permute-start(bf16[2,144,512]{2,1,0:T(8,128)(2,1)S(1)} %collective-permute-done.refs_2_), channel_id=1, source_target_pairs={{0,32},{4,228},{8,40},{12,236},{16,48},{20,244},{24,56},{28,252},{... | collective-permute-start | bytes 884744 | tf_op jit(solution)/shard_map/ppermute | solution.py:376
  27.6 8.2 %collective-permute-start.9 = (bf16[64,3200]{1,0:T(8,128)(2,1)S(1)}, bf16[64,3200]{1,0:T(8,128)(2,1)S(1)}, u32[]{:S(2)}, u32[]{:S(2)}) collective-permute-start(bf16[64,3200]{1,0:T(8,128)(2,1)S(1)} %collective-permute-done.1.p1_in), channel_id=1, source_target_pairs={{0,8},{4,28},{8,16},{12,4},{16,24},{20,12},{24,0},{28,20},{32,40},... | collective-permute-start | bytes 1228808 | tf_op jit(solution)/shard_map/ppermute | solution.py:380
  28.8 7.8 %collective-permute-start.8 = (bf16[2,144,512]{2,1,0:T(8,128)(2,1)}, bf16[2,144,512]{2,1,0:T(8,128)(2,1)}, u32[]{:S(2)}, u32[]{:S(2)}) collective-permute-start(bf16[2,144,512]{2,1,0:T(8,128)(2,1)} %collective-permute-done.4.refs_3_), channel_id=1, source_target_pairs={{0,32},{4,228},{8,40},{12,236},{16,48},{20,244},{24,56},{28,252},{... | collective-permute-start | bytes 884744 | tf_op jit(solution)/shard_map/ppermute | solution.py:376
  31.3 7.4 %collective-permute-start.7 = (bf16[2,144,512]{2,1,0:T(8,128)(2,1)}, bf16[2,144,512]{2,1,0:T(8,128)(2,1)}, u32[]{:S(2)}, u32[]{:S(2)}) collective-permute-start(bf16[2,144,512]{2,1,0:T(8,128)(2,1)} %collective-permute-done.2.refs_4_), channel_id=1, source_target_pairs={{0,32},{4,228},{8,40},{12,236},{16,48},{20,244},{24,56},{28,252},{... | collective-permute-start | bytes 884744 | tf_op jit(solution)/shard_map/ppermute | solution.py:376
  34.7 34.8 %copy-start = (bf16[64,128,128]{2,1,0:T(8,128)(2,1)}, bf16[64,128,128]{2,1,0:T(8,128)(2,1)S(1)}, u32[]{:S(2)}) copy-start(bf16[64,128,128]{2,1,0:T(8,128)(2,1)S(1)} %all-to-all-done.both.refs_13_) | copy-start | bytes 6291460
  34.7 8.1 %copy-start.14 = (bf16[2,144,512]{2,1,0:T(8,128)(2,1)S(1)}, bf16[2,144,512]{2,1,0:T(8,128)(2,1)}, u32[]{:S(2)}) copy-start(bf16[2,144,512]{2,1,0:T(8,128)(2,1)} %copy-done.13) | copy-start | bytes 884740
  34.7 17.1 %copy-start.3 = (bf16[64,3200]{1,0:T(8,128)(2,1)S(1)}, bf16[64,3200]{1,0:T(8,128)(2,1)}, u32[]{:S(2)}) copy-start(bf16[64,3200]{1,0:T(8,128)(2,1)} %get-tuple-element.29.p0_in) | copy-start | bytes 1228804
  38.7 12.4 %collective-permute-start.10 = (bf16[32,128,128]{2,1,0:T(8,128)(2,1)S(1)}, bf16[32,128,128]{2,1,0:T(8,128)(2,1)S(1)}, u32[]{:S(2)}, u32[]{:S(2)}) collective-permute-start(bf16[32,128,128]{2,1,0:T(8,128)(2,1)S(1)} %bitcast.15), channel_id=1, source_target_pairs={{0,4},{4,0},{8,12},{12,8},{16,20},{20,16},{24,28},{28,24},{32,36},... | collective-permute-start | bytes 3145736 | tf_op jit(solution)/shard_map/ppermute | solution.py:388
  42.3 25.5 %collective-permute-start.21 = (bf16[32,128,128]{2,1,0:T(8,128)(2,1)}, bf16[32,128,128]{2,1,0:T(8,128)(2,1)}, u32[]{:S(2)}, u32[]{:S(2)}) collective-permute-start(bf16[32,128,128]{2,1,0:T(8,128)(2,1)} %bitcast.12), channel_id=1, source_target_pairs={{0,4},{4,0},{8,12},{12,8},{16,20},{20,16},{24,28},{28,24},{32,36},... | collective-permute-start | bytes 3145736 | tf_op jit(solution)/shard_map/ppermute | solution.py:388
  42.3 7.2 %collective-permute-start.17 = (bf16[64,3200]{1,0:T(8,128)(2,1)S(1)}, bf16[64,3200]{1,0:T(8,128)(2,1)S(1)}, u32[]{:S(2)}, u32[]{:S(2)}) collective-permute-start(bf16[64,3200]{1,0:T(8,128)(2,1)S(1)} %copy-done.22), channel_id=1, source_target_pairs={{0,4},{4,0},{8,12},{12,8},{16,20},{20,16},{24,28},{28,24},{32,36},... | collective-permute-start | bytes 1228808 | tf_op jit(solution)/shard_map/ppermute | solution.py:388
  42.8 4.7 %collective-permute-start.16 = (bf16[2,144,512]{2,1,0:T(8,128)(2,1)S(1)}, bf16[2,144,512]{2,1,0:T(8,128)(2,1)S(1)}, u32[]{:S(2)}, u32[]{:S(2)}) collective-permute-start(bf16[2,144,512]{2,1,0:T(8,128)(2,1)S(1)} %copy-done.14), channel_id=1, source_target_pairs={{0,4},{4,0},{8,12},{12,8},{16,20},{20,16},{24,28},{28,24},{32,36},... | collective-permute-start | bytes 884744 | tf_op jit(solution)/shard_map/ppermute | solution.py:388
  42.9 5.7 %collective-permute-start.15 = (bf16[2,144,512]{2,1,0:T(8,128)(2,1)}, bf16[2,144,512]{2,1,0:T(8,128)(2,1)S(1)}, u32[]{:S(2)}, u32[]{:S(2)}) collective-permute-start(bf16[2,144,512]{2,1,0:T(8,128)(2,1)} %collective-permute-done.4.refs_3_), channel_id=1, source_target_pairs={{0,4},{4,0},{8,12},{12,8},{16,20},{20,16},{24,28},{28,24},{32,36},... | collective-permute-start | bytes 884744 | tf_op jit(solution)/shard_map/ppermute | solution.py:388
  48.2 12.8 %collective-permute-start.14 = (bf16[2,144,512]{2,1,0:T(8,128)(2,1)}, bf16[2,144,512]{2,1,0:T(8,128)(2,1)}, u32[]{:S(2)}, u32[]{:S(2)}) collective-permute-start(bf16[2,144,512]{2,1,0:T(8,128)(2,1)} %collective-permute-done.2.refs_4_), channel_id=1, source_target_pairs={{0,4},{4,0},{8,12},{12,8},{16,20},{20,16},{24,28},{28,24},{32,36},... | collective-permute-start | bytes 884744 | tf_op jit(solution)/shard_map/ppermute | solution.py:388
  49.3 11.8 %collective-permute-start.13 = (bf16[2,144,512]{2,1,0:T(8,128)(2,1)}, bf16[2,144,512]{2,1,0:T(8,128)(2,1)}, u32[]{:S(2)}, u32[]{:S(2)}) collective-permute-start(bf16[2,144,512]{2,1,0:T(8,128)(2,1)} %collective-permute-done.8.refs_5_), channel_id=1, source_target_pairs={{0,4},{4,0},{8,12},{12,8},{16,20},{20,16},{24,28},{28,24},{32,36},... | collective-permute-start | bytes 884744 | tf_op jit(solution)/shard_map/ppermute | solution.py:388
  50.2 16.9 %collective-permute-start.11 = (bf16[2,144,512]{2,1,0:T(8,128)(2,1)}, bf16[2,144,512]{2,1,0:T(8,128)(2,1)}, u32[]{:S(2)}, u32[]{:S(2)}) collective-permute-start(bf16[2,144,512]{2,1,0:T(8,128)(2,1)} %collective-permute-done.8.refs_5_), channel_id=1, source_target_pairs={{0,32},{4,228},{8,40},{12,236},{16,48},{20,244},{24,56},{28,252},{... | collective-permute-start | bytes 884744 | tf_op jit(solution)/shard_map/ppermute | solution.py:376
  51.0 10.0 %copy-start.1 = (bf16[32,128,128]{2,1,0:T(8,128)(2,1)}, bf16[32,128,128]{2,1,0:T(8,128)(2,1)S(1)}, u32[]{:S(2)}) copy-start(bf16[32,128,128]{2,1,0:T(8,128)(2,1)S(1)} %collective-permute-done.10.k_swap) | copy-start | bytes 3145732
  51.0 16.6 %collective-permute-start.12 = (bf16[2,144,512]{2,1,0:T(8,128)(2,1)}, bf16[2,144,512]{2,1,0:T(8,128)(2,1)}, u32[]{:S(2)}, u32[]{:S(2)}) collective-permute-start(bf16[2,144,512]{2,1,0:T(8,128)(2,1)} %collective-permute-done.7.refs_0_), channel_id=1, source_target_pairs={{0,32},{4,228},{8,40},{12,236},{16,48},{20,244},{24,56},{28,252},{... | collective-permute-start | bytes 884744 | tf_op jit(solution)/shard_map/ppermute | solution.py:376
  54.8 14.7 %copy-start.20 = (s32[4]{0:T(128)}, s32[4]{0:T(128)S(1)}, u32[]{:S(2)}) copy-start(s32[4]{0:T(128)S(1)} %pad_add_fusion.place.refs_6_) | copy-start | bytes 52
  61.1 6.7 %collective-permute-start.20 = (bf16[2,144,512]{2,1,0:T(8,128)(2,1)}, bf16[2,144,512]{2,1,0:T(8,128)(2,1)S(1)}, u32[]{:S(2)}, u32[]{:S(2)}) collective-permute-start(bf16[2,144,512]{2,1,0:T(8,128)(2,1)} %collective-permute-done.7.refs_0_), channel_id=1, source_target_pairs={{0,4},{4,0},{8,12},{12,8},{16,20},{20,16},{24,28},{28,24},{32,36},... | collective-permute-start | bytes 884744 | tf_op jit(solution)/shard_map/ppermute | solution.py:388
  67.1 2.0 %collective-permute-start.19 = (bf16[2,144,512]{2,1,0:T(8,128)(2,1)}, bf16[2,144,512]{2,1,0:T(8,128)(2,1)S(1)}, u32[]{:S(2)}, u32[]{:S(2)}) collective-permute-start(bf16[2,144,512]{2,1,0:T(8,128)(2,1)} %collective-permute-done.11.refs_1_), channel_id=1, source_target_pairs={{0,4},{4,0},{8,12},{12,8},{16,20},{20,16},{24,28},{28,24},{32,36},... | collective-permute-start | bytes 884744 | tf_op jit(solution)/shard_map/ppermute | solution.py:388
  67.6 1.8 %collective-permute-start.18 = (bf16[2,144,512]{2,1,0:T(8,128)(2,1)}, bf16[2,144,512]{2,1,0:T(8,128)(2,1)S(1)}, u32[]{:S(2)}, u32[]{:S(2)}) collective-permute-start(bf16[2,144,512]{2,1,0:T(8,128)(2,1)} %collective-permute-done.12.refs_2_), channel_id=1, source_target_pairs={{0,4},{4,0},{8,12},{12,8},{16,20},{20,16},{24,28},{28,24},{32,36},... | collective-permute-start | bytes 884744 | tf_op jit(solution)/shard_map/ppermute | solution.py:388
  77.7 19.1 %collective-permute-start.22 = (bf16[64,2176]{1,0:T(8,128)(2,1)S(1)}, bf16[64,2176]{1,0:T(8,128)(2,1)S(1)}, u32[]{:S(2)}, u32[]{:S(2)}) collective-permute-start(bf16[64,2176]{1,0:T(8,128)(2,1)S(1)} %get-tuple-element.45), channel_id=1, source_target_pairs={{0,24},{4,12},{8,0},{12,20},{16,8},{20,28},{24,16},{28,4},{32,56},... | collective-permute-start | bytes 835592 | tf_op jit(solution)/shard_map/ppermute | solution.py:380
  79.0 17.8 %collective-permute-start.23 = (bf16[64,2176]{1,0:T(8,128)(2,1)S(1)}, bf16[64,2176]{1,0:T(8,128)(2,1)S(1)}, u32[]{:S(2)}, u32[]{:S(2)}) collective-permute-start(bf16[64,2176]{1,0:T(8,128)(2,1)S(1)} %get-tuple-element.46), channel_id=1, source_target_pairs={{0,16},{4,20},{8,24},{12,28},{16,0},{20,4},{24,8},{28,12},{32,48},... | collective-permute-start | bytes 835592 | tf_op jit(solution)/shard_map/ppermute | solution.py:380
  81.5 15.4 %collective-permute-start.24 = (bf16[64,2176]{1,0:T(8,128)(2,1)S(1)}, bf16[64,2176]{1,0:T(8,128)(2,1)S(1)}, u32[]{:S(2)}, u32[]{:S(2)}) collective-permute-start(bf16[64,2176]{1,0:T(8,128)(2,1)S(1)} %get-tuple-element.47), channel_id=1, source_target_pairs={{0,8},{4,28},{8,16},{12,4},{16,24},{20,12},{24,0},{28,20},{32,40},... | collective-permute-start | bytes 835592 | tf_op jit(solution)/shard_map/ppermute | solution.py:380
  (17 other events, 56.6 us)

commit v3 on v2

--- a/solution.py
+++ b/solution.py
@@ -123,16 +123,12 @@
     return load_all(pairs, sems)
 
 
-def query_kernel(
-    place, p0_in, p1_in, p2_in, p3_in, both, k_swap, q_lat, q_rot, page_bit, slot_of,
-    p0, p1, p2, p3, whole, turned, p_sems, sems,
+def gather_kernel(
+    place, p0, p1, p2, p3, q_nope, q_rot, page_bit, pick_out, partner_out, chosen_out, flags, turned
 ):
-    p_copies = load_all(list(zip((p0_in, p1_in, p2_in, p3_in), (p0, p1, p2, p3))), p_sems)
-    copies = gather_weights(place, both, k_swap, 0, whole, sems)
-    for copy in p_copies:
-        copy.wait()
     z, x, core = place[0], place[1], place[2]
     pays = (p0, p1, p2, p3)
+    missing = []
     lane = iota((ROWS, 128), 1)
     wide = iota((ROWS, SLOTS), 1)
     picks, bits, places = ([], []), ([], []), []
@@ -141,7 +137,7 @@
         columns = [
             jnp.sum(jnp.where(lane == at, code, 0.0), axis=1, keepdims=True).astype(I32) for at in range(4)
         ]
-        noted = jnp.zeros((ROWS, 128), F32)
+        found = []
         for k in range(2):
             slot, rank = columns[k], columns[2 + k]
             away = (z - lax.shift_right_logical(slot, 4)) * (1 - 2 * core)
@@ -152,22 +148,39 @@
             at = jnp.where(here, (order * 2 + other) * 16 + peer * 4 + rank, -1)
             picks[k].append((wide == at).astype(F32))
             bits[k].append(lax.bitwise_and(slot, 1).astype(F32) * jnp.ones((1, 128), F32))
-            noted = jnp.where(lane == k, at.astype(F32), noted)
-        slot_of[peer * ROWS : (peer + 1) * ROWS, :] = noted
+            found.append(jnp.where(here, 1.0, 0.0))
+        missing.append(jnp.concatenate(found, axis=1))
     pick = [jnp.concatenate(p, axis=0) for p in picks]
     bit = [jnp.concatenate(b, axis=0) for b in bits]
     page_bit[...] = dot(pick[0], bit[0], FIRST) + dot(pick[1], bit[1], FIRST)
     turned[...] = jnp.transpose(pick[0] + pick[1]).astype(BF16)
-    for copy in copies:
-        copy.wait()
+    pick_out[...] = (pick[0] + pick[1]).astype(BF16)
+    pair = dot(pick[0], pick[1], FIRST) + dot(pick[1], pick[0], FIRST)
+    partner_out[...] = pair.astype(BF16)
+    found = jnp.concatenate(missing, axis=0)
+    chosen_out[...] = (pick[0] + pick[1] * (1.0 - found[:, 0:1])).astype(BF16)
+    flags[:, :128] = jnp.sum(pair, axis=1, keepdims=True) * jnp.ones((1, 128), F32)
+    flags[:, 128:] = jnp.maximum(found[:, 0:1], found[:, 1:2]) * jnp.ones((1, 128), F32)
 
     def two_heads(i, carry):
         rot = pl.ds(pl.multiple_of(QN + i * 128, 128), 128)
         gathered = dot(turned[...], jnp.concatenate([p[:, rot] for p in pays], axis=0)).astype(BF16)
         at = pl.ds(pl.multiple_of(i * 2 * NOPE, 128), 2 * NOPE)
-        left = dot(turned[...], jnp.concatenate([p[:, at] for p in pays], axis=0)).astype(BF16)
+        q_nope[:, at] = dot(turned[...], jnp.concatenate([p[:, at] for p in pays], axis=0)).astype(BF16)
         for k in range(2):
             q_rot[2 * i + k] = gathered[:, k * ROPE : (k + 1) * ROPE]
+        return carry
+
+    lax.fori_loop(0, HEADS // 2, two_heads, 0)
+
+
+def query_kernel(place, q_nope, both, k_swap, q_lat, whole, sems):
+    for copy in gather_weights(place, both, k_swap, 0, whole, sems):
+        copy.wait()
+
+    def two_heads(i, carry):
+        left = q_nope[:, pl.ds(pl.multiple_of(i * 2 * NOPE, 128), 2 * NOPE)]
+        for k in range(2):
             q_lat[2 * i + k] = dot(left[:, k * NOPE : (k + 1) * NOPE], whole[2 * i + k]).astype(BF16)
         return carry
 
@@ -245,20 +258,19 @@
 def late_kernel(*refs):
     units = refs[:LATE]
     (
-        place, q_lat, q_rot, page_bit, slot_of, early, early_logs, weights, v_swap,
+        place, q_lat, q_rot, page_bit, pick, partner, chosen, flags, early, early_logs, weights, v_swap,
         r0, r1, r2, r3, held, result, logs, whole, parts, sems, w_sems,
     ) = refs[LATE:]
     start_units(units, held, sems)
     copies = gather_weights(place, weights, v_swap, 1, whole, w_sems)
     attend_units(LATE, EARLY, units[0], q_lat, q_rot, page_bit, held, sems, result, logs)
-    highest = lax.Precision.HIGHEST
-    wide = iota((SLOTS, SLOTS), 1).astype(F32)
-    at0, at1 = slot_of[:, 0:1], slot_of[:, 1:2]
-    pick0, pick1 = (wide == at0).astype(F32), (wide == at1).astype(F32)
-    partner = dot(pick0, pick1, FIRST) + dot(pick1, pick0, FIRST)
-    has = jnp.sum(partner, axis=1, keepdims=True)
     log = jnp.concatenate([early_logs[...], logs[...]], axis=0)
-    other = dot(partner, log, precision=highest) + (has - 1.0) * (-LOW)
+    other = (flags[:, :128] - 1.0) * (-LOW)
+    rest = log
+    for _ in range(3):
+        part = rest.astype(BF16)
+        rest = rest - part.astype(F32)
+        other = other + dot(partner[...], part)
     top = jnp.maximum(log, other)
     mine = jnp.exp(log - top)
     both = mine + jnp.exp(other - top)
@@ -270,15 +282,13 @@
         mixed = jnp.concatenate([early[head], result[head]], axis=0)
         part = dot(mixed, whole[head], LAST) * weight[:, head : head + 1]
         parts[:, head * VDIM : (head + 1) * VDIM] = part.astype(BF16)
-    first = jnp.where(at0 >= 0.0, 1.0, 0.0)
-    row_log = dot(pick0 + pick1 * (1.0 - first), merged, precision=highest)
-    none = (at0 < 0.0) & (at1 < 0.0)
-    row_log = jnp.where(none, LOW, row_log)
-    packed = pack_log(row_log)
-    pick = (pick0 + pick1).astype(BF16)
+    lane = iota((SLOTS, 128), 1)
+    empty = jnp.where(lane < 16, LOW, 0.0)
+    packed = dot(chosen[...], pack_log(merged))
+    packed = jnp.where(flags[:, 128:] > 0.5, packed, empty).astype(BF16)
     for peer, out in enumerate((r0, r1, r2, r3)):
         rows = slice(peer * ROWS, (peer + 1) * ROWS)
-        out[:, :OUT] = dot(pick[rows], parts[...]).astype(BF16)
+        out[:, :OUT] = dot(pick[rows, :], parts[...]).astype(BF16)
         out[:, OUT:] = packed[rows]
 
 
@@ -440,28 +450,36 @@
     pays = [pay, a_pay[1], a_pay[2], swap(b_pay[1])]
     a.append(ring_z(after(a[2], b[1], b_pay[1])))
     b.append(ring_z(b[2]))
+    square = (SLOTS, SLOTS)
+    q_slots, q_rot, page_bit, *ties = pl.pallas_call(
+        gather_kernel,
+        out_shape=(
+            struct(SLOTS, QN), struct(HEADS, SLOTS, ROPE), struct(SLOTS, 128, dtype=F32),
+            struct(*square), struct(*square), struct(*square), struct(*square, dtype=F32),
+        ),
+        in_specs=[SMEM] + [VMEM] * 4,
+        out_specs=(VMEM,) * 7,
+        scratch_shapes=[pltpu.VMEM(square, BF16)],
+        compiler_params=params(60),
+        cost_estimate=cost(3),
+        name="gather",
+    )(place, *pays)
+
     split = both.reshape(NY, HEADS, NOPE, 128)
     k_part, v_part = split[:, : HEADS // 2], split[:, HEADS // 2 :]
-    k_swap = swap(after(k_part.reshape(NY * HEADS // 2, NOPE, 128), a[3], b[2], a_pay[2]))
+    k_swap = swap(after(k_part.reshape(NY * HEADS // 2, NOPE, 128), a[3], b[2], q_slots))
     v_swap = swap(v_part.reshape(NY * HEADS // 2, NOPE, 128))
 
-    q_lat, q_rot, page_bit, slot_of = pl.pallas_call(
+    q_lat = pl.pallas_call(
         query_kernel,
-        out_shape=(
-            struct(HEADS, SLOTS, KVL), struct(HEADS, SLOTS, ROPE),
-            struct(SLOTS, 128, dtype=F32), struct(4 * ROWS, 128, dtype=F32),
-        ),
-        in_specs=[SMEM] + [ANY] * 6,
-        out_specs=(VMEM,) * 4,
-        scratch_shapes=[
-            *[pltpu.VMEM((ROWS, PAY), BF16)] * 4,
-            pltpu.VMEM((HEADS, NOPE, KVL), BF16), pltpu.VMEM((SLOTS, 4 * ROWS), BF16),
-            pltpu.SemaphoreType.DMA((4,)), pltpu.SemaphoreType.DMA((8,)),
-        ],
-        compiler_params=params(32),
-        cost_estimate=cost(4),
+        out_shape=struct(HEADS, SLOTS, KVL),
+        in_specs=[SMEM, VMEM] + [ANY] * 2,
+        out_specs=VMEM,
+        scratch_shapes=[pltpu.VMEM((HEADS, NOPE, KVL), BF16), pltpu.SemaphoreType.DMA((8,))],
+        compiler_params=params(20),
+        cost_estimate=cost(3),
         name="queries",
-    )(place, *pays, both, k_swap)
+    )(place, q_slots, both, k_swap)
 
     a.append(ring_z(after(a[3], b[2], a_pay[2])))
     a_swap = [None] + [swap(u) for u in a[1:4]]
@@ -474,7 +492,7 @@
         in_specs=[ANY] * EARLY + [VMEM] * 3,
         out_specs=(VMEM, VMEM),
         scratch_shapes=[pltpu.VMEM((EARLY, 2, UNIT, KVL), BF16), pltpu.SemaphoreType.DMA((EARLY,))],
-        compiler_params=params(32),
+        compiler_params=params(20),
         cost_estimate=cost(1),
         name="early_pages",
     )(*early_units, q_lat, q_rot, page_bit)
@@ -485,17 +503,17 @@
     returns = pl.pallas_call(
         late_kernel,
         out_shape=(struct(ROWS, RET),) * 4,
-        in_specs=[ANY] * LATE + [SMEM] + [VMEM] * 6 + [ANY] * 2,
+        in_specs=[ANY] * LATE + [SMEM] + [VMEM] * 9 + [ANY] * 2,
         out_specs=(VMEM,) * 4,
         scratch_shapes=[
             pltpu.VMEM((LATE, 2, UNIT, KVL), BF16), pltpu.VMEM((HEADS, LATE * 16, KVL), BF16),
             pltpu.VMEM((LATE * 16, 128), F32), pltpu.VMEM((HEADS, VDIM, KVL), BF16), pltpu.VMEM((SLOTS, OUT), BF16),
             pltpu.SemaphoreType.DMA((LATE,)), pltpu.SemaphoreType.DMA((8,)),
         ],
-        compiler_params=params(32),
+        compiler_params=params(20),
         cost_estimate=cost(7),
         name="late_pages",
-    )(*late_units, place, q_lat, q_rot, page_bit, slot_of, early, early_logs, both, v_swap)
+    )(*late_units, place, q_lat, q_rot, page_bit, *ties, early, early_logs, both, v_swap)
 
     backs = [returns[0], back_x(returns[1]), back_x(returns[2], 2), ring_x(returns[3])]
     k_swap, returns = lax.optimization_barrier((k_swap, returns))
@@ -513,7 +531,7 @@
             pltpu.SemaphoreType.DMA((8,)), pltpu.SemaphoreType.DMA((8,)),
             pltpu.SemaphoreType.DMA((3,)), pltpu.SemaphoreType.DMA((8,)),
         ],
-        compiler_params=params(60),
+        compiler_params=params(34),
         cost_estimate=cost(8),
         name="suffix",
     )(place, suffix_len.reshape(1, -1), q_nope, q_rope, suffix_latent, suffix_rope, both, k_swap, v_swap)

time: 99.9 us -> 92.1 us (0.922)
  local copies, waits for them, and re-layouts: 10.6 us -> 2.09 us
  starting transfers between devices: 38.1 us -> 35.7 us
  waiting for transfers between devices: 10.1 us -> 12.1 us
    unnamed x46 -> x28, local copies, waits for them, and re-layouts: 7.69 us -> 0.07 us
    pallas_call x1 -> x2, Pallas kernels: 6.17 us -> 9.33 us  [the longest x1 6.07 us: shards(): pl.pallas_call(gather_kernel, out_shape=(struct(SLOTS, QN), struct(HEADS,...]
    pallas_call x1, Pallas kernels: 14.2 us -> 11.3 us  [shards(): pl.pallas_call(suffix_kernel, out_shape=struct(ROWS, RET), in_specs=[SMEM...]
    ppermute x12, starting transfers between devices: 7.87 us -> 5.57 us  [swap(): lax.ppermute(a, 'rows', [(row_of(z, x, c), row_of(z, x, 1 - c)) for z, x,...]
    ppermute x7, waiting for transfers between devices: 4.1 us -> 6.26 us  [ring_z(): lax.ppermute(a, 'rows', [(row_of(z, x, c), row_of(z + 1 - 2 * c, x, c)) f...]
  transfers between devices with their start and end apart: 26 -> 26, of which waited for: 6 -> 7; matrix products, arithmetic and copies ran while one was open for 1% -> 1% of each run, Pallas kernels for 29% -> 32%
where the time goes in v3:
time: 92.1 us; the launch traced here: 91 us
  Pallas kernels  38.6 us (42%)
  starting transfers between devices  35.7 us (39%)
  waiting for transfers between devices  12.1 us (13%)
  other arithmetic  2.2 us (2%)
  local copies, waits for them, and re-layouts  2.09 us (2%)
    ppermute x7, starting transfers between devices, ring_z(): lax.ppermute(a, 'rows', [(row_of(z, x, c), row_of(z + 1 - 2 * c, x, c)) f...  17.7 us
    pallas_call x1, Pallas kernels, shards(): pl.pallas_call(suffix_kernel, out_shape=struct(ROWS, RET), in_specs=[SMEM...  11.3 us
    pallas_call x1, Pallas kernels, shards(): pl.pallas_call(late_kernel, out_shape=(struct(ROWS, RET),) * 4, in_specs=...  7.52 us
    ppermute x6, starting transfers between devices, ring_x(): lax.ppermute(a, 'rows', [(row_of(z, x, c), row_of(z, x + steps * (1 - 2 *...  7.38 us
    ppermute x7, waiting for transfers between devices, ring_z(): lax.ppermute(a, 'rows', [(row_of(z, x, c), row_of(z + 1 - 2 * c, x, c)) f...  6.26 us
    pallas_call x1, Pallas kernels, shards(): pl.pallas_call(gather_kernel, out_shape=(struct(SLOTS, QN), struct(HEADS,...  6.07 us
    pallas_call x1, Pallas kernels, shards(): pl.pallas_call(early_kernel, out_shape=(struct(HEADS, EARLY * 16, KVL), s...  6.07 us
    ppermute x12, starting transfers between devices, swap(): lax.ppermute(a, 'rows', [(row_of(z, x, c), row_of(z, x, 1 - c)) for z, x,...  5.57 us
  transfers between devices with their start and end apart: 26, of which 7 were waited for; matrix products, arithmetic and copies ran while one was open for 1% of the time, Pallas kernels for 32%

profile of v3, /device:TPU:1, one launch (start us, length us, event | category | flops | bytes accessed | tf_op | source)
XLA Modules:
  0.0 91.0 jit_solution(1878414065475054149)
XLA Ops:
  0.0 1.8 %constant_dynamic-slice_fusion = (bf16[4,8,128,128]{3,2,1,0:T(8,128)(2,1)S(1)}, bf16[4,8,128,128]{3,2,1,0:T(8,128)(2,1)S(1)}) fusion(bf16[4,16,128,128]{3,2,1,0:T(8,128)(2,1)} %bitcast.18, s32[]{:T(128)S(6)} %select_n.30, bf16[4,16,128,128]{3,2,1,0:T(8,128)(2,1)} %bitcast.19), kind=kLoop, calls=%fused_computation.2 | loop fusion | bytes 4194308 | tf_op jit(solution)/shard_map/dynamic_slice | solution.py:423
  1.8 1.5 %pad_maximum_fusion = bf16[4,16,128,128]{3,2,1,0:T(8,128)(2,1)} fusion(bf16[4,8,128,128]{3,2,1,0:T(8,128)(2,1)S(1)} %get-tuple-element.57, bf16[4,8,128,128]{3,2,1,0:T(8,128)(2,1)S(1)} %get-tuple-element.58), kind=kLoop, calls=%fused_computation | loop fusion | flops 1048576 | bytes 4194304 | tf_op jit(solution)/shard_map/concatenate | solution.py:427
  3.3 5.0 %all-to-all-start = ((bf16[64,128,128]{2,1,0:T(8,128)(2,1)}), bf16[64,128,128]{2,1,0:T(8,128)(2,1)S(1)}, u32[]{:S(2)}, u32[]{:S(2)}) async-start(bf16[64,128,128]{2,1,0:T(8,128)(2,1)} %bitcast.15), calls=%async_computation | async-start | bytes 4194304 | tf_op jit(solution)/shard_map/all_to_all | solution.py:416
  8.3 2.8 %pack.1 = (bf16[2,144,512]{2,1,0:T(8,128)(2,1)}, bf16[64,3200]{1,0:T(8,128)(2,1)}) custom-call(s32[2,64]{1,0:T(2,128)} %bitcast.20, s32[1,128]{1,0:T(1,128)} %bitcast.21, bf16[2,8192]{1,0:T(2,128)(2,1)} %rope_in.2, bf16[2,128,512]{2,1,0:T(8,128)(2,1)} %latent_in.2, bf16[64,2048]{1,0:T(8,128)(2,1)} %q_nope_in.1, bf16[64,1024]{1,0:T(8,128)(2,1)} %q_rope_in.1), custom_call_target="tpu_custom_call" | custom-call | flops 2000000 | bytes 6000000 | tf_op jit(solution)/shard_map/pack/pallas_call | solution.py:430
  11.1 1.9 %collective-permute-start.5 = (bf16[64,3200]{1,0:T(8,128)(2,1)}, bf16[64,3200]{1,0:T(8,128)(2,1)S(1)}, u32[]{:S(2)}, u32[]{:S(2)}) collective-permute-start(bf16[64,3200]{1,0:T(8,128)(2,1)} %get-tuple-element.32.p0), channel_id=1, source_target_pairs={{0,4},{4,0},{8,12},{12,8},{16,20},{20,16},{24,28},{28,24},{32,36},... | collective-permute-start | bytes 1228808 | tf_op jit(solution)/shard_map/ppermute | solution.py:398
  13.0 1.6 %collective-permute-start.1 = (bf16[64,3200]{1,0:T(8,128)(2,1)}, bf16[64,3200]{1,0:T(8,128)(2,1)}, u32[]{:S(2)}, u32[]{:S(2)}) collective-permute-start(bf16[64,3200]{1,0:T(8,128)(2,1)} %get-tuple-element.32.p0), channel_id=1, source_target_pairs={{0,8},{4,28},{8,16},{12,4},{16,24},{20,12},{24,0},{28,20},{32,40},... | collective-permute-start | bytes 1228808 | tf_op jit(solution)/shard_map/ppermute | solution.py:390
  14.6 1.6 %collective-permute-start.6 = (bf16[64,3200]{1,0:T(8,128)(2,1)S(1)}, bf16[64,3200]{1,0:T(8,128)(2,1)}, u32[]{:S(2)}, u32[]{:S(2)}) collective-permute-start(bf16[64,3200]{1,0:T(8,128)(2,1)S(1)} %collective-permute-done.5), channel_id=1, source_target_pairs={{0,8},{4,28},{8,16},{12,4},{16,24},{20,12},{24,0},{28,20},{32,40},... | collective-permute-start | bytes 1228808 | tf_op jit(solution)/shard_map/ppermute | solution.py:390
  16.2 5.6 %collective-permute-start = (bf16[2,144,512]{2,1,0:T(8,128)(2,1)}, bf16[2,144,512]{2,1,0:T(8,128)(2,1)S(1)}, u32[]{:S(2)}, u32[]{:S(2)}) collective-permute-start(bf16[2,144,512]{2,1,0:T(8,128)(2,1)} %get-tuple-element.31.refs_0_), channel_id=1, source_target_pairs={{0,32},{4,228},{8,40},{12,236},{16,48},{20,244},{24,56},{28,252},{... | collective-permute-start | bytes 884744 | tf_op jit(solution)/shard_map/ppermute | solution.py:386
  21.8 4.0 %collective-permute-done.refs_2_ = bf16[2,144,512]{2,1,0:T(8,128)(2,1)S(1)} collective-permute-done((bf16[2,144,512]{2,1,0:T(8,128)(2,1)}, bf16[2,144,512]{2,1,0:T(8,128)(2,1)S(1)}, u32[]{:S(2)}, u32[]{:S(2)}) %collective-permute-start) | collective-permute-done | bytes 294944 | tf_op jit(solution)/shard_map/ppermute | solution.py:386
  25.8 0.5 collective-permute-start.9
  26.3 1.5 %collective-permute-start.10 = (bf16[64,3200]{1,0:T(8,128)(2,1)}, bf16[64,3200]{1,0:T(8,128)(2,1)}, u32[]{:S(2)}, u32[]{:S(2)}) collective-permute-start(bf16[64,3200]{1,0:T(8,128)(2,1)} %collective-permute-done.6), channel_id=1, source_target_pairs={{0,4},{4,0},{8,12},{12,8},{16,20},{20,16},{24,28},{28,24},{32,36},... | collective-permute-start | bytes 1228808 | tf_op jit(solution)/shard_map/ppermute | solution.py:398
  27.9 3.8 %collective-permute-start.4 = (bf16[2,144,512]{2,1,0:T(8,128)(2,1)S(1)}, bf16[2,144,512]{2,1,0:T(8,128)(2,1)S(1)}, u32[]{:S(2)}, u32[]{:S(2)}) collective-permute-start(bf16[2,144,512]{2,1,0:T(8,128)(2,1)S(1)} %collective-permute-done.3.refs_1_), channel_id=1, source_target_pairs={{0,32},{4,228},{8,40},{12,236},{16,48},{20,244},{24,56},{28,252},{... | collective-permute-start | bytes 884744 | tf_op jit(solution)/shard_map/ppermute | solution.py:386
  31.7 0.7 collective-permute-start.2
  32.4 0.7 pad_add_fusion.place.refs_6_
  33.1 2.3 %collective-permute-done.4.refs_3_ = bf16[2,144,512]{2,1,0:T(8,128)(2,1)S(1)} collective-permute-done((bf16[2,144,512]{2,1,0:T(8,128)(2,1)S(1)}, bf16[2,144,512]{2,1,0:T(8,128)(2,1)S(1)}, u32[]{:S(2)}, u32[]{:S(2)}) %collective-permute-start.4) | collective-permute-done | bytes 294944 | tf_op jit(solution)/shard_map/ppermute | solution.py:386
  35.4 3.4 %collective-permute-start.8 = (bf16[2,144,512]{2,1,0:T(8,128)(2,1)S(1)}, bf16[2,144,512]{2,1,0:T(8,128)(2,1)}, u32[]{:S(2)}, u32[]{:S(2)}) collective-permute-start(bf16[2,144,512]{2,1,0:T(8,128)(2,1)S(1)} %collective-permute-done.4.refs_3_), channel_id=1, source_target_pairs={{0,32},{4,228},{8,40},{12,236},{16,48},{20,244},{24,56},{28,252},{... | collective-permute-start | bytes 884744 | tf_op jit(solution)/shard_map/ppermute | solution.py:386
  38.8 2.9 %collective-permute-start.7 = (bf16[2,144,512]{2,1,0:T(8,128)(2,1)S(1)}, bf16[2,144,512]{2,1,0:T(8,128)(2,1)}, u32[]{:S(2)}, u32[]{:S(2)}) collective-permute-start(bf16[2,144,512]{2,1,0:T(8,128)(2,1)S(1)} %collective-permute-done.2.refs_4_), channel_id=1, source_target_pairs={{0,32},{4,228},{8,40},{12,236},{16,48},{20,244},{24,56},{28,252},{... | collective-permute-start | bytes 884744 | tf_op jit(solution)/shard_map/ppermute | solution.py:386
  41.6 6.1 %gather.1 = (bf16[256,2048]{1,0:T(8,128)(2,1)}, bf16[16,256,64]{2,1,0:T(8,128)(2,1)}, f32[256,128]{1,0:T(8,128)}, bf16[256,256]{1,0:T(8,128)(2,1)}, bf16[256,256...) custom-call(s32[4]{0:T(128)} %pad_add_fusion.place.refs_6_, bf16[64,3200]{1,0:T(8,128)(2,1)} %get-tuple-element.32.p0, ...), custom_call_target="tpu_custom_call" | custom-call | flops 3000000 | bytes 9000000 | tf_op jit(solution)/shard_map/gather/pallas_call | solution.py:454
  48.1 0.5 collective-permute-start.21
  49.2 3.4 %collective-permute-done.17.refs_9_ = bf16[2,144,512]{2,1,0:T(8,128)(2,1)S(1)} collective-permute-done((bf16[2,144,512]{2,1,0:T(8,128)(2,1)S(1)}, bf16[2,144,512]{2,1,0:T(8,128)(2,1)S(1)}, u32[]{:S(2)}, u32[]{:S(2)}) %collective-permute-start.17) | collective-permute-done | bytes 294944 | tf_op jit(solution)/shard_map/ppermute | solution.py:398
  53.1 0.8 collective-permute-start.12
  53.9 0.5 collective-permute-start.13
  54.4 3.3 %queries.1.refs_10_.refs_7_ = bf16[16,256,512]{2,1,0:T(8,128)(2,1)S(1)} custom-call(s32[4]{0:T(128)S(1)} %copy-done.12, bf16[256,2048]{1,0:T(8,128)(2,1)S(1)} %copy-done.2, bf16[64,128,128]{2,1,0:T(8,128)(2,1)S(1)} %all-to-all-done.both.refs_16_, bf16[32,128,128]{2,1,0:T(8,128)(2,1)S(1)} %collective-permute-done.11.k_swap), custom_call_target="tpu_custom_call" | custom-call | flops 3000000 | bytes 9000000 | tf_op jit(solution)/shard_map/queries/pallas_call | solution.py:473
  57.9 6.1 %early_pages.1 = (bf16[16,160,512]{2,1,0:T(8,128)(2,1)S(1)}, f32[160,128]{1,0:T(8,128)S(1)}) custom-call(bf16[2,144,512]{2,1,0:T(8,128)(2,1)S(1)} %copy-done.7, bf16[2,144,512]{2,1,0:T(8,128)(2,1)S(1)} %collective-permute-done.3.refs_1_, bf16[2,144,512]{2,1,0:T(8,128)(2,1)S(1)} %collective-permute-done.refs_2_, ...), custom_call_target="tpu_custom_call" | custom-call | flops 1000000 | bytes 3000000 | tf_op jit(solution)/shard_map/early_pages/pallas_call | solution.py:489
  64.0 0.6 collective-permute-start.19
  64.6 1.1 %collective-permute-done.19.refs_4_ = bf16[2,144,512]{2,1,0:T(8,128)(2,1)S(1)} collective-permute-done((bf16[2,144,512]{2,1,0:T(8,128)(2,1)S(1)}, bf16[2,144,512]{2,1,0:T(8,128)(2,1)S(1)}, u32[]{:S(2)}, u32[]{:S(2)}) %collective-permute-start.19) | collective-permute-done | bytes 294944 | tf_op jit(solution)/shard_map/ppermute | solution.py:398
  66.2 7.5 %late_pages.1 = (bf16[64,2176]{1,0:T(8,128)(2,1)S(1)}, bf16[64,2176]{1,0:T(8,128)(2,1)S(1)}, bf16[64,2176]{1,0:T(8,128)(2,1)S(1)}, bf16[64,2176]{1,0:T(8,128)(2,1)S(1)}) custom-call(bf16[2,144,512]{2,1,0:T(8,128)(2,1)} %collective-permute-done.7.refs_0_, bf16[2,144,512]{2,1,0:T(8,128)(2,1)S(1)} %collective-permute-done.12.refs_1_, ...), custom_call_target="tpu_custom_call" | custom-call | flops 7000000 | bytes 21000000 | tf_op jit(solution)/shard_map/late_pages/pallas_call | solution.py:503
  73.8 2.9 %collective-permute-start.23 = (bf16[64,2176]{1,0:T(8,128)(2,1)S(1)}, bf16[64,2176]{1,0:T(8,128)(2,1)S(1)}, u32[]{:S(2)}, u32[]{:S(2)}) collective-permute-start(bf16[64,2176]{1,0:T(8,128)(2,1)S(1)} %get-tuple-element.52), channel_id=1, source_target_pairs={{0,16},{4,20},{8,24},{12,28},{16,0},{20,4},{24,8},{28,12},{32,48},... | collective-permute-start | bytes 835592 | tf_op jit(solution)/shard_map/ppermute | solution.py:390
  76.8 0.7 collective-permute-start.24
  77.4 11.3 %suffix.1.own = bf16[64,2176]{1,0:T(8,128)(2,1)S(1)} custom-call(s32[4]{0:T(128)S(1)} %copy-done.12, s32[1,64]{1,0:T(1,128)S(1)} %bitcast.14, bf16[64,2048]{1,0:T(8,128)(2,1)S(1)} %copy-done.3, bf16[64,1024]{1,0:T(8,128)(2,1)S(1)} %copy-done.5, bf16[64,64,512]{2,1,0:T(8,128)(2,1)S(1)} %copy-done, bf16[64,4096]{1,0:T(8,128)(2,1)S(1)} %copy-done.6, ...), custom_call_target="tpu_custom_call" | custom-call | flops 8000000 | bytes 24000000 | tf_op jit(solution)/shard_map/suffix/pallas_call | solution.py:520
  88.8 0.5 collective-permute-done.24.r3
  89.3 1.7 %combine.1 = bf16[64,2048]{1,0:T(8,128)(2,1)} custom-call(bf16[64,2176]{1,0:T(8,128)(2,1)S(1)} %suffix.1.own, bf16[64,2176]{1,0:T(8,128)(2,1)S(1)} %get-tuple-element.50.r0, bf16[64,2176]{1,0:T(8,128)(2,1)S(1)} %collective-permute-done.22.r1, bf16[64,2176]{1,0:T(8,128)(2,1)S(1)} %collective-permute-done.23.r2, bf16[64,2176]{1,0:T(8,128)(2,1)S(1)} %collective-permute-done.24.r3), custom_call_target="tpu_custom_call" | custom-call | flops 2000000 | bytes 6000000 | tf_op jit(solution)/shard_map/combine/pallas_call | solution.py:539
  (59 shorter events, 2.2 us)
Async XLA Ops:
  3.3 44.4 %all-to-all-start = ((bf16[64,128,128]{2,1,0:T(8,128)(2,1)}), bf16[64,128,128]{2,1,0:T(8,128)(2,1)S(1)}, u32[]{:S(2)}, u32[]{:S(2)}) async-start(bf16[64,128,128]{2,1,0:T(8,128)(2,1)} %bitcast.15), calls=%async_computation | async-start | bytes 4194304 | tf_op jit(solution)/shard_map/all_to_all | solution.py:416
  11.1 3.5 %collective-permute-start.5 = (bf16[64,3200]{1,0:T(8,128)(2,1)}, bf16[64,3200]{1,0:T(8,128)(2,1)S(1)}, u32[]{:S(2)}, u32[]{:S(2)}) collective-permute-start(bf16[64,3200]{1,0:T(8,128)(2,1)} %get-tuple-element.32.p0), channel_id=1, source_target_pairs={{0,4},{4,0},{8,12},{12,8},{16,20},{20,16},{24,28},{28,24},{32,36},... | collective-permute-start | bytes 1228808 | tf_op jit(solution)/shard_map/ppermute | solution.py:398
  13.0 12.7 %collective-permute-start.1 = (bf16[64,3200]{1,0:T(8,128)(2,1)}, bf16[64,3200]{1,0:T(8,128)(2,1)}, u32[]{:S(2)}, u32[]{:S(2)}) collective-permute-start(bf16[64,3200]{1,0:T(8,128)(2,1)} %get-tuple-element.32.p0), channel_id=1, source_target_pairs={{0,8},{4,28},{8,16},{12,4},{16,24},{20,12},{24,0},{28,20},{32,40},... | collective-permute-start | bytes 1228808 | tf_op jit(solution)/shard_map/ppermute | solution.py:390
  14.6 11.7 %collective-permute-start.6 = (bf16[64,3200]{1,0:T(8,128)(2,1)S(1)}, bf16[64,3200]{1,0:T(8,128)(2,1)}, u32[]{:S(2)}, u32[]{:S(2)}) collective-permute-start(bf16[64,3200]{1,0:T(8,128)(2,1)S(1)} %collective-permute-done.5), channel_id=1, source_target_pairs={{0,8},{4,28},{8,16},{12,4},{16,24},{20,12},{24,0},{28,20},{32,40},... | collective-permute-start | bytes 1228808 | tf_op jit(solution)/shard_map/ppermute | solution.py:390
  16.2 9.6 %collective-permute-start = (bf16[2,144,512]{2,1,0:T(8,128)(2,1)}, bf16[2,144,512]{2,1,0:T(8,128)(2,1)S(1)}, u32[]{:S(2)}, u32[]{:S(2)}) collective-permute-start(bf16[2,144,512]{2,1,0:T(8,128)(2,1)} %get-tuple-element.31.refs_0_), channel_id=1, source_target_pairs={{0,32},{4,228},{8,40},{12,236},{16,48},{20,244},{24,56},{28,252},{... | collective-permute-start | bytes 884744 | tf_op jit(solution)/shard_map/ppermute | solution.py:386
  21.8 6.1 %collective-permute-start.3 = (bf16[2,144,512]{2,1,0:T(8,128)(2,1)}, bf16[2,144,512]{2,1,0:T(8,128)(2,1)S(1)}, u32[]{:S(2)}, u32[]{:S(2)}) collective-permute-start(bf16[2,144,512]{2,1,0:T(8,128)(2,1)} %get-tuple-element.31.refs_0_), channel_id=1, source_target_pairs={{0,4},{4,0},{8,12},{12,8},{16,20},{20,16},{24,28},{28,24},{32,36},... | collective-permute-start | bytes 884744 | tf_op jit(solution)/shard_map/ppermute | solution.py:398
  25.8 15.9 %collective-permute-start.9 = (bf16[64,3200]{1,0:T(8,128)(2,1)}, bf16[64,3200]{1,0:T(8,128)(2,1)}, u32[]{:S(2)}, u32[]{:S(2)}) collective-permute-start(bf16[64,3200]{1,0:T(8,128)(2,1)} %collective-permute-done.1.p1), channel_id=1, source_target_pairs={{0,8},{4,28},{8,16},{12,4},{16,24},{20,12},{24,0},{28,20},{32,40},... | collective-permute-start | bytes 1228808 | tf_op jit(solution)/shard_map/ppermute | solution.py:390
  26.3 15.3 %collective-permute-start.10 = (bf16[64,3200]{1,0:T(8,128)(2,1)}, bf16[64,3200]{1,0:T(8,128)(2,1)}, u32[]{:S(2)}, u32[]{:S(2)}) collective-permute-start(bf16[64,3200]{1,0:T(8,128)(2,1)} %collective-permute-done.6), channel_id=1, source_target_pairs={{0,4},{4,0},{8,12},{12,8},{16,20},{20,16},{24,28},{28,24},{32,36},... | collective-permute-start | bytes 1228808 | tf_op jit(solution)/shard_map/ppermute | solution.py:398
  27.9 7.5 %collective-permute-start.4 = (bf16[2,144,512]{2,1,0:T(8,128)(2,1)S(1)}, bf16[2,144,512]{2,1,0:T(8,128)(2,1)S(1)}, u32[]{:S(2)}, u32[]{:S(2)}) collective-permute-start(bf16[2,144,512]{2,1,0:T(8,128)(2,1)S(1)} %collective-permute-done.3.refs_1_), channel_id=1, source_target_pairs={{0,32},{4,228},{8,40},{12,236},{16,48},{20,244},{24,56},{28,252},{... | collective-permute-start | bytes 884744 | tf_op jit(solution)/shard_map/ppermute | solution.py:386
  31.7 7.1 %collective-permute-start.2 = (bf16[2,144,512]{2,1,0:T(8,128)(2,1)S(1)}, bf16[2,144,512]{2,1,0:T(8,128)(2,1)S(1)}, u32[]{:S(2)}, u32[]{:S(2)}) collective-permute-start(bf16[2,144,512]{2,1,0:T(8,128)(2,1)S(1)} %collective-permute-done.refs_2_), channel_id=1, source_target_pairs={{0,32},{4,228},{8,40},{12,236},{16,48},{20,244},{24,56},{28,252},{... | collective-permute-start | bytes 884744 | tf_op jit(solution)/shard_map/ppermute | solution.py:386
  35.4 12.6 %collective-permute-start.8 = (bf16[2,144,512]{2,1,0:T(8,128)(2,1)S(1)}, bf16[2,144,512]{2,1,0:T(8,128)(2,1)}, u32[]{:S(2)}, u32[]{:S(2)}) collective-permute-start(bf16[2,144,512]{2,1,0:T(8,128)(2,1)S(1)} %collective-permute-done.4.refs_3_), channel_id=1, source_target_pairs={{0,32},{4,228},{8,40},{12,236},{16,48},{20,244},{24,56},{28,252},{... | collective-permute-start | bytes 884744 | tf_op jit(solution)/shard_map/ppermute | solution.py:386
  38.8 9.2 %collective-permute-start.7 = (bf16[2,144,512]{2,1,0:T(8,128)(2,1)S(1)}, bf16[2,144,512]{2,1,0:T(8,128)(2,1)}, u32[]{:S(2)}, u32[]{:S(2)}) collective-permute-start(bf16[2,144,512]{2,1,0:T(8,128)(2,1)S(1)} %collective-permute-done.2.refs_4_), channel_id=1, source_target_pairs={{0,32},{4,228},{8,40},{12,236},{16,48},{20,244},{24,56},{28,252},{... | collective-permute-start | bytes 884744 | tf_op jit(solution)/shard_map/ppermute | solution.py:386
  48.0 5.9 %collective-permute-start.11 = (bf16[32,128,128]{2,1,0:T(8,128)(2,1)S(1)}, bf16[32,128,128]{2,1,0:T(8,128)(2,1)S(1)}, u32[]{:S(2)}, u32[]{:S(2)}) collective-permute-start(bf16[32,128,128]{2,1,0:T(8,128)(2,1)S(1)} %bitcast.17), channel_id=1, source_target_pairs={{0,4},{4,0},{8,12},{12,8},{16,20},{20,16},{24,28},{28,24},{32,36},... | collective-permute-start | bytes 3145736 | tf_op jit(solution)/shard_map/ppermute | solution.py:398
  48.1 9.7 %copy-start.1 = (bf16[16,256,64]{2,1,0:T(8,128)(2,1)S(1)}, bf16[16,256,64]{2,1,0:T(8,128)(2,1)}, u32[]{:S(2)}) copy-start(bf16[16,256,64]{2,1,0:T(8,128)(2,1)} %get-tuple-element.40.refs_11_.refs_8_) | copy-start | bytes 1572868
  48.1 16.5 %collective-permute-start.21 = (bf16[32,128,128]{2,1,0:T(8,128)(2,1)S(1)}, bf16[32,128,128]{2,1,0:T(8,128)(2,1)S(1)}, u32[]{:S(2)}, u32[]{:S(2)}) collective-permute-start(bf16[32,128,128]{2,1,0:T(8,128)(2,1)S(1)} %bitcast.16), channel_id=1, source_target_pairs={{0,4},{4,0},{8,12},{12,8},{16,20},{20,16},{24,28},{28,24},{32,36},... | collective-permute-start | bytes 3145736 | tf_op jit(solution)/shard_map/ppermute | solution.py:398
  48.6 4.1 %collective-permute-start.17 = (bf16[2,144,512]{2,1,0:T(8,128)(2,1)S(1)}, bf16[2,144,512]{2,1,0:T(8,128)(2,1)S(1)}, u32[]{:S(2)}, u32[]{:S(2)}) collective-permute-start(bf16[2,144,512]{2,1,0:T(8,128)(2,1)S(1)} %collective-permute-done.refs_2_), channel_id=1, source_target_pairs={{0,4},{4,0},{8,12},{12,8},{16,20},{20,16},{24,28},{28,24},{32,36},... | collective-permute-start | bytes 884744 | tf_op jit(solution)/shard_map/ppermute | solution.py:398
  48.7 4.4 %collective-permute-start.16 = (bf16[2,144,512]{2,1,0:T(8,128)(2,1)S(1)}, bf16[2,144,512]{2,1,0:T(8,128)(2,1)S(1)}, u32[]{:S(2)}, u32[]{:S(2)}) collective-permute-start(bf16[2,144,512]{2,1,0:T(8,128)(2,1)S(1)} %collective-permute-done.4.refs_3_), channel_id=1, source_target_pairs={{0,4},{4,0},{8,12},{12,8},{16,20},{20,16},{24,28},{28,24},{32,36},... | collective-permute-start | bytes 884744 | tf_op jit(solution)/shard_map/ppermute | solution.py:398
  49.1 8.6 %collective-permute-start.15 = (bf16[2,144,512]{2,1,0:T(8,128)(2,1)S(1)}, bf16[2,144,512]{2,1,0:T(8,128)(2,1)S(1)}, u32[]{:S(2)}, u32[]{:S(2)}) collective-permute-start(bf16[2,144,512]{2,1,0:T(8,128)(2,1)S(1)} %collective-permute-done.2.refs_4_), channel_id=1, source_target_pairs={{0,4},{4,0},{8,12},{12,8},{16,20},{20,16},{24,28},{28,24},{32,36},... | collective-permute-start | bytes 884744 | tf_op jit(solution)/shard_map/ppermute | solution.py:398
  52.7 5.1 %collective-permute-start.14 = (bf16[2,144,512]{2,1,0:T(8,128)(2,1)}, bf16[2,144,512]{2,1,0:T(8,128)(2,1)S(1)}, u32[]{:S(2)}, u32[]{:S(2)}) collective-permute-start(bf16[2,144,512]{2,1,0:T(8,128)(2,1)} %collective-permute-done.8.refs_5_), channel_id=1, source_target_pairs={{0,4},{4,0},{8,12},{12,8},{16,20},{20,16},{24,28},{28,24},{32,36},... | collective-permute-start | bytes 884744 | tf_op jit(solution)/shard_map/ppermute | solution.py:398
  53.1 10.9 %collective-permute-start.12 = (bf16[2,144,512]{2,1,0:T(8,128)(2,1)}, bf16[2,144,512]{2,1,0:T(8,128)(2,1)S(1)}, u32[]{:S(2)}, u32[]{:S(2)}) collective-permute-start(bf16[2,144,512]{2,1,0:T(8,128)(2,1)} %collective-permute-done.8.refs_5_), channel_id=1, source_target_pairs={{0,32},{4,228},{8,40},{12,236},{16,48},{20,244},{24,56},{28,252},{... | collective-permute-start | bytes 884744 | tf_op jit(solution)/shard_map/ppermute | solution.py:386
  53.9 10.6 %collective-permute-start.13 = (bf16[2,144,512]{2,1,0:T(8,128)(2,1)}, bf16[2,144,512]{2,1,0:T(8,128)(2,1)S(1)}, u32[]{:S(2)}, u32[]{:S(2)}) collective-permute-start(bf16[2,144,512]{2,1,0:T(8,128)(2,1)} %collective-permute-done.7.refs_0_), channel_id=1, source_target_pairs={{0,32},{4,228},{8,40},{12,236},{16,48},{20,244},{24,56},{28,252},{... | collective-permute-start | bytes 884744 | tf_op jit(solution)/shard_map/ppermute | solution.py:386
  57.7 6.9 %collective-permute-start.20 = (bf16[2,144,512]{2,1,0:T(8,128)(2,1)}, bf16[2,144,512]{2,1,0:T(8,128)(2,1)S(1)}, u32[]{:S(2)}, u32[]{:S(2)}) collective-permute-start(bf16[2,144,512]{2,1,0:T(8,128)(2,1)} %collective-permute-done.7.refs_0_), channel_id=1, source_target_pairs={{0,4},{4,0},{8,12},{12,8},{16,20},{20,16},{24,28},{28,24},{32,36},... | collective-permute-start | bytes 884744 | tf_op jit(solution)/shard_map/ppermute | solution.py:398
  64.0 1.8 %collective-permute-start.19 = (bf16[2,144,512]{2,1,0:T(8,128)(2,1)S(1)}, bf16[2,144,512]{2,1,0:T(8,128)(2,1)S(1)}, u32[]{:S(2)}, u32[]{:S(2)}) collective-permute-start(bf16[2,144,512]{2,1,0:T(8,128)(2,1)S(1)} %collective-permute-done.12.refs_1_), channel_id=1, source_target_pairs={{0,4},{4,0},{8,12},{12,8},{16,20},{20,16},{24,28},{28,24},{32,36},... | collective-permute-start | bytes 884744 | tf_op jit(solution)/shard_map/ppermute | solution.py:398
  64.5 1.6 %collective-permute-start.18 = (bf16[2,144,512]{2,1,0:T(8,128)(2,1)S(1)}, bf16[2,144,512]{2,1,0:T(8,128)(2,1)S(1)}, u32[]{:S(2)}, u32[]{:S(2)}) collective-permute-start(bf16[2,144,512]{2,1,0:T(8,128)(2,1)S(1)} %collective-permute-done.13.refs_2_), channel_id=1, source_target_pairs={{0,4},{4,0},{8,12},{12,8},{16,20},{20,16},{24,28},{28,24},{32,36},... | collective-permute-start | bytes 884744 | tf_op jit(solution)/shard_map/ppermute | solution.py:398
  66.2 11.3 %copy-start = (bf16[64,64,512]{2,1,0:T(8,128)(2,1)S(1)}, bf16[64,64,512]{2,1,0:T(8,128)(2,1)}, u32[]{:S(2)}) copy-start(bf16[64,64,512]{2,1,0:T(8,128)(2,1)} %latent_in.3) | copy-start | bytes 12582916
  66.2 11.2 %copy-start.3 = (bf16[64,2048]{1,0:T(8,128)(2,1)S(1)}, bf16[64,2048]{1,0:T(8,128)(2,1)}, u32[]{:S(2)}) copy-start(bf16[64,2048]{1,0:T(8,128)(2,1)} %q_nope_in.1) | copy-start | bytes 786436
  66.2 11.2 %copy-start.5 = (bf16[64,1024]{1,0:T(8,128)(2,1)S(1)}, bf16[64,1024]{1,0:T(8,128)(2,1)}, u32[]{:S(2)}) copy-start(bf16[64,1024]{1,0:T(8,128)(2,1)} %q_rope_in.1) | copy-start | bytes 393220
  66.2 11.2 %copy-start.6 = (bf16[64,4096]{1,0:T(8,128)(2,1)S(1)}, bf16[64,4096]{1,0:T(8,128)(2,1)}, u32[]{:S(2)}) copy-start(bf16[64,4096]{1,0:T(8,128)(2,1)} %rope_in.3) | copy-start | bytes 1572868
  66.2 11.2 %copy-start.13 = (s32[64]{0:T(128)S(1)}, s32[64]{0:T(128)}, u32[]{:S(2)}) copy-start(s32[64]{0:T(128)} %param.21) | copy-start | bytes 772
  73.8 15.0 %collective-permute-start.22 = (bf16[64,2176]{1,0:T(8,128)(2,1)S(1)}, bf16[64,2176]{1,0:T(8,128)(2,1)S(1)}, u32[]{:S(2)}, u32[]{:S(2)}) collective-permute-start(bf16[64,2176]{1,0:T(8,128)(2,1)S(1)} %get-tuple-element.51), channel_id=1, source_target_pairs={{0,24},{4,12},{8,0},{12,20},{16,8},{20,28},{24,16},{28,4},{32,56},... | collective-permute-start | bytes 835592 | tf_op jit(solution)/shard_map/ppermute | solution.py:390
  73.8 14.9 %collective-permute-start.23 = (bf16[64,2176]{1,0:T(8,128)(2,1)S(1)}, bf16[64,2176]{1,0:T(8,128)(2,1)S(1)}, u32[]{:S(2)}, u32[]{:S(2)}) collective-permute-start(bf16[64,2176]{1,0:T(8,128)(2,1)S(1)} %get-tuple-element.52), channel_id=1, source_target_pairs={{0,16},{4,20},{8,24},{12,28},{16,0},{20,4},{24,8},{28,12},{32,48},... | collective-permute-start | bytes 835592 | tf_op jit(solution)/shard_map/ppermute | solution.py:390
  76.8 12.6 %collective-permute-start.24 = (bf16[64,2176]{1,0:T(8,128)(2,1)S(1)}, bf16[64,2176]{1,0:T(8,128)(2,1)S(1)}, u32[]{:S(2)}, u32[]{:S(2)}) collective-permute-start(bf16[64,2176]{1,0:T(8,128)(2,1)S(1)} %get-tuple-element.53), channel_id=1, source_target_pairs={{0,8},{4,28},{8,16},{12,4},{16,24},{20,12},{24,0},{28,20},{32,40},... | collective-permute-start | bytes 835592 | tf_op jit(solution)/shard_map/ppermute | solution.py:390
  (8 other events, 66.0 us)

commit v4 on v3

--- a/solution.py
+++ b/solution.py
@@ -60,13 +60,21 @@
     return copies
 
 
-def pack_kernel(pattern, page_slot, rope_in, latent_in, q_nope, q_rope, pages, pay, rope, sems):
+def pack_kernel(
+    pattern, page_slot, rope_in, latent_in, q_nope, q_rope, w_uk, w_uv, pages, pay, weights, rope, sems
+):
+    core, heads = lax.rem(lax.axis_index("rows"), NC), HEADS // 2
     copies = load_all(
         [
             (rope_in, rope),
             (latent_in, pages.at[:, :PAGE, :]),
             (q_nope, pay.at[:, :QN]),
             (q_rope, pay.at[:, QN : QN + QR]),
+        ]
+        + [
+            (full.at[pl.ds(to * HEADS + heads * core, heads)], weights.at[pl.ds((2 * to + i) * heads, heads)])
+            for i, full in enumerate((w_uk, w_uv))
+            for to in range(NY)
         ],
         sems,
     )
@@ -418,25 +426,17 @@
     def after(a, *others):
         return lax.optimization_barrier((a, *others))[0]
 
-    def halve(full):
-        whole = full.reshape(NY, HEADS, *full.shape[1:])
-        half = lax.dynamic_slice_in_dim(whole, (row % NC) * (HEADS // 2), HEADS // 2, 1)
-        return half.reshape(NY * HEADS // 2, *full.shape[1:])
-
-    half = (NY, HEADS // 2, NOPE, 128)
-    both = jnp.concatenate([halve(w).reshape(half) for w in (w_uk, w_uv)], axis=1).reshape(NY * HEADS, NOPE, 128)
-    page_pattern = after(page_pattern, both)
-    both = exchange(both)
-    pages, pay = pl.pallas_call(
+    pages, pay, both = pl.pallas_call(
         pack_kernel,
-        out_shape=(struct(2, UNIT, KVL), struct(ROWS, PAY)),
-        in_specs=[VMEM] * 2 + [HBM] * 4,
-        out_specs=(VMEM,) * 2,
-        scratch_shapes=[pltpu.VMEM((2, PAGE * ROPE), BF16), pltpu.SemaphoreType.DMA((4,))],
+        out_shape=(struct(2, UNIT, KVL), struct(ROWS, PAY), struct(NY * HEADS, NOPE, 128)),
+        in_specs=[VMEM] * 2 + [HBM] * 6,
+        out_specs=(VMEM,) * 3,
+        scratch_shapes=[pltpu.VMEM((2, PAGE * ROPE), BF16), pltpu.SemaphoreType.DMA((4 + 2 * NY,))],
         compiler_params=params(60),
         cost_estimate=cost(2),
         name="pack",
-    )(page_pattern.T, page_slot.reshape(1, -1), prefix_rope, prefix_latent, q_nope, q_rope)
+    )(page_pattern.T, page_slot.reshape(1, -1), prefix_rope, prefix_latent, q_nope, q_rope, w_uk, w_uv)
+    both = exchange(both)
 
     a, b = [pages], [swap(pages)]
     a_pay, b_pay = [pay], [swap(pay)]
@@ -450,6 +450,7 @@
     pays = [pay, a_pay[1], a_pay[2], swap(b_pay[1])]
     a.append(ring_z(after(a[2], b[1], b_pay[1])))
     b.append(ring_z(b[2]))
+    a_swap, b_swap = [None, swap(a[1])], [None, swap(b[1])]
     square = (SLOTS, SLOTS)
     q_slots, q_rot, page_bit, *ties = pl.pallas_call(
         gather_kernel,
@@ -463,7 +464,7 @@
         compiler_params=params(60),
         cost_estimate=cost(3),
         name="gather",
-    )(place, *pays)
+    )(place, after(pays[0], a_swap[1], b_swap[1]), *pays[1:])
 
     split = both.reshape(NY, HEADS, NOPE, 128)
     k_part, v_part = split[:, : HEADS // 2], split[:, HEADS // 2 :]
@@ -482,8 +483,8 @@
     )(place, q_slots, both, k_swap)
 
     a.append(ring_z(after(a[3], b[2], a_pay[2])))
-    a_swap = [None] + [swap(u) for u in a[1:4]]
-    b_swap = [None] + [swap(u) for u in b[1:3]]
+    a_swap += [swap(a[2]), swap(a[3])]
+    b_swap.append(swap(b[2]))
     early_units = [a[0], b[0], a[1], b[1], a[2], b[2], b_swap[2], a_swap[2], b_swap[1], a_swap[1]]
 
     early, early_logs = pl.pallas_call(

time: 92.1 us -> 86.8 us (0.942)
  waiting for transfers between devices: 12.1 us -> 8.75 us
  local copies, waits for them, and re-layouts: 2.09 us -> 0.21 us
  other arithmetic: 2.2 us -> 0.59 us
  starting transfers between devices: 35.7 us -> 37 us
  Pallas kernels: 38.6 us -> 39.8 us
    ppermute x12, waiting for transfers between devices: 5.25 us -> 1.96 us  [swap(): lax.ppermute(a, 'rows', [(row_of(z, x, c), row_of(z, x, 1 - c)) for z, x,...]
    ppermute x12, starting transfers between devices: 5.57 us -> 7.93 us  [swap(): lax.ppermute(a, 'rows', [(row_of(z, x, c), row_of(z, x, 1 - c)) for z, x,...]
    dynamic_slice x1 -> x0, local copies, waits for them, and re-layouts: 1.78 us -> none  [halve(): lax.dynamic_slice_in_dim(whole, row % NC * (HEADS // 2), HEADS // 2, 1)]
    concatenate x1 -> x0, other arithmetic: 1.53 us -> none  [shards(): jnp.concatenate([halve(w).reshape(half) for w in (w_uk, w_uv)], axis=1)]
    pallas_call x1, Pallas kernels: 2.77 us -> 4.06 us  [shards(): pl.pallas_call(pack_kernel, out_shape=(struct(2, UNIT, KVL), struct(ROWS,...]
    ppermute x7, starting transfers between devices: 17.7 us -> 16.7 us  [ring_z(): lax.ppermute(a, 'rows', [(row_of(z, x, c), row_of(z + 1 - 2 * c, x, c)) f...]
  transfers between devices with their start and end apart: 26 -> 26, of which waited for: 7 -> 7; matrix products, arithmetic and copies ran while one was open for 1% -> 1% of each run, Pallas kernels for 32% -> 31%
where the time goes in v4:
time: 86.8 us; the launch traced here: 86.5 us
  Pallas kernels  39.8 us (46%)
  starting transfers between devices  37 us (43%)
  waiting for transfers between devices  8.75 us (10%)
    ppermute x7, starting transfers between devices, ring_z(): lax.ppermute(a, 'rows', [(row_of(z, x, c), row_of(z + 1 - 2 * c, x, c)) f...  16.7 us
    pallas_call x1, Pallas kernels, shards(): pl.pallas_call(suffix_kernel, out_shape=struct(ROWS, RET), in_specs=[SMEM...  11.3 us
    ppermute x12, starting transfers between devices, swap(): lax.ppermute(a, 'rows', [(row_of(z, x, c), row_of(z, x, 1 - c)) for z, x,...  7.93 us
    pallas_call x1, Pallas kernels, shards(): pl.pallas_call(late_kernel, out_shape=(struct(ROWS, RET),) * 4, in_specs=...  7.52 us
    ppermute x6, starting transfers between devices, ring_x(): lax.ppermute(a, 'rows', [(row_of(z, x, c), row_of(z, x + steps * (1 - 2 *...  7.19 us
    ppermute x7, waiting for transfers between devices, ring_z(): lax.ppermute(a, 'rows', [(row_of(z, x, c), row_of(z + 1 - 2 * c, x, c)) f...  6.25 us
    pallas_call x1, Pallas kernels, shards(): pl.pallas_call(gather_kernel, out_shape=(struct(SLOTS, QN), struct(HEADS,...  6.07 us
    pallas_call x1, Pallas kernels, shards(): pl.pallas_call(early_kernel, out_shape=(struct(HEADS, EARLY * 16, KVL), s...  5.89 us
  transfers between devices with their start and end apart: 26, of which 7 were waited for; matrix products, arithmetic and copies ran while one was open for 1% of the time, Pallas kernels for 31%

profile of v4, /device:TPU:1, one launch (start us, length us, event | category | flops | bytes accessed | tf_op | source)
XLA Modules:
  0.0 86.5 jit_solution(16429890704894853270)
XLA Ops:
  0.0 4.1 %pack.1 = (bf16[2,144,512]{2,1,0:T(8,128)(2,1)}, bf16[64,3200]{1,0:T(8,128)(2,1)}, bf16[64,128,128]{2,1,0:T(8,128)(2,1)}) custom-call(s32[2,64]{1,0:T(2,128)} %bitcast.14, s32[1,128]{1,0:T(1,128)} %bitcast.15, bf16[2,8192]{1,0:T(2,128)(2,1)} %rope_in.2, bf16[2,128,512]{2,1,0:T(8,128)(2,1)} %latent_in.2, bf16[64,2048]{1,0:T(8,128)(2,1)} %q_nope_in.1, ...), custom_call_target="tpu_custom_call" | custom-call | flops 2000000 | bytes 6000000 | tf_op jit(solution)/shard_map/pack/pallas_call | solution.py:429
  4.1 5.2 %all-to-all-start = ((bf16[64,128,128]{2,1,0:T(8,128)(2,1)}), bf16[64,128,128]{2,1,0:T(8,128)(2,1)S(1)}, u32[]{:S(2)}, u32[]{:S(2)}) async-start(bf16[64,128,128]{2,1,0:T(8,128)(2,1)} %get-tuple-element.31), calls=%async_computation | async-start | bytes 4194304 | tf_op jit(solution)/shard_map/all_to_all | solution.py:424
  9.2 1.9 %collective-permute-start.5 = (bf16[64,3200]{1,0:T(8,128)(2,1)}, bf16[64,3200]{1,0:T(8,128)(2,1)S(1)}, u32[]{:S(2)}, u32[]{:S(2)}) collective-permute-start(bf16[64,3200]{1,0:T(8,128)(2,1)} %get-tuple-element.37.p0), channel_id=1, source_target_pairs={{0,4},{4,0},{8,12},{12,8},{16,20},{20,16},{24,28},{28,24},{32,36},... | collective-permute-start | bytes 1228808 | tf_op jit(solution)/shard_map/ppermute | solution.py:406
  11.3 1.5 %collective-permute-start.1 = (bf16[64,3200]{1,0:T(8,128)(2,1)}, bf16[64,3200]{1,0:T(8,128)(2,1)}, u32[]{:S(2)}, u32[]{:S(2)}) collective-permute-start(bf16[64,3200]{1,0:T(8,128)(2,1)} %get-tuple-element.37.p0), channel_id=1, source_target_pairs={{0,8},{4,28},{8,16},{12,4},{16,24},{20,12},{24,0},{28,20},{32,40},... | collective-permute-start | bytes 1228808 | tf_op jit(solution)/shard_map/ppermute | solution.py:398
  12.8 1.5 %collective-permute-start.6 = (bf16[64,3200]{1,0:T(8,128)(2,1)S(1)}, bf16[64,3200]{1,0:T(8,128)(2,1)}, u32[]{:S(2)}, u32[]{:S(2)}) collective-permute-start(bf16[64,3200]{1,0:T(8,128)(2,1)S(1)} %collective-permute-done.5), channel_id=1, source_target_pairs={{0,8},{4,28},{8,16},{12,4},{16,24},{20,12},{24,0},{28,20},{32,40},... | collective-permute-start | bytes 1228808 | tf_op jit(solution)/shard_map/ppermute | solution.py:398
  14.3 5.6 %collective-permute-start = (bf16[2,144,512]{2,1,0:T(8,128)(2,1)S(1)}, bf16[2,144,512]{2,1,0:T(8,128)(2,1)S(1)}, u32[]{:S(2)}, u32[]{:S(2)}) collective-permute-start(bf16[2,144,512]{2,1,0:T(8,128)(2,1)S(1)} %copy-done.7), channel_id=1, source_target_pairs={{0,32},{4,228},{8,40},{12,236},{16,48},{20,244},{24,56},{28,252},{... | collective-permute-start | bytes 884744 | tf_op jit(solution)/shard_map/ppermute | solution.py:394
  19.8 0.7 collective-permute-start.4
  20.6 2.9 %collective-permute-done.refs_2_ = bf16[2,144,512]{2,1,0:T(8,128)(2,1)S(1)} collective-permute-done((bf16[2,144,512]{2,1,0:T(8,128)(2,1)S(1)}, bf16[2,144,512]{2,1,0:T(8,128)(2,1)S(1)}, u32[]{:S(2)}, u32[]{:S(2)}) %collective-permute-start) | collective-permute-done | bytes 294944 | tf_op jit(solution)/shard_map/ppermute | solution.py:394
  23.5 0.5 collective-permute-start.11
  24.1 1.6 %collective-permute-start.12 = (bf16[64,3200]{1,0:T(8,128)(2,1)}, bf16[64,3200]{1,0:T(8,128)(2,1)}, u32[]{:S(2)}, u32[]{:S(2)}) collective-permute-start(bf16[64,3200]{1,0:T(8,128)(2,1)} %collective-permute-done.6), channel_id=1, source_target_pairs={{0,4},{4,0},{8,12},{12,8},{16,20},{20,16},{24,28},{28,24},{32,36},... | collective-permute-start | bytes 1228808 | tf_op jit(solution)/shard_map/ppermute | solution.py:406
  25.7 4.5 %collective-permute-start.2 = (bf16[2,144,512]{2,1,0:T(8,128)(2,1)S(1)}, bf16[2,144,512]{2,1,0:T(8,128)(2,1)}, u32[]{:S(2)}, u32[]{:S(2)}) collective-permute-start(bf16[2,144,512]{2,1,0:T(8,128)(2,1)S(1)} %collective-permute-done.refs_2_), channel_id=1, source_target_pairs={{0,32},{4,228},{8,40},{12,236},{16,48},{20,244},{24,56},{28,252},{... | collective-permute-start | bytes 884744 | tf_op jit(solution)/shard_map/ppermute | solution.py:394
  30.2 0.5 collective-permute-start.10
  30.7 0.6 pad_add_fusion.place.refs_6_
  31.3 2.6 %collective-permute-done.2.refs_4_ = bf16[2,144,512]{2,1,0:T(8,128)(2,1)} collective-permute-done((bf16[2,144,512]{2,1,0:T(8,128)(2,1)S(1)}, bf16[2,144,512]{2,1,0:T(8,128)(2,1)}, u32[]{:S(2)}, u32[]{:S(2)}) %collective-permute-start.2) | collective-permute-done | bytes 294944 | tf_op jit(solution)/shard_map/ppermute | solution.py:394
  33.8 3.4 %collective-permute-start.7 = (bf16[2,144,512]{2,1,0:T(8,128)(2,1)}, bf16[2,144,512]{2,1,0:T(8,128)(2,1)}, u32[]{:S(2)}, u32[]{:S(2)}) collective-permute-start(bf16[2,144,512]{2,1,0:T(8,128)(2,1)} %collective-permute-done.2.refs_4_), channel_id=1, source_target_pairs={{0,32},{4,228},{8,40},{12,236},{16,48},{20,244},{24,56},{28,252},{... | collective-permute-start | bytes 884744 | tf_op jit(solution)/shard_map/ppermute | solution.py:394
  37.3 6.1 %gather.1 = (bf16[256,2048]{1,0:T(8,128)(2,1)}, bf16[16,256,64]{2,1,0:T(8,128)(2,1)}, f32[256,128]{1,0:T(8,128)}, bf16[256,256]{1,0:T(8,128)(2,1)}, bf16[256,256...) custom-call(s32[4]{0:T(128)} %pad_add_fusion.place.refs_6_, bf16[64,3200]{1,0:T(8,128)(2,1)} %get-tuple-element.37.p0, ...), custom_call_target="tpu_custom_call" | custom-call | flops 3000000 | bytes 9000000 | tf_op jit(solution)/shard_map/gather/pallas_call | solution.py:455
  43.5 0.7 collective-permute-done.8.refs_5_
  44.3 2.4 %collective-permute-start.13 = (bf16[32,128,128]{2,1,0:T(8,128)(2,1)S(1)}, bf16[32,128,128]{2,1,0:T(8,128)(2,1)S(1)}, u32[]{:S(2)}, u32[]{:S(2)}) collective-permute-start(bf16[32,128,128]{2,1,0:T(8,128)(2,1)S(1)} %bitcast.13), channel_id=1, source_target_pairs={{0,4},{4,0},{8,12},{12,8},{16,20},{20,16},{24,28},{28,24},{32,36},... | collective-permute-start | bytes 3145736 | tf_op jit(solution)/shard_map/ppermute | solution.py:406
  46.7 0.4 collective-permute-start.17
  47.3 1.3 %collective-permute-start.14 = (bf16[2,144,512]{2,1,0:T(8,128)(2,1)}, bf16[2,144,512]{2,1,0:T(8,128)(2,1)S(1)}, u32[]{:S(2)}, u32[]{:S(2)}) collective-permute-start(bf16[2,144,512]{2,1,0:T(8,128)(2,1)} %collective-permute-done.8.refs_5_), channel_id=1, source_target_pairs={{0,32},{4,228},{8,40},{12,236},{16,48},{20,244},{24,56},{28,252},{... | collective-permute-start | bytes 884744 | tf_op jit(solution)/shard_map/ppermute | solution.py:394
  48.9 1.2 %collective-permute-start.15 = (bf16[2,144,512]{2,1,0:T(8,128)(2,1)}, bf16[2,144,512]{2,1,0:T(8,128)(2,1)S(1)}, u32[]{:S(2)}, u32[]{:S(2)}) collective-permute-start(bf16[2,144,512]{2,1,0:T(8,128)(2,1)} %collective-permute-done.7.refs_0_), channel_id=1, source_target_pairs={{0,32},{4,228},{8,40},{12,236},{16,48},{20,244},{24,56},{28,252},{... | collective-permute-start | bytes 884744 | tf_op jit(solution)/shard_map/ppermute | solution.py:394
  50.2 3.3 %queries.1.refs_10_.refs_7_ = bf16[16,256,512]{2,1,0:T(8,128)(2,1)S(1)} custom-call(s32[4]{0:T(128)S(1)} %copy-done.12, bf16[256,2048]{1,0:T(8,128)(2,1)S(1)} %copy-done.2, bf16[64,128,128]{2,1,0:T(8,128)(2,1)S(1)} %all-to-all-done.both.refs_16_, bf16[32,128,128]{2,1,0:T(8,128)(2,1)S(1)} %collective-permute-done.13.k_swap), custom_call_target="tpu_custom_call" | custom-call | flops 3000000 | bytes 9000000 | tf_op jit(solution)/shard_map/queries/pallas_call | solution.py:474
  53.6 5.9 %early_pages.1 = (bf16[16,160,512]{2,1,0:T(8,128)(2,1)S(1)}, f32[160,128]{1,0:T(8,128)S(1)}) custom-call(bf16[2,144,512]{2,1,0:T(8,128)(2,1)S(1)} %copy-done.7, bf16[2,144,512]{2,1,0:T(8,128)(2,1)S(1)} %collective-permute-done.3.refs_1_, bf16[2,144,512]{2,1,0:T(8,128)(2,1)S(1)} %collective-permute-done.refs_2_, ...), custom_call_target="tpu_custom_call" | custom-call | flops 1000000 | bytes 3000000 | tf_op jit(solution)/shard_map/early_pages/pallas_call | solution.py:490
  59.5 0.6 collective-permute-start.19
  60.2 1.1 %collective-permute-done.19.refs_4_ = bf16[2,144,512]{2,1,0:T(8,128)(2,1)S(1)} collective-permute-done((bf16[2,144,512]{2,1,0:T(8,128)(2,1)S(1)}, bf16[2,144,512]{2,1,0:T(8,128)(2,1)S(1)}, u32[]{:S(2)}, u32[]{:S(2)}) %collective-permute-start.19) | collective-permute-done | bytes 294944 | tf_op jit(solution)/shard_map/ppermute | solution.py:406
  61.3 0.4 collective-permute-done.18.refs_3_
  61.8 7.5 %late_pages.1 = (bf16[64,2176]{1,0:T(8,128)(2,1)S(1)}, bf16[64,2176]{1,0:T(8,128)(2,1)S(1)}, bf16[64,2176]{1,0:T(8,128)(2,1)S(1)}, bf16[64,2176]{1,0:T(8,128)(2,1)S(1)}) custom-call(bf16[2,144,512]{2,1,0:T(8,128)(2,1)} %collective-permute-done.7.refs_0_, bf16[2,144,512]{2,1,0:T(8,128)(2,1)S(1)} %collective-permute-done.14.refs_1_, ...), custom_call_target="tpu_custom_call" | custom-call | flops 7000000 | bytes 21000000 | tf_op jit(solution)/shard_map/late_pages/pallas_call | solution.py:504
  69.4 2.4 %collective-permute-start.23 = (bf16[64,2176]{1,0:T(8,128)(2,1)S(1)}, bf16[64,2176]{1,0:T(8,128)(2,1)S(1)}, u32[]{:S(2)}, u32[]{:S(2)}) collective-permute-start(bf16[64,2176]{1,0:T(8,128)(2,1)S(1)} %get-tuple-element.54), channel_id=1, source_target_pairs={{0,16},{4,20},{8,24},{12,28},{16,0},{20,4},{24,8},{28,12},{32,48},... | collective-permute-start | bytes 835592 | tf_op jit(solution)/shard_map/ppermute | solution.py:398
  71.8 1.1 %collective-permute-start.24 = (bf16[64,2176]{1,0:T(8,128)(2,1)S(1)}, bf16[64,2176]{1,0:T(8,128)(2,1)S(1)}, u32[]{:S(2)}, u32[]{:S(2)}) collective-permute-start(bf16[64,2176]{1,0:T(8,128)(2,1)S(1)} %get-tuple-element.55), channel_id=1, source_target_pairs={{0,8},{4,28},{8,16},{12,4},{16,24},{20,12},{24,0},{28,20},{32,40},... | collective-permute-start | bytes 835592 | tf_op jit(solution)/shard_map/ppermute | solution.py:398
  73.0 11.3 %suffix.1.own = bf16[64,2176]{1,0:T(8,128)(2,1)S(1)} custom-call(s32[4]{0:T(128)S(1)} %copy-done.12, s32[1,64]{1,0:T(1,128)S(1)} %bitcast.11, bf16[64,2048]{1,0:T(8,128)(2,1)S(1)} %copy-done.3, bf16[64,1024]{1,0:T(8,128)(2,1)S(1)} %copy-done.5, bf16[64,64,512]{2,1,0:T(8,128)(2,1)S(1)} %copy-done, bf16[64,4096]{1,0:T(8,128)(2,1)S(1)} %copy-done.6, ...), custom_call_target="tpu_custom_call" | custom-call | flops 8000000 | bytes 24000000 | tf_op jit(solution)/shard_map/suffix/pallas_call | solution.py:521
  84.3 0.5 collective-permute-done.24.r3
  84.9 1.7 %combine.1 = bf16[64,2048]{1,0:T(8,128)(2,1)} custom-call(bf16[64,2176]{1,0:T(8,128)(2,1)S(1)} %suffix.1.own, bf16[64,2176]{1,0:T(8,128)(2,1)S(1)} %get-tuple-element.52.r0, bf16[64,2176]{1,0:T(8,128)(2,1)S(1)} %collective-permute-done.22.r1, bf16[64,2176]{1,0:T(8,128)(2,1)S(1)} %collective-permute-done.23.r2, bf16[64,2176]{1,0:T(8,128)(2,1)S(1)} %collective-permute-done.24.r3), custom_call_target="tpu_custom_call" | custom-call | flops 2000000 | bytes 6000000 | tf_op jit(solution)/shard_map/combine/pallas_call | solution.py:540
  (57 shorter events, 1.3 us)
Async XLA Ops:
  4.1 39.3 %all-to-all-start = ((bf16[64,128,128]{2,1,0:T(8,128)(2,1)}), bf16[64,128,128]{2,1,0:T(8,128)(2,1)S(1)}, u32[]{:S(2)}, u32[]{:S(2)}) async-start(bf16[64,128,128]{2,1,0:T(8,128)(2,1)} %get-tuple-element.31), calls=%async_computation | async-start | bytes 4194304 | tf_op jit(solution)/shard_map/all_to_all | solution.py:424
  9.2 3.5 %collective-permute-start.5 = (bf16[64,3200]{1,0:T(8,128)(2,1)}, bf16[64,3200]{1,0:T(8,128)(2,1)S(1)}, u32[]{:S(2)}, u32[]{:S(2)}) collective-permute-start(bf16[64,3200]{1,0:T(8,128)(2,1)} %get-tuple-element.37.p0), channel_id=1, source_target_pairs={{0,4},{4,0},{8,12},{12,8},{16,20},{20,16},{24,28},{28,24},{32,36},... | collective-permute-start | bytes 1228808 | tf_op jit(solution)/shard_map/ppermute | solution.py:406
  11.2 8.7 %collective-permute-start.3 = (bf16[2,144,512]{2,1,0:T(8,128)(2,1)S(1)}, bf16[2,144,512]{2,1,0:T(8,128)(2,1)S(1)}, u32[]{:S(2)}, u32[]{:S(2)}) collective-permute-start(bf16[2,144,512]{2,1,0:T(8,128)(2,1)S(1)} %copy-done.7), channel_id=1, source_target_pairs={{0,4},{4,0},{8,12},{12,8},{16,20},{20,16},{24,28},{28,24},{32,36},... | collective-permute-start | bytes 884744 | tf_op jit(solution)/shard_map/ppermute | solution.py:406
  11.3 12.2 %collective-permute-start.1 = (bf16[64,3200]{1,0:T(8,128)(2,1)}, bf16[64,3200]{1,0:T(8,128)(2,1)}, u32[]{:S(2)}, u32[]{:S(2)}) collective-permute-start(bf16[64,3200]{1,0:T(8,128)(2,1)} %get-tuple-element.37.p0), channel_id=1, source_target_pairs={{0,8},{4,28},{8,16},{12,4},{16,24},{20,12},{24,0},{28,20},{32,40},... | collective-permute-start | bytes 1228808 | tf_op jit(solution)/shard_map/ppermute | solution.py:398
  12.8 11.3 %collective-permute-start.6 = (bf16[64,3200]{1,0:T(8,128)(2,1)S(1)}, bf16[64,3200]{1,0:T(8,128)(2,1)}, u32[]{:S(2)}, u32[]{:S(2)}) collective-permute-start(bf16[64,3200]{1,0:T(8,128)(2,1)S(1)} %collective-permute-done.5), channel_id=1, source_target_pairs={{0,8},{4,28},{8,16},{12,4},{16,24},{20,12},{24,0},{28,20},{32,40},... | collective-permute-start | bytes 1228808 | tf_op jit(solution)/shard_map/ppermute | solution.py:398
  14.3 9.2 %collective-permute-start = (bf16[2,144,512]{2,1,0:T(8,128)(2,1)S(1)}, bf16[2,144,512]{2,1,0:T(8,128)(2,1)S(1)}, u32[]{:S(2)}, u32[]{:S(2)}) collective-permute-start(bf16[2,144,512]{2,1,0:T(8,128)(2,1)S(1)} %copy-done.7), channel_id=1, source_target_pairs={{0,32},{4,228},{8,40},{12,236},{16,48},{20,244},{24,56},{28,252},{... | collective-permute-start | bytes 884744 | tf_op jit(solution)/shard_map/ppermute | solution.py:394
  19.8 10.3 %collective-permute-start.4 = (bf16[2,144,512]{2,1,0:T(8,128)(2,1)S(1)}, bf16[2,144,512]{2,1,0:T(8,128)(2,1)S(1)}, u32[]{:S(2)}, u32[]{:S(2)}) collective-permute-start(bf16[2,144,512]{2,1,0:T(8,128)(2,1)S(1)} %collective-permute-done.3.refs_1_), channel_id=1, source_target_pairs={{0,32},{4,228},{8,40},{12,236},{16,48},{20,244},{24,56},{28,252},{... | collective-permute-start | bytes 884744 | tf_op jit(solution)/shard_map/ppermute | solution.py:394
  23.5 13.8 %collective-permute-start.11 = (bf16[64,3200]{1,0:T(8,128)(2,1)}, bf16[64,3200]{1,0:T(8,128)(2,1)}, u32[]{:S(2)}, u32[]{:S(2)}) collective-permute-start(bf16[64,3200]{1,0:T(8,128)(2,1)} %collective-permute-done.1.p1), channel_id=1, source_target_pairs={{0,8},{4,28},{8,16},{12,4},{16,24},{20,12},{24,0},{28,20},{32,40},... | collective-permute-start | bytes 1228808 | tf_op jit(solution)/shard_map/ppermute | solution.py:398
  24.1 13.2 %collective-permute-start.12 = (bf16[64,3200]{1,0:T(8,128)(2,1)}, bf16[64,3200]{1,0:T(8,128)(2,1)}, u32[]{:S(2)}, u32[]{:S(2)}) collective-permute-start(bf16[64,3200]{1,0:T(8,128)(2,1)} %collective-permute-done.6), channel_id=1, source_target_pairs={{0,4},{4,0},{8,12},{12,8},{16,20},{20,16},{24,28},{28,24},{32,36},... | collective-permute-start | bytes 1228808 | tf_op jit(solution)/shard_map/ppermute | solution.py:406
  25.7 8.1 %collective-permute-start.2 = (bf16[2,144,512]{2,1,0:T(8,128)(2,1)S(1)}, bf16[2,144,512]{2,1,0:T(8,128)(2,1)}, u32[]{:S(2)}, u32[]{:S(2)}) collective-permute-start(bf16[2,144,512]{2,1,0:T(8,128)(2,1)S(1)} %collective-permute-done.refs_2_), channel_id=1, source_target_pairs={{0,32},{4,228},{8,40},{12,236},{16,48},{20,244},{24,56},{28,252},{... | collective-permute-start | bytes 884744 | tf_op jit(solution)/shard_map/ppermute | solution.py:394
  30.2 7.1 %collective-permute-start.9 = (bf16[2,144,512]{2,1,0:T(8,128)(2,1)S(1)}, bf16[2,144,512]{2,1,0:T(8,128)(2,1)}, u32[]{:S(2)}, u32[]{:S(2)}) collective-permute-start(bf16[2,144,512]{2,1,0:T(8,128)(2,1)S(1)} %collective-permute-done.refs_2_), channel_id=1, source_target_pairs={{0,4},{4,0},{8,12},{12,8},{16,20},{20,16},{24,28},{28,24},{32,36},... | collective-permute-start | bytes 884744 | tf_op jit(solution)/shard_map/ppermute | solution.py:406
  30.2 7.1 %collective-permute-start.10 = (bf16[2,144,512]{2,1,0:T(8,128)(2,1)S(1)}, bf16[2,144,512]{2,1,0:T(8,128)(2,1)}, u32[]{:S(2)}, u32[]{:S(2)}) collective-permute-start(bf16[2,144,512]{2,1,0:T(8,128)(2,1)S(1)} %collective-permute-done.4.refs_3_), channel_id=1, source_target_pairs={{0,4},{4,0},{8,12},{12,8},{16,20},{20,16},{24,28},{28,24},{32,36},... | collective-permute-start | bytes 884744 | tf_op jit(solution)/shard_map/ppermute | solution.py:406
  33.8 9.7 %collective-permute-start.7 = (bf16[2,144,512]{2,1,0:T(8,128)(2,1)}, bf16[2,144,512]{2,1,0:T(8,128)(2,1)}, u32[]{:S(2)}, u32[]{:S(2)}) collective-permute-start(bf16[2,144,512]{2,1,0:T(8,128)(2,1)} %collective-permute-done.2.refs_4_), channel_id=1, source_target_pairs={{0,32},{4,228},{8,40},{12,236},{16,48},{20,244},{24,56},{28,252},{... | collective-permute-start | bytes 884744 | tf_op jit(solution)/shard_map/ppermute | solution.py:394
  37.2 7.0 %collective-permute-start.8 = (bf16[2,144,512]{2,1,0:T(8,128)(2,1)S(1)}, bf16[2,144,512]{2,1,0:T(8,128)(2,1)}, u32[]{:S(2)}, u32[]{:S(2)}) collective-permute-start(bf16[2,144,512]{2,1,0:T(8,128)(2,1)S(1)} %collective-permute-done.4.refs_3_), channel_id=1, source_target_pairs={{0,32},{4,228},{8,40},{12,236},{16,48},{20,244},{24,56},{28,252},{... | collective-permute-start | bytes 884744 | tf_op jit(solution)/shard_map/ppermute | solution.py:394
  44.3 4.7 %collective-permute-start.13 = (bf16[32,128,128]{2,1,0:T(8,128)(2,1)S(1)}, bf16[32,128,128]{2,1,0:T(8,128)(2,1)S(1)}, u32[]{:S(2)}, u32[]{:S(2)}) collective-permute-start(bf16[32,128,128]{2,1,0:T(8,128)(2,1)S(1)} %bitcast.13), channel_id=1, source_target_pairs={{0,4},{4,0},{8,12},{12,8},{16,20},{20,16},{24,28},{28,24},{32,36},... | collective-permute-start | bytes 3145736 | tf_op jit(solution)/shard_map/ppermute | solution.py:406
  46.7 13.5 %collective-permute-start.21 = (bf16[32,128,128]{2,1,0:T(8,128)(2,1)S(1)}, bf16[32,128,128]{2,1,0:T(8,128)(2,1)S(1)}, u32[]{:S(2)}, u32[]{:S(2)}) collective-permute-start(bf16[32,128,128]{2,1,0:T(8,128)(2,1)S(1)} %bitcast.12), channel_id=1, source_target_pairs={{0,4},{4,0},{8,12},{12,8},{16,20},{20,16},{24,28},{28,24},{32,36},... | collective-permute-start | bytes 3145736 | tf_op jit(solution)/shard_map/ppermute | solution.py:406
  46.7 6.7 %collective-permute-start.17 = (bf16[2,144,512]{2,1,0:T(8,128)(2,1)}, bf16[2,144,512]{2,1,0:T(8,128)(2,1)S(1)}, u32[]{:S(2)}, u32[]{:S(2)}) collective-permute-start(bf16[2,144,512]{2,1,0:T(8,128)(2,1)} %collective-permute-done.2.refs_4_), channel_id=1, source_target_pairs={{0,4},{4,0},{8,12},{12,8},{16,20},{20,16},{24,28},{28,24},{32,36},... | collective-permute-start | bytes 884744 | tf_op jit(solution)/shard_map/ppermute | solution.py:406
  47.2 6.4 %collective-permute-start.16 = (bf16[2,144,512]{2,1,0:T(8,128)(2,1)}, bf16[2,144,512]{2,1,0:T(8,128)(2,1)S(1)}, u32[]{:S(2)}, u32[]{:S(2)}) collective-permute-start(bf16[2,144,512]{2,1,0:T(8,128)(2,1)} %collective-permute-done.8.refs_5_), channel_id=1, source_target_pairs={{0,4},{4,0},{8,12},{12,8},{16,20},{20,16},{24,28},{28,24},{32,36},... | collective-permute-start | bytes 884744 | tf_op jit(solution)/shard_map/ppermute | solution.py:406
  47.3 12.2 %collective-permute-start.14 = (bf16[2,144,512]{2,1,0:T(8,128)(2,1)}, bf16[2,144,512]{2,1,0:T(8,128)(2,1)S(1)}, u32[]{:S(2)}, u32[]{:S(2)}) collective-permute-start(bf16[2,144,512]{2,1,0:T(8,128)(2,1)} %collective-permute-done.8.refs_5_), channel_id=1, source_target_pairs={{0,32},{4,228},{8,40},{12,236},{16,48},{20,244},{24,56},{28,252},{... | collective-permute-start | bytes 884744 | tf_op jit(solution)/shard_map/ppermute | solution.py:394
  48.9 11.1 %collective-permute-start.15 = (bf16[2,144,512]{2,1,0:T(8,128)(2,1)}, bf16[2,144,512]{2,1,0:T(8,128)(2,1)S(1)}, u32[]{:S(2)}, u32[]{:S(2)}) collective-permute-start(bf16[2,144,512]{2,1,0:T(8,128)(2,1)} %collective-permute-done.7.refs_0_), channel_id=1, source_target_pairs={{0,32},{4,228},{8,40},{12,236},{16,48},{20,244},{24,56},{28,252},{... | collective-permute-start | bytes 884744 | tf_op jit(solution)/shard_map/ppermute | solution.py:394
  53.4 6.8 %collective-permute-start.20 = (bf16[2,144,512]{2,1,0:T(8,128)(2,1)}, bf16[2,144,512]{2,1,0:T(8,128)(2,1)S(1)}, u32[]{:S(2)}, u32[]{:S(2)}) collective-permute-start(bf16[2,144,512]{2,1,0:T(8,128)(2,1)} %collective-permute-done.7.refs_0_), channel_id=1, source_target_pairs={{0,4},{4,0},{8,12},{12,8},{16,20},{20,16},{24,28},{28,24},{32,36},... | collective-permute-start | bytes 884744 | tf_op jit(solution)/shard_map/ppermute | solution.py:406
  53.6 8.1 %copy-start.8 = (f32[256,256]{1,0:T(8,128)S(1)}, f32[256,256]{1,0:T(8,128)}, u32[]{:S(2)}) copy-start(f32[256,256]{1,0:T(8,128)} %get-tuple-element.50.refs_13_) | copy-start | bytes 786436
  59.5 1.8 %collective-permute-start.19 = (bf16[2,144,512]{2,1,0:T(8,128)(2,1)S(1)}, bf16[2,144,512]{2,1,0:T(8,128)(2,1)S(1)}, u32[]{:S(2)}, u32[]{:S(2)}) collective-permute-start(bf16[2,144,512]{2,1,0:T(8,128)(2,1)S(1)} %collective-permute-done.14.refs_1_), channel_id=1, source_target_pairs={{0,4},{4,0},{8,12},{12,8},{16,20},{20,16},{24,28},{28,24},{32,36},... | collective-permute-start | bytes 884744 | tf_op jit(solution)/shard_map/ppermute | solution.py:406
  60.1 1.6 %collective-permute-start.18 = (bf16[2,144,512]{2,1,0:T(8,128)(2,1)S(1)}, bf16[2,144,512]{2,1,0:T(8,128)(2,1)S(1)}, u32[]{:S(2)}, u32[]{:S(2)}) collective-permute-start(bf16[2,144,512]{2,1,0:T(8,128)(2,1)S(1)} %collective-permute-done.15.refs_2_), channel_id=1, source_target_pairs={{0,4},{4,0},{8,12},{12,8},{16,20},{20,16},{24,28},{28,24},{32,36},... | collective-permute-start | bytes 884744 | tf_op jit(solution)/shard_map/ppermute | solution.py:406
  61.7 11.3 %copy-start = (bf16[64,64,512]{2,1,0:T(8,128)(2,1)S(1)}, bf16[64,64,512]{2,1,0:T(8,128)(2,1)}, u32[]{:S(2)}) copy-start(bf16[64,64,512]{2,1,0:T(8,128)(2,1)} %latent_in.3) | copy-start | bytes 12582916
  61.7 11.3 %copy-start.3 = (bf16[64,2048]{1,0:T(8,128)(2,1)S(1)}, bf16[64,2048]{1,0:T(8,128)(2,1)}, u32[]{:S(2)}) copy-start(bf16[64,2048]{1,0:T(8,128)(2,1)} %q_nope_in.1) | copy-start | bytes 786436
  61.7 11.3 %copy-start.5 = (bf16[64,1024]{1,0:T(8,128)(2,1)S(1)}, bf16[64,1024]{1,0:T(8,128)(2,1)}, u32[]{:S(2)}) copy-start(bf16[64,1024]{1,0:T(8,128)(2,1)} %q_rope_in.1) | copy-start | bytes 393220
  61.8 11.2 %copy-start.6 = (bf16[64,4096]{1,0:T(8,128)(2,1)S(1)}, bf16[64,4096]{1,0:T(8,128)(2,1)}, u32[]{:S(2)}) copy-start(bf16[64,4096]{1,0:T(8,128)(2,1)} %rope_in.3) | copy-start | bytes 1572868
  61.8 11.2 %copy-start.13 = (s32[64]{0:T(128)S(1)}, s32[64]{0:T(128)}, u32[]{:S(2)}) copy-start(s32[64]{0:T(128)} %param.21) | copy-start | bytes 772
  69.3 15.0 %collective-permute-start.22 = (bf16[64,2176]{1,0:T(8,128)(2,1)S(1)}, bf16[64,2176]{1,0:T(8,128)(2,1)S(1)}, u32[]{:S(2)}, u32[]{:S(2)}) collective-permute-start(bf16[64,2176]{1,0:T(8,128)(2,1)S(1)} %get-tuple-element.53), channel_id=1, source_target_pairs={{0,24},{4,12},{8,0},{12,20},{16,8},{20,28},{24,16},{28,4},{32,56},... | collective-permute-start | bytes 835592 | tf_op jit(solution)/shard_map/ppermute | solution.py:398
  69.4 14.9 %collective-permute-start.23 = (bf16[64,2176]{1,0:T(8,128)(2,1)S(1)}, bf16[64,2176]{1,0:T(8,128)(2,1)S(1)}, u32[]{:S(2)}, u32[]{:S(2)}) collective-permute-start(bf16[64,2176]{1,0:T(8,128)(2,1)S(1)} %get-tuple-element.54), channel_id=1, source_target_pairs={{0,16},{4,20},{8,24},{12,28},{16,0},{20,4},{24,8},{28,12},{32,48},... | collective-permute-start | bytes 835592 | tf_op jit(solution)/shard_map/ppermute | solution.py:398
  71.8 13.0 %collective-permute-start.24 = (bf16[64,2176]{1,0:T(8,128)(2,1)S(1)}, bf16[64,2176]{1,0:T(8,128)(2,1)S(1)}, u32[]{:S(2)}, u32[]{:S(2)}) collective-permute-start(bf16[64,2176]{1,0:T(8,128)(2,1)S(1)} %get-tuple-element.55), channel_id=1, source_target_pairs={{0,8},{4,28},{8,16},{12,4},{16,24},{20,12},{24,0},{28,20},{32,40},... | collective-permute-start | bytes 835592 | tf_op jit(solution)/shard_map/ppermute | solution.py:398
  (8 other events, 58.9 us)

commit v5 on v4

--- a/solution.py
+++ b/solution.py
@@ -468,7 +468,7 @@
 
     split = both.reshape(NY, HEADS, NOPE, 128)
     k_part, v_part = split[:, : HEADS // 2], split[:, HEADS // 2 :]
-    k_swap = swap(after(k_part.reshape(NY * HEADS // 2, NOPE, 128), a[3], b[2], q_slots))
+    k_swap = swap(after(k_part.reshape(NY * HEADS // 2, NOPE, 128), a[3], q_slots))
     v_swap = swap(v_part.reshape(NY * HEADS // 2, NOPE, 128))
 
     q_lat = pl.pallas_call(

time: 86.8 us -> 90.6 us (1.044); the launches traced: 86.5 us -> 89.3 us
  waiting for transfers between devices: 8.75 us -> 12.3 us
  starting transfers between devices: 37 us -> 36 us
    ppermute x7, waiting for transfers between devices: 6.25 us -> 10.6 us  [ring_z(): lax.ppermute(a, 'rows', [(row_of(z, x, c), row_of(z + 1 - 2 * c, x, c)) f...]
    ppermute x7, starting transfers between devices: 16.7 us -> 15.1 us  [ring_z(): lax.ppermute(a, 'rows', [(row_of(z, x, c), row_of(z + 1 - 2 * c, x, c)) f...]
  transfers between devices with their start and end apart: 26 -> 26, of which waited for: 7 -> 6; matrix products, arithmetic and copies ran while one was open for 1% -> 1% of each run, Pallas kernels for 31% -> 30%
where the time goes in v5:
time: 90.6 us; the launch traced here: 89.3 us
  Pallas kernels  39.8 us (44%)
  starting transfers between devices  36 us (40%)
  waiting for transfers between devices  12.3 us (14%)
    ppermute x7, starting transfers between devices, ring_z(): lax.ppermute(a, 'rows', [(row_of(z, x, c), row_of(z + 1 - 2 * c, x, c)) f...  15.1 us
    pallas_call x1, Pallas kernels, shards(): pl.pallas_call(suffix_kernel, out_shape=struct(ROWS, RET), in_specs=[SMEM...  11.3 us
    ppermute x7, waiting for transfers between devices, ring_z(): lax.ppermute(a, 'rows', [(row_of(z, x, c), row_of(z + 1 - 2 * c, x, c)) f...  10.6 us
    ppermute x12, starting transfers between devices, swap(): lax.ppermute(a, 'rows', [(row_of(z, x, c), row_of(z, x, 1 - c)) for z, x,...  8.57 us
    pallas_call x1, Pallas kernels, shards(): pl.pallas_call(late_kernel, out_shape=(struct(ROWS, RET),) * 4, in_specs=...  7.53 us
    ppermute x6, starting transfers between devices, ring_x(): lax.ppermute(a, 'rows', [(row_of(z, x, c), row_of(z, x + steps * (1 - 2 *...  7.2 us
    pallas_call x1, Pallas kernels, shards(): pl.pallas_call(gather_kernel, out_shape=(struct(SLOTS, QN), struct(HEADS,...  6.07 us
    pallas_call x1, Pallas kernels, shards(): pl.pallas_call(early_kernel, out_shape=(struct(HEADS, EARLY * 16, KVL), s...  5.95 us
  transfers between devices with their start and end apart: 26, of which 6 were waited for; matrix products, arithmetic and copies ran while one was open for 1% of the time, Pallas kernels for 30%

profile of v5, /device:TPU:1, one launch (start us, length us, event | category | flops | bytes accessed | tf_op | source)
XLA Modules:
  0.0 89.3 jit_solution(6058168688750887546)
XLA Ops:
  0.0 4.1 %pack.1 = (bf16[2,144,512]{2,1,0:T(8,128)(2,1)}, bf16[64,3200]{1,0:T(8,128)(2,1)}, bf16[64,128,128]{2,1,0:T(8,128)(2,1)}) custom-call(s32[2,64]{1,0:T(2,128)} %bitcast.14, s32[1,128]{1,0:T(1,128)} %bitcast.15, bf16[2,8192]{1,0:T(2,128)(2,1)} %rope_in.2, bf16[2,128,512]{2,1,0:T(8,128)(2,1)} %latent_in.2, bf16[64,2048]{1,0:T(8,128)(2,1)} %q_nope_in.1, ...), custom_call_target="tpu_custom_call" | custom-call | flops 2000000 | bytes 6000000 | tf_op jit(solution)/shard_map/pack/pallas_call | solution.py:429
  4.1 5.2 %all-to-all-start = ((bf16[64,128,128]{2,1,0:T(8,128)(2,1)}), bf16[64,128,128]{2,1,0:T(8,128)(2,1)S(1)}, u32[]{:S(2)}, u32[]{:S(2)}) async-start(bf16[64,128,128]{2,1,0:T(8,128)(2,1)} %get-tuple-element.31), calls=%async_computation | async-start | bytes 4194304 | tf_op jit(solution)/shard_map/all_to_all | solution.py:424
  9.2 1.9 %collective-permute-start.5 = (bf16[64,3200]{1,0:T(8,128)(2,1)}, bf16[64,3200]{1,0:T(8,128)(2,1)S(1)}, u32[]{:S(2)}, u32[]{:S(2)}) collective-permute-start(bf16[64,3200]{1,0:T(8,128)(2,1)} %get-tuple-element.36.p0), channel_id=1, source_target_pairs={{0,4},{4,0},{8,12},{12,8},{16,20},{20,16},{24,28},{28,24},{32,36},... | collective-permute-start | bytes 1228808 | tf_op jit(solution)/shard_map/ppermute | solution.py:406
  11.3 1.5 %collective-permute-start.1 = (bf16[64,3200]{1,0:T(8,128)(2,1)}, bf16[64,3200]{1,0:T(8,128)(2,1)}, u32[]{:S(2)}, u32[]{:S(2)}) collective-permute-start(bf16[64,3200]{1,0:T(8,128)(2,1)} %get-tuple-element.36.p0), channel_id=1, source_target_pairs={{0,8},{4,28},{8,16},{12,4},{16,24},{20,12},{24,0},{28,20},{32,40},... | collective-permute-start | bytes 1228808 | tf_op jit(solution)/shard_map/ppermute | solution.py:398
  12.8 1.5 %collective-permute-start.6 = (bf16[64,3200]{1,0:T(8,128)(2,1)S(1)}, bf16[64,3200]{1,0:T(8,128)(2,1)}, u32[]{:S(2)}, u32[]{:S(2)}) collective-permute-start(bf16[64,3200]{1,0:T(8,128)(2,1)S(1)} %collective-permute-done.5), channel_id=1, source_target_pairs={{0,8},{4,28},{8,16},{12,4},{16,24},{20,12},{24,0},{28,20},{32,40},... | collective-permute-start | bytes 1228808 | tf_op jit(solution)/shard_map/ppermute | solution.py:398
  14.3 5.6 %collective-permute-start = (bf16[2,144,512]{2,1,0:T(8,128)(2,1)S(1)}, bf16[2,144,512]{2,1,0:T(8,128)(2,1)S(1)}, u32[]{:S(2)}, u32[]{:S(2)}) collective-permute-start(bf16[2,144,512]{2,1,0:T(8,128)(2,1)S(1)} %copy-done.7), channel_id=1, source_target_pairs={{0,32},{4,228},{8,40},{12,236},{16,48},{20,244},{24,56},{28,252},{... | collective-permute-start | bytes 884744 | tf_op jit(solution)/shard_map/ppermute | solution.py:394
  19.8 0.7 collective-permute-start.4
  20.6 2.9 %collective-permute-done.refs_2_ = bf16[2,144,512]{2,1,0:T(8,128)(2,1)S(1)} collective-permute-done((bf16[2,144,512]{2,1,0:T(8,128)(2,1)S(1)}, bf16[2,144,512]{2,1,0:T(8,128)(2,1)S(1)}, u32[]{:S(2)}, u32[]{:S(2)}) %collective-permute-start) | collective-permute-done | bytes 294944 | tf_op jit(solution)/shard_map/ppermute | solution.py:394
  23.5 0.5 collective-permute-start.10
  24.1 1.6 %collective-permute-start.11 = (bf16[64,3200]{1,0:T(8,128)(2,1)}, bf16[64,3200]{1,0:T(8,128)(2,1)}, u32[]{:S(2)}, u32[]{:S(2)}) collective-permute-start(bf16[64,3200]{1,0:T(8,128)(2,1)} %collective-permute-done.6), channel_id=1, source_target_pairs={{0,4},{4,0},{8,12},{12,8},{16,20},{20,16},{24,28},{28,24},{32,36},... | collective-permute-start | bytes 1228808 | tf_op jit(solution)/shard_map/ppermute | solution.py:406
  25.7 4.5 %collective-permute-start.2 = (bf16[2,144,512]{2,1,0:T(8,128)(2,1)S(1)}, bf16[2,144,512]{2,1,0:T(8,128)(2,1)}, u32[]{:S(2)}, u32[]{:S(2)}) collective-permute-start(bf16[2,144,512]{2,1,0:T(8,128)(2,1)S(1)} %collective-permute-done.refs_2_), channel_id=1, source_target_pairs={{0,32},{4,228},{8,40},{12,236},{16,48},{20,244},{24,56},{28,252},{... | collective-permute-start | bytes 884744 | tf_op jit(solution)/shard_map/ppermute | solution.py:394
  30.2 0.5 collective-permute-start.9
  30.7 0.6 pad_add_fusion.place.refs_6_
  31.3 2.5 %collective-permute-done.2.refs_4_ = bf16[2,144,512]{2,1,0:T(8,128)(2,1)} collective-permute-done((bf16[2,144,512]{2,1,0:T(8,128)(2,1)S(1)}, bf16[2,144,512]{2,1,0:T(8,128)(2,1)}, u32[]{:S(2)}, u32[]{:S(2)}) %collective-permute-start.2) | collective-permute-done | bytes 294944 | tf_op jit(solution)/shard_map/ppermute | solution.py:394
  33.8 3.4 %collective-permute-start.7 = (bf16[2,144,512]{2,1,0:T(8,128)(2,1)}, bf16[2,144,512]{2,1,0:T(8,128)(2,1)}, u32[]{:S(2)}, u32[]{:S(2)}) collective-permute-start(bf16[2,144,512]{2,1,0:T(8,128)(2,1)} %collective-permute-done.2.refs_4_), channel_id=1, source_target_pairs={{0,32},{4,228},{8,40},{12,236},{16,48},{20,244},{24,56},{28,252},{... | collective-permute-start | bytes 884744 | tf_op jit(solution)/shard_map/ppermute | solution.py:394
  37.3 6.1 %gather.1 = (bf16[256,2048]{1,0:T(8,128)(2,1)}, bf16[16,256,64]{2,1,0:T(8,128)(2,1)}, f32[256,128]{1,0:T(8,128)}, bf16[256,256]{1,0:T(8,128)(2,1)}, bf16[256,256...) custom-call(s32[4]{0:T(128)} %pad_add_fusion.place.refs_6_, bf16[64,3200]{1,0:T(8,128)(2,1)} %get-tuple-element.36.p0, ...), custom_call_target="tpu_custom_call" | custom-call | flops 3000000 | bytes 9000000 | tf_op jit(solution)/shard_map/gather/pallas_call | solution.py:455
  43.6 0.5 collective-permute-start.21
  44.1 0.7 collective-permute-start.13
  44.9 5.1 %collective-permute-done.13.refs_5_ = bf16[2,144,512]{2,1,0:T(8,128)(2,1)S(1)} collective-permute-done((bf16[2,144,512]{2,1,0:T(8,128)(2,1)S(1)}, bf16[2,144,512]{2,1,0:T(8,128)(2,1)S(1)}, u32[]{:S(2)}, u32[]{:S(2)}) %collective-permute-start.13) | collective-permute-done | bytes 294944 | tf_op jit(solution)/shard_map/ppermute | solution.py:394
  50.0 2.2 %collective-permute-start.16 = (bf16[2,144,512]{2,1,0:T(8,128)(2,1)S(1)}, bf16[2,144,512]{2,1,0:T(8,128)(2,1)S(1)}, u32[]{:S(2)}, u32[]{:S(2)}) collective-permute-start(bf16[2,144,512]{2,1,0:T(8,128)(2,1)S(1)} %collective-permute-done.13.refs_5_), channel_id=1, source_target_pairs={{0,4},{4,0},{8,12},{12,8},{16,20},{20,16},{24,28},{28,24},{32,36},... | collective-permute-start | bytes 884744 | tf_op jit(solution)/shard_map/ppermute | solution.py:406
  52.3 3.2 %queries.1.refs_10_.refs_7_ = bf16[16,256,512]{2,1,0:T(8,128)(2,1)S(1)} custom-call(s32[4]{0:T(128)S(1)} %copy-done.12, bf16[256,2048]{1,0:T(8,128)(2,1)S(1)} %copy-done.2, bf16[64,128,128]{2,1,0:T(8,128)(2,1)S(1)} %all-to-all-done.both.refs_16_, bf16[32,128,128]{2,1,0:T(8,128)(2,1)S(1)} %collective-permute-done.12.k_swap), custom_call_target="tpu_custom_call" | custom-call | flops 3000000 | bytes 9000000 | tf_op jit(solution)/shard_map/queries/pallas_call | solution.py:474
  55.6 0.4 collective-permute-start.20
  56.0 5.9 %early_pages.1 = (bf16[16,160,512]{2,1,0:T(8,128)(2,1)S(1)}, f32[160,128]{1,0:T(8,128)S(1)}) custom-call(bf16[2,144,512]{2,1,0:T(8,128)(2,1)S(1)} %copy-done.7, bf16[2,144,512]{2,1,0:T(8,128)(2,1)S(1)} %collective-permute-done.3.refs_1_, bf16[2,144,512]{2,1,0:T(8,128)(2,1)S(1)} %collective-permute-done.refs_2_, ...), custom_call_target="tpu_custom_call" | custom-call | flops 1000000 | bytes 3000000 | tf_op jit(solution)/shard_map/early_pages/pallas_call | solution.py:490
  62.3 0.9 %collective-permute-start.18 = (bf16[2,144,512]{2,1,0:T(8,128)(2,1)S(1)}, bf16[2,144,512]{2,1,0:T(8,128)(2,1)S(1)}, u32[]{:S(2)}, u32[]{:S(2)}) collective-permute-start(bf16[2,144,512]{2,1,0:T(8,128)(2,1)S(1)} %collective-permute-done.15.refs_2_), channel_id=1, source_target_pairs={{0,4},{4,0},{8,12},{12,8},{16,20},{20,16},{24,28},{28,24},{32,36},... | collective-permute-start | bytes 884744 | tf_op jit(solution)/shard_map/ppermute | solution.py:406
  63.3 0.4 collective-permute-done.19.refs_4_
  63.7 0.8 collective-permute-done.18.refs_3_
  64.5 7.5 %late_pages.1 = (bf16[64,2176]{1,0:T(8,128)(2,1)S(1)}, bf16[64,2176]{1,0:T(8,128)(2,1)S(1)}, bf16[64,2176]{1,0:T(8,128)(2,1)S(1)}, bf16[64,2176]{1,0:T(8,128)(2,1)S(1)}) custom-call(bf16[2,144,512]{2,1,0:T(8,128)(2,1)} %collective-permute-done.7.refs_0_, bf16[2,144,512]{2,1,0:T(8,128)(2,1)S(1)} %collective-permute-done.14.refs_1_, ...), custom_call_target="tpu_custom_call" | custom-call | flops 7000000 | bytes 21000000 | tf_op jit(solution)/shard_map/late_pages/pallas_call | solution.py:504
  72.2 2.6 %collective-permute-start.23 = (bf16[64,2176]{1,0:T(8,128)(2,1)S(1)}, bf16[64,2176]{1,0:T(8,128)(2,1)S(1)}, u32[]{:S(2)}, u32[]{:S(2)}) collective-permute-start(bf16[64,2176]{1,0:T(8,128)(2,1)S(1)} %get-tuple-element.54), channel_id=1, source_target_pairs={{0,16},{4,20},{8,24},{12,28},{16,0},{20,4},{24,8},{28,12},{32,48},... | collective-permute-start | bytes 835592 | tf_op jit(solution)/shard_map/ppermute | solution.py:398
  74.7 1.0 %collective-permute-start.24 = (bf16[64,2176]{1,0:T(8,128)(2,1)S(1)}, bf16[64,2176]{1,0:T(8,128)(2,1)S(1)}, u32[]{:S(2)}, u32[]{:S(2)}) collective-permute-start(bf16[64,2176]{1,0:T(8,128)(2,1)S(1)} %get-tuple-element.55), channel_id=1, source_target_pairs={{0,8},{4,28},{8,16},{12,4},{16,24},{20,12},{24,0},{28,20},{32,40},... | collective-permute-start | bytes 835592 | tf_op jit(solution)/shard_map/ppermute | solution.py:398
  75.8 11.3 %suffix.1.own = bf16[64,2176]{1,0:T(8,128)(2,1)S(1)} custom-call(s32[4]{0:T(128)S(1)} %copy-done.12, s32[1,64]{1,0:T(1,128)S(1)} %bitcast.11, bf16[64,2048]{1,0:T(8,128)(2,1)S(1)} %copy-done.3, bf16[64,1024]{1,0:T(8,128)(2,1)S(1)} %copy-done.5, bf16[64,64,512]{2,1,0:T(8,128)(2,1)S(1)} %copy-done, bf16[64,4096]{1,0:T(8,128)(2,1)S(1)} %copy-done.6, ...), custom_call_target="tpu_custom_call" | custom-call | flops 8000000 | bytes 24000000 | tf_op jit(solution)/shard_map/suffix/pallas_call | solution.py:521
  87.1 0.5 collective-permute-done.24.r3
  87.6 1.7 %combine.1 = bf16[64,2048]{1,0:T(8,128)(2,1)} custom-call(bf16[64,2176]{1,0:T(8,128)(2,1)S(1)} %suffix.1.own, bf16[64,2176]{1,0:T(8,128)(2,1)S(1)} %get-tuple-element.52.r0, bf16[64,2176]{1,0:T(8,128)(2,1)S(1)} %collective-permute-done.22.r1, bf16[64,2176]{1,0:T(8,128)(2,1)S(1)} %collective-permute-done.23.r2, bf16[64,2176]{1,0:T(8,128)(2,1)S(1)} %collective-permute-done.24.r3), custom_call_target="tpu_custom_call" | custom-call | flops 2000000 | bytes 6000000 | tf_op jit(solution)/shard_map/combine/pallas_call | solution.py:540
  (57 shorter events, 1.0 us)
Async XLA Ops:
  4.1 39.2 %all-to-all-start = ((bf16[64,128,128]{2,1,0:T(8,128)(2,1)}), bf16[64,128,128]{2,1,0:T(8,128)(2,1)S(1)}, u32[]{:S(2)}, u32[]{:S(2)}) async-start(bf16[64,128,128]{2,1,0:T(8,128)(2,1)} %get-tuple-element.31), calls=%async_computation | async-start | bytes 4194304 | tf_op jit(solution)/shard_map/all_to_all | solution.py:424
  9.2 3.5 %collective-permute-start.5 = (bf16[64,3200]{1,0:T(8,128)(2,1)}, bf16[64,3200]{1,0:T(8,128)(2,1)S(1)}, u32[]{:S(2)}, u32[]{:S(2)}) collective-permute-start(bf16[64,3200]{1,0:T(8,128)(2,1)} %get-tuple-element.36.p0), channel_id=1, source_target_pairs={{0,4},{4,0},{8,12},{12,8},{16,20},{20,16},{24,28},{28,24},{32,36},... | collective-permute-start | bytes 1228808 | tf_op jit(solution)/shard_map/ppermute | solution.py:406
  11.2 8.7 %collective-permute-start.3 = (bf16[2,144,512]{2,1,0:T(8,128)(2,1)S(1)}, bf16[2,144,512]{2,1,0:T(8,128)(2,1)S(1)}, u32[]{:S(2)}, u32[]{:S(2)}) collective-permute-start(bf16[2,144,512]{2,1,0:T(8,128)(2,1)S(1)} %copy-done.7), channel_id=1, source_target_pairs={{0,4},{4,0},{8,12},{12,8},{16,20},{20,16},{24,28},{28,24},{32,36},... | collective-permute-start | bytes 884744 | tf_op jit(solution)/shard_map/ppermute | solution.py:406
  11.3 12.2 %collective-permute-start.1 = (bf16[64,3200]{1,0:T(8,128)(2,1)}, bf16[64,3200]{1,0:T(8,128)(2,1)}, u32[]{:S(2)}, u32[]{:S(2)}) collective-permute-start(bf16[64,3200]{1,0:T(8,128)(2,1)} %get-tuple-element.36.p0), channel_id=1, source_target_pairs={{0,8},{4,28},{8,16},{12,4},{16,24},{20,12},{24,0},{28,20},{32,40},... | collective-permute-start | bytes 1228808 | tf_op jit(solution)/shard_map/ppermute | solution.py:398
  12.8 11.3 %collective-permute-start.6 = (bf16[64,3200]{1,0:T(8,128)(2,1)S(1)}, bf16[64,3200]{1,0:T(8,128)(2,1)}, u32[]{:S(2)}, u32[]{:S(2)}) collective-permute-start(bf16[64,3200]{1,0:T(8,128)(2,1)S(1)} %collective-permute-done.5), channel_id=1, source_target_pairs={{0,8},{4,28},{8,16},{12,4},{16,24},{20,12},{24,0},{28,20},{32,40},... | collective-permute-start | bytes 1228808 | tf_op jit(solution)/shard_map/ppermute | solution.py:398
  14.3 9.2 %collective-permute-start = (bf16[2,144,512]{2,1,0:T(8,128)(2,1)S(1)}, bf16[2,144,512]{2,1,0:T(8,128)(2,1)S(1)}, u32[]{:S(2)}, u32[]{:S(2)}) collective-permute-start(bf16[2,144,512]{2,1,0:T(8,128)(2,1)S(1)} %copy-done.7), channel_id=1, source_target_pairs={{0,32},{4,228},{8,40},{12,236},{16,48},{20,244},{24,56},{28,252},{... | collective-permute-start | bytes 884744 | tf_op jit(solution)/shard_map/ppermute | solution.py:394
  19.8 10.3 %collective-permute-start.4 = (bf16[2,144,512]{2,1,0:T(8,128)(2,1)S(1)}, bf16[2,144,512]{2,1,0:T(8,128)(2,1)S(1)}, u32[]{:S(2)}, u32[]{:S(2)}) collective-permute-start(bf16[2,144,512]{2,1,0:T(8,128)(2,1)S(1)} %collective-permute-done.3.refs_1_), channel_id=1, source_target_pairs={{0,32},{4,228},{8,40},{12,236},{16,48},{20,244},{24,56},{28,252},{... | collective-permute-start | bytes 884744 | tf_op jit(solution)/shard_map/ppermute | solution.py:394
  23.5 13.7 %collective-permute-start.10 = (bf16[64,3200]{1,0:T(8,128)(2,1)}, bf16[64,3200]{1,0:T(8,128)(2,1)}, u32[]{:S(2)}, u32[]{:S(2)}) collective-permute-start(bf16[64,3200]{1,0:T(8,128)(2,1)} %collective-permute-done.1.p1), channel_id=1, source_target_pairs={{0,8},{4,28},{8,16},{12,4},{16,24},{20,12},{24,0},{28,20},{32,40},... | collective-permute-start | bytes 1228808 | tf_op jit(solution)/shard_map/ppermute | solution.py:398
  24.1 13.2 %collective-permute-start.11 = (bf16[64,3200]{1,0:T(8,128)(2,1)}, bf16[64,3200]{1,0:T(8,128)(2,1)}, u32[]{:S(2)}, u32[]{:S(2)}) collective-permute-start(bf16[64,3200]{1,0:T(8,128)(2,1)} %collective-permute-done.6), channel_id=1, source_target_pairs={{0,4},{4,0},{8,12},{12,8},{16,20},{20,16},{24,28},{28,24},{32,36},... | collective-permute-start | bytes 1228808 | tf_op jit(solution)/shard_map/ppermute | solution.py:406
  25.7 8.1 %collective-permute-start.2 = (bf16[2,144,512]{2,1,0:T(8,128)(2,1)S(1)}, bf16[2,144,512]{2,1,0:T(8,128)(2,1)}, u32[]{:S(2)}, u32[]{:S(2)}) collective-permute-start(bf16[2,144,512]{2,1,0:T(8,128)(2,1)S(1)} %collective-permute-done.refs_2_), channel_id=1, source_target_pairs={{0,32},{4,228},{8,40},{12,236},{16,48},{20,244},{24,56},{28,252},{... | collective-permute-start | bytes 884744 | tf_op jit(solution)/shard_map/ppermute | solution.py:394
  30.2 7.1 %collective-permute-start.8 = (bf16[2,144,512]{2,1,0:T(8,128)(2,1)S(1)}, bf16[2,144,512]{2,1,0:T(8,128)(2,1)}, u32[]{:S(2)}, u32[]{:S(2)}) collective-permute-start(bf16[2,144,512]{2,1,0:T(8,128)(2,1)S(1)} %collective-permute-done.refs_2_), channel_id=1, source_target_pairs={{0,4},{4,0},{8,12},{12,8},{16,20},{20,16},{24,28},{28,24},{32,36},... | collective-permute-start | bytes 884744 | tf_op jit(solution)/shard_map/ppermute | solution.py:406
  30.2 7.1 %collective-permute-start.9 = (bf16[2,144,512]{2,1,0:T(8,128)(2,1)S(1)}, bf16[2,144,512]{2,1,0:T(8,128)(2,1)}, u32[]{:S(2)}, u32[]{:S(2)}) collective-permute-start(bf16[2,144,512]{2,1,0:T(8,128)(2,1)S(1)} %collective-permute-done.4.refs_3_), channel_id=1, source_target_pairs={{0,4},{4,0},{8,12},{12,8},{16,20},{20,16},{24,28},{28,24},{32,36},... | collective-permute-start | bytes 884744 | tf_op jit(solution)/shard_map/ppermute | solution.py:406
  33.8 9.7 %collective-permute-start.7 = (bf16[2,144,512]{2,1,0:T(8,128)(2,1)}, bf16[2,144,512]{2,1,0:T(8,128)(2,1)}, u32[]{:S(2)}, u32[]{:S(2)}) collective-permute-start(bf16[2,144,512]{2,1,0:T(8,128)(2,1)} %collective-permute-done.2.refs_4_), channel_id=1, source_target_pairs={{0,32},{4,228},{8,40},{12,236},{16,48},{20,244},{24,56},{28,252},{... | collective-permute-start | bytes 884744 | tf_op jit(solution)/shard_map/ppermute | solution.py:394
  43.5 8.7 %collective-permute-start.12 = (bf16[32,128,128]{2,1,0:T(8,128)(2,1)S(1)}, bf16[32,128,128]{2,1,0:T(8,128)(2,1)S(1)}, u32[]{:S(2)}, u32[]{:S(2)}) collective-permute-start(bf16[32,128,128]{2,1,0:T(8,128)(2,1)S(1)} %bitcast.13), channel_id=1, source_target_pairs={{0,4},{4,0},{8,12},{12,8},{16,20},{20,16},{24,28},{28,24},{32,36},... | collective-permute-start | bytes 3145736 | tf_op jit(solution)/shard_map/ppermute | solution.py:406
  43.6 12.4 %copy-start.1 = (bf16[16,256,64]{2,1,0:T(8,128)(2,1)S(1)}, bf16[16,256,64]{2,1,0:T(8,128)(2,1)}, u32[]{:S(2)}) copy-start(bf16[16,256,64]{2,1,0:T(8,128)(2,1)} %get-tuple-element.42.refs_11_.refs_8_) | copy-start | bytes 1572868
  43.6 12.4 %copy-start.4 = (f32[256,128]{1,0:T(8,128)S(1)}, f32[256,128]{1,0:T(8,128)}, u32[]{:S(2)}) copy-start(f32[256,128]{1,0:T(8,128)} %get-tuple-element.43.refs_12_.refs_9_) | copy-start | bytes 393220
  43.6 19.6 %collective-permute-start.21 = (bf16[32,128,128]{2,1,0:T(8,128)(2,1)S(1)}, bf16[32,128,128]{2,1,0:T(8,128)(2,1)S(1)}, u32[]{:S(2)}, u32[]{:S(2)}) collective-permute-start(bf16[32,128,128]{2,1,0:T(8,128)(2,1)S(1)} %bitcast.12), channel_id=1, source_target_pairs={{0,4},{4,0},{8,12},{12,8},{16,20},{20,16},{24,28},{28,24},{32,36},... | collective-permute-start | bytes 3145736 | tf_op jit(solution)/shard_map/ppermute | solution.py:406
  44.1 5.9 %collective-permute-start.13 = (bf16[2,144,512]{2,1,0:T(8,128)(2,1)S(1)}, bf16[2,144,512]{2,1,0:T(8,128)(2,1)S(1)}, u32[]{:S(2)}, u32[]{:S(2)}) collective-permute-start(bf16[2,144,512]{2,1,0:T(8,128)(2,1)S(1)} %collective-permute-done.4.refs_3_), channel_id=1, source_target_pairs={{0,32},{4,228},{8,40},{12,236},{16,48},{20,244},{24,56},{28,252},{... | collective-permute-start | bytes 884744 | tf_op jit(solution)/shard_map/ppermute | solution.py:394
  44.8 10.7 %collective-permute-start.17 = (bf16[2,144,512]{2,1,0:T(8,128)(2,1)}, bf16[2,144,512]{2,1,0:T(8,128)(2,1)S(1)}, u32[]{:S(2)}, u32[]{:S(2)}) collective-permute-start(bf16[2,144,512]{2,1,0:T(8,128)(2,1)} %collective-permute-done.2.refs_4_), channel_id=1, source_target_pairs={{0,4},{4,0},{8,12},{12,8},{16,20},{20,16},{24,28},{28,24},{32,36},... | collective-permute-start | bytes 884744 | tf_op jit(solution)/shard_map/ppermute | solution.py:406
  50.0 6.0 %collective-permute-start.16 = (bf16[2,144,512]{2,1,0:T(8,128)(2,1)S(1)}, bf16[2,144,512]{2,1,0:T(8,128)(2,1)S(1)}, u32[]{:S(2)}, u32[]{:S(2)}) collective-permute-start(bf16[2,144,512]{2,1,0:T(8,128)(2,1)S(1)} %collective-permute-done.13.refs_5_), channel_id=1, source_target_pairs={{0,4},{4,0},{8,12},{12,8},{16,20},{20,16},{24,28},{28,24},{32,36},... | collective-permute-start | bytes 884744 | tf_op jit(solution)/shard_map/ppermute | solution.py:406
  52.2 9.8 %collective-permute-start.14 = (bf16[2,144,512]{2,1,0:T(8,128)(2,1)S(1)}, bf16[2,144,512]{2,1,0:T(8,128)(2,1)S(1)}, u32[]{:S(2)}, u32[]{:S(2)}) collective-permute-start(bf16[2,144,512]{2,1,0:T(8,128)(2,1)S(1)} %collective-permute-done.13.refs_5_), channel_id=1, source_target_pairs={{0,32},{4,228},{8,40},{12,236},{16,48},{20,244},{24,56},{28,252},{... | collective-permute-start | bytes 884744 | tf_op jit(solution)/shard_map/ppermute | solution.py:394
  52.2 10.1 %collective-permute-start.15 = (bf16[2,144,512]{2,1,0:T(8,128)(2,1)}, bf16[2,144,512]{2,1,0:T(8,128)(2,1)S(1)}, u32[]{:S(2)}, u32[]{:S(2)}) collective-permute-start(bf16[2,144,512]{2,1,0:T(8,128)(2,1)} %collective-permute-done.7.refs_0_), channel_id=1, source_target_pairs={{0,32},{4,228},{8,40},{12,236},{16,48},{20,244},{24,56},{28,252},{... | collective-permute-start | bytes 884744 | tf_op jit(solution)/shard_map/ppermute | solution.py:394
  55.6 7.7 %collective-permute-start.20 = (bf16[2,144,512]{2,1,0:T(8,128)(2,1)}, bf16[2,144,512]{2,1,0:T(8,128)(2,1)S(1)}, u32[]{:S(2)}, u32[]{:S(2)}) collective-permute-start(bf16[2,144,512]{2,1,0:T(8,128)(2,1)} %collective-permute-done.7.refs_0_), channel_id=1, source_target_pairs={{0,4},{4,0},{8,12},{12,8},{16,20},{20,16},{24,28},{28,24},{32,36},... | collective-permute-start | bytes 884744 | tf_op jit(solution)/shard_map/ppermute | solution.py:406
  62.0 1.7 %collective-permute-start.19 = (bf16[2,144,512]{2,1,0:T(8,128)(2,1)S(1)}, bf16[2,144,512]{2,1,0:T(8,128)(2,1)S(1)}, u32[]{:S(2)}, u32[]{:S(2)}) collective-permute-start(bf16[2,144,512]{2,1,0:T(8,128)(2,1)S(1)} %collective-permute-done.14.refs_1_), channel_id=1, source_target_pairs={{0,4},{4,0},{8,12},{12,8},{16,20},{20,16},{24,28},{28,24},{32,36},... | collective-permute-start | bytes 884744 | tf_op jit(solution)/shard_map/ppermute | solution.py:406
  62.3 2.2 %collective-permute-start.18 = (bf16[2,144,512]{2,1,0:T(8,128)(2,1)S(1)}, bf16[2,144,512]{2,1,0:T(8,128)(2,1)S(1)}, u32[]{:S(2)}, u32[]{:S(2)}) collective-permute-start(bf16[2,144,512]{2,1,0:T(8,128)(2,1)S(1)} %collective-permute-done.15.refs_2_), channel_id=1, source_target_pairs={{0,4},{4,0},{8,12},{12,8},{16,20},{20,16},{24,28},{28,24},{32,36},... | collective-permute-start | bytes 884744 | tf_op jit(solution)/shard_map/ppermute | solution.py:406
  64.5 11.3 %copy-start = (bf16[64,64,512]{2,1,0:T(8,128)(2,1)S(1)}, bf16[64,64,512]{2,1,0:T(8,128)(2,1)}, u32[]{:S(2)}) copy-start(bf16[64,64,512]{2,1,0:T(8,128)(2,1)} %latent_in.3) | copy-start | bytes 12582916
  64.5 11.3 %copy-start.3 = (bf16[64,2048]{1,0:T(8,128)(2,1)S(1)}, bf16[64,2048]{1,0:T(8,128)(2,1)}, u32[]{:S(2)}) copy-start(bf16[64,2048]{1,0:T(8,128)(2,1)} %q_nope_in.1) | copy-start | bytes 786436
  64.5 11.3 %copy-start.5 = (bf16[64,1024]{1,0:T(8,128)(2,1)S(1)}, bf16[64,1024]{1,0:T(8,128)(2,1)}, u32[]{:S(2)}) copy-start(bf16[64,1024]{1,0:T(8,128)(2,1)} %q_rope_in.1) | copy-start | bytes 393220
  64.5 11.3 %copy-start.6 = (bf16[64,4096]{1,0:T(8,128)(2,1)S(1)}, bf16[64,4096]{1,0:T(8,128)(2,1)}, u32[]{:S(2)}) copy-start(bf16[64,4096]{1,0:T(8,128)(2,1)} %rope_in.3) | copy-start | bytes 1572868
  72.1 15.0 %collective-permute-start.22 = (bf16[64,2176]{1,0:T(8,128)(2,1)S(1)}, bf16[64,2176]{1,0:T(8,128)(2,1)S(1)}, u32[]{:S(2)}, u32[]{:S(2)}) collective-permute-start(bf16[64,2176]{1,0:T(8,128)(2,1)S(1)} %get-tuple-element.53), channel_id=1, source_target_pairs={{0,24},{4,12},{8,0},{12,20},{16,8},{20,28},{24,16},{28,4},{32,56},... | collective-permute-start | bytes 835592 | tf_op jit(solution)/shard_map/ppermute | solution.py:398
  72.2 14.9 %collective-permute-start.23 = (bf16[64,2176]{1,0:T(8,128)(2,1)S(1)}, bf16[64,2176]{1,0:T(8,128)(2,1)S(1)}, u32[]{:S(2)}, u32[]{:S(2)}) collective-permute-start(bf16[64,2176]{1,0:T(8,128)(2,1)S(1)} %get-tuple-element.54), channel_id=1, source_target_pairs={{0,16},{4,20},{8,24},{12,28},{16,0},{20,4},{24,8},{28,12},{32,48},... | collective-permute-start | bytes 835592 | tf_op jit(solution)/shard_map/ppermute | solution.py:398
  74.7 12.9 %collective-permute-start.24 = (bf16[64,2176]{1,0:T(8,128)(2,1)S(1)}, bf16[64,2176]{1,0:T(8,128)(2,1)S(1)}, u32[]{:S(2)}, u32[]{:S(2)}) collective-permute-start(bf16[64,2176]{1,0:T(8,128)(2,1)S(1)} %get-tuple-element.55), channel_id=1, source_target_pairs={{0,8},{4,28},{8,16},{12,4},{16,24},{20,12},{24,0},{28,20},{32,40},... | collective-permute-start | bytes 835592 | tf_op jit(solution)/shard_map/ppermute | solution.py:398
  (8 other events, 70.2 us)

commit v6 on v4

--- a/solution.py
+++ b/solution.py
@@ -26,7 +26,8 @@
 SLOTS = 256
 PAIRS = 16
 EARLY = 10
-LATE = PAIRS - EARLY
+MID = 4
+LATE = PAIRS - EARLY - MID
 SCALE = (NOPE + ROPE) ** -0.5
 OUT = HEADS * VDIM
 RET = OUT + 128
@@ -153,7 +154,9 @@
             order = jnp.where(away < 3, away, jnp.where(away >= 6, away - 3, away + 2))
             other = jnp.where(lax.bitwise_and(lax.shift_right_logical(slot, 1), 1) != core, 1, 0)
             here = lax.bitwise_and(lax.shift_right_logical(slot, 2), 3) == x
-            at = jnp.where(here, (order * 2 + other) * 16 + peer * 4 + rank, -1)
+            order = order * 2 + other
+            order = jnp.where(order == 13, 15, jnp.where(order == 15, 13, order))
+            at = jnp.where(here, order * 16 + peer * 4 + rank, -1)
             picks[k].append((wide == at).astype(F32))
             bits[k].append(lax.bitwise_and(slot, 1).astype(F32) * jnp.ones((1, 128), F32))
             found.append(jnp.where(here, 1.0, 0.0))
@@ -247,11 +250,11 @@
     lax.fori_loop(0, count // 2, body, 0)
 
 
-def early_kernel(*refs):
-    units = refs[:EARLY]
-    q_lat, q_rot, page_bit, result, logs, held, sems = refs[EARLY:]
+def units_kernel(count, base, *refs):
+    units = refs[:count]
+    q_lat, q_rot, page_bit, result, logs, held, sems = refs[count:]
     start_units(units, held, sems)
-    attend_units(EARLY, 0, units[0], q_lat, q_rot, page_bit, held, sems, result, logs)
+    attend_units(count, base, units[0], q_lat, q_rot, page_bit, held, sems, result, logs)
 
 
 def pack_log(log):
@@ -266,13 +269,13 @@
 def late_kernel(*refs):
     units = refs[:LATE]
     (
-        place, q_lat, q_rot, page_bit, pick, partner, chosen, flags, early, early_logs, weights, v_swap,
+        place, q_lat, q_rot, page_bit, pick, partner, chosen, flags, early, early_logs, mid, mid_logs, weights, v_swap,
         r0, r1, r2, r3, held, result, logs, whole, parts, sems, w_sems,
     ) = refs[LATE:]
     start_units(units, held, sems)
     copies = gather_weights(place, weights, v_swap, 1, whole, w_sems)
-    attend_units(LATE, EARLY, units[0], q_lat, q_rot, page_bit, held, sems, result, logs)
-    log = jnp.concatenate([early_logs[...], logs[...]], axis=0)
+    attend_units(LATE, EARLY + MID, units[0], q_lat, q_rot, page_bit, held, sems, result, logs)
+    log = jnp.concatenate([early_logs[...], mid_logs[...], logs[...]], axis=0)
     other = (flags[:, :128] - 1.0) * (-LOW)
     rest = log
     for _ in range(3):
@@ -287,7 +290,7 @@
     for copy in copies:
         copy.wait()
     for head in range(HEADS):
-        mixed = jnp.concatenate([early[head], result[head]], axis=0)
+        mixed = jnp.concatenate([early[head], mid[head], result[head]], axis=0)
         part = dot(mixed, whole[head], LAST) * weight[:, head : head + 1]
         parts[:, head * VDIM : (head + 1) * VDIM] = part.astype(BF16)
     lane = iota((SLOTS, 128), 1)
@@ -487,24 +490,29 @@
     b_swap.append(swap(b[2]))
     early_units = [a[0], b[0], a[1], b[1], a[2], b[2], b_swap[2], a_swap[2], b_swap[1], a_swap[1]]
 
-    early, early_logs = pl.pallas_call(
-        early_kernel,
-        out_shape=(struct(HEADS, EARLY * 16, KVL), struct(EARLY * 16, 128, dtype=F32)),
-        in_specs=[ANY] * EARLY + [VMEM] * 3,
-        out_specs=(VMEM, VMEM),
-        scratch_shapes=[pltpu.VMEM((EARLY, 2, UNIT, KVL), BF16), pltpu.SemaphoreType.DMA((EARLY,))],
-        compiler_params=params(20),
-        cost_estimate=cost(1),
-        name="early_pages",
-    )(*early_units, q_lat, q_rot, page_bit)
-
+    def attend(units, base, bits, name):
+        count = len(units)
+        return pl.pallas_call(
+            functools.partial(units_kernel, count, base),
+            out_shape=(struct(HEADS, count * 16, KVL), struct(count * 16, 128, dtype=F32)),
+            in_specs=[ANY] * count + [VMEM] * 3,
+            out_specs=(VMEM, VMEM),
+            scratch_shapes=[pltpu.VMEM((count, 2, UNIT, KVL), BF16), pltpu.SemaphoreType.DMA((count,))],
+            compiler_params=params(20),
+            cost_estimate=cost(1 if base == 0 else 3),
+            name=name,
+        )(*units, q_lat, q_rot, bits)
+
+    early, early_logs = attend(early_units, 0, page_bit, "early_pages")
     a_swap.append(swap(after(a[4], early_logs)))
     b_swap.append(swap(after(b[3], early_logs)))
-    late_units = [a[3], b[3], a[4], a_swap[4], b_swap[3], a_swap[3]]
+    mid_units = [a[3], b[3], a[4], a_swap[3]]
+    mid, mid_logs = attend(mid_units, EARLY, after(page_bit, early_logs), "mid_pages")
+    late_units = [b_swap[3], a_swap[4]]
     returns = pl.pallas_call(
         late_kernel,
         out_shape=(struct(ROWS, RET),) * 4,
-        in_specs=[ANY] * LATE + [SMEM] + [VMEM] * 9 + [ANY] * 2,
+        in_specs=[ANY] * LATE + [SMEM] + [VMEM] * 11 + [ANY] * 2,
         out_specs=(VMEM,) * 4,
         scratch_shapes=[
             pltpu.VMEM((LATE, 2, UNIT, KVL), BF16), pltpu.VMEM((HEADS, LATE * 16, KVL), BF16),
@@ -514,7 +522,7 @@
         compiler_params=params(20),
         cost_estimate=cost(7),
         name="late_pages",
-    )(*late_units, place, q_lat, q_rot, page_bit, *ties, early, early_logs, both, v_swap)
+    )(*late_units, place, q_lat, q_rot, page_bit, *ties, early, early_logs, mid, mid_logs, both, v_swap)
 
     backs = [returns[0], back_x(returns[1]), back_x(returns[2], 2), ring_x(returns[3])]
     k_swap, returns = lax.optimization_barrier((k_swap, returns))

time: 86.8 us -> 85.4 us (0.984)
  waiting for transfers between devices: 8.75 us -> 7.13 us
    pallas_call x1 -> x2, Pallas kernels: 5.89 us -> 9.05 us  [attend(): pl.pallas_call(functools.partial(units_kernel, count, base), out_shape=(s...]
    pallas_call x1, Pallas kernels: 7.52 us -> 4.46 us  [shards(): pl.pallas_call(late_kernel, out_shape=(struct(ROWS, RET),) * 4, in_specs=...]
    ppermute x12, waiting for transfers between devices: 1.96 us -> 0.45 us  [swap(): lax.ppermute(a, 'rows', [(row_of(z, x, c), row_of(z, x, 1 - c)) for z, x,...]
  transfers between devices with their start and end apart: 26 -> 26, of which waited for: 7 -> 5; matrix products, arithmetic and copies ran while one was open for 1% -> 1% of each run, Pallas kernels for 31% -> 35%
where the time goes in v6:
time: 85.4 us; the launch traced here: 85.2 us
  Pallas kernels  39.9 us (47%)
  starting transfers between devices  37 us (43%)
  waiting for transfers between devices  7.13 us (8%)
    ppermute x7, starting transfers between devices, ring_z(): lax.ppermute(a, 'rows', [(row_of(z, x, c), row_of(z + 1 - 2 * c, x, c)) f...  16.7 us
    pallas_call x1, Pallas kernels, shards(): pl.pallas_call(suffix_kernel, out_shape=struct(ROWS, RET), in_specs=[SMEM...  11.3 us
    pallas_call x2, Pallas kernels, attend(): pl.pallas_call(functools.partial(units_kernel, count, base), out_shape=(s...  9.05 us
    ppermute x12, starting transfers between devices, swap(): lax.ppermute(a, 'rows', [(row_of(z, x, c), row_of(z, x, 1 - c)) for z, x,...  7.93 us
    ppermute x6, starting transfers between devices, ring_x(): lax.ppermute(a, 'rows', [(row_of(z, x, c), row_of(z, x + steps * (1 - 2 *...  7.2 us
    ppermute x7, waiting for transfers between devices, ring_z(): lax.ppermute(a, 'rows', [(row_of(z, x, c), row_of(z + 1 - 2 * c, x, c)) f...  6.13 us
    pallas_call x1, Pallas kernels, shards(): pl.pallas_call(gather_kernel, out_shape=(struct(SLOTS, QN), struct(HEADS,...  6.08 us
    all_to_all x1, starting transfers between devices, exchange(): return lax.all_to_all(a, 'proj', split_axis=0, concat_axis=0, tiled=True)  5.16 us
  transfers between devices with their start and end apart: 26, of which 5 were waited for; matrix products, arithmetic and copies ran while one was open for 1% of the time, Pallas kernels for 35%

profile of v6, /device:TPU:1, one launch (start us, length us, event | category | flops | bytes accessed | tf_op | source)
XLA Modules:
  0.0 85.2 jit_solution(17777830568564137018)
XLA Ops:
  0.0 4.1 %pack.1 = (bf16[2,144,512]{2,1,0:T(8,128)(2,1)}, bf16[64,3200]{1,0:T(8,128)(2,1)}, bf16[64,128,128]{2,1,0:T(8,128)(2,1)}) custom-call(s32[2,64]{1,0:T(2,128)} %bitcast.14, s32[1,128]{1,0:T(1,128)} %bitcast.15, bf16[2,8192]{1,0:T(2,128)(2,1)} %rope_in.2, bf16[2,128,512]{2,1,0:T(8,128)(2,1)} %latent_in.2, bf16[64,2048]{1,0:T(8,128)(2,1)} %q_nope_in.1, ...), custom_call_target="tpu_custom_call" | custom-call | flops 2000000 | bytes 6000000 | tf_op jit(solution)/shard_map/pack/pallas_call | solution.py:432
  4.1 5.2 %all-to-all-start = ((bf16[64,128,128]{2,1,0:T(8,128)(2,1)}), bf16[64,128,128]{2,1,0:T(8,128)(2,1)S(1)}, u32[]{:S(2)}, u32[]{:S(2)}) async-start(bf16[64,128,128]{2,1,0:T(8,128)(2,1)} %get-tuple-element.34), calls=%async_computation | async-start | bytes 4194304 | tf_op jit(solution)/shard_map/all_to_all | solution.py:427
  9.2 1.9 %collective-permute-start.5 = (bf16[64,3200]{1,0:T(8,128)(2,1)}, bf16[64,3200]{1,0:T(8,128)(2,1)S(1)}, u32[]{:S(2)}, u32[]{:S(2)}) collective-permute-start(bf16[64,3200]{1,0:T(8,128)(2,1)} %get-tuple-element.40.p0), channel_id=1, source_target_pairs={{0,4},{4,0},{8,12},{12,8},{16,20},{20,16},{24,28},{28,24},{32,36},... | collective-permute-start | bytes 1228808 | tf_op jit(solution)/shard_map/ppermute | solution.py:409
  11.3 1.5 %collective-permute-start.1 = (bf16[64,3200]{1,0:T(8,128)(2,1)}, bf16[64,3200]{1,0:T(8,128)(2,1)}, u32[]{:S(2)}, u32[]{:S(2)}) collective-permute-start(bf16[64,3200]{1,0:T(8,128)(2,1)} %get-tuple-element.40.p0), channel_id=1, source_target_pairs={{0,8},{4,28},{8,16},{12,4},{16,24},{20,12},{24,0},{28,20},{32,40},... | collective-permute-start | bytes 1228808 | tf_op jit(solution)/shard_map/ppermute | solution.py:401
  12.8 1.5 %collective-permute-start.6 = (bf16[64,3200]{1,0:T(8,128)(2,1)S(1)}, bf16[64,3200]{1,0:T(8,128)(2,1)}, u32[]{:S(2)}, u32[]{:S(2)}) collective-permute-start(bf16[64,3200]{1,0:T(8,128)(2,1)S(1)} %collective-permute-done.5), channel_id=1, source_target_pairs={{0,8},{4,28},{8,16},{12,4},{16,24},{20,12},{24,0},{28,20},{32,40},... | collective-permute-start | bytes 1228808 | tf_op jit(solution)/shard_map/ppermute | solution.py:401
  14.3 5.6 %collective-permute-start = (bf16[2,144,512]{2,1,0:T(8,128)(2,1)S(1)}, bf16[2,144,512]{2,1,0:T(8,128)(2,1)S(1)}, u32[]{:S(2)}, u32[]{:S(2)}) collective-permute-start(bf16[2,144,512]{2,1,0:T(8,128)(2,1)S(1)} %copy-done.7), channel_id=1, source_target_pairs={{0,32},{4,228},{8,40},{12,236},{16,48},{20,244},{24,56},{28,252},{... | collective-permute-start | bytes 884744 | tf_op jit(solution)/shard_map/ppermute | solution.py:397
  19.8 0.7 collective-permute-start.4
  20.6 2.9 %collective-permute-done.refs_2_ = bf16[2,144,512]{2,1,0:T(8,128)(2,1)S(1)} collective-permute-done((bf16[2,144,512]{2,1,0:T(8,128)(2,1)S(1)}, bf16[2,144,512]{2,1,0:T(8,128)(2,1)S(1)}, u32[]{:S(2)}, u32[]{:S(2)}) %collective-permute-start) | collective-permute-done | bytes 294944 | tf_op jit(solution)/shard_map/ppermute | solution.py:397
  23.5 0.5 collective-permute-start.11
  24.1 1.6 %collective-permute-start.12 = (bf16[64,3200]{1,0:T(8,128)(2,1)}, bf16[64,3200]{1,0:T(8,128)(2,1)}, u32[]{:S(2)}, u32[]{:S(2)}) collective-permute-start(bf16[64,3200]{1,0:T(8,128)(2,1)} %collective-permute-done.6), channel_id=1, source_target_pairs={{0,4},{4,0},{8,12},{12,8},{16,20},{20,16},{24,28},{28,24},{32,36},... | collective-permute-start | bytes 1228808 | tf_op jit(solution)/shard_map/ppermute | solution.py:409
  25.7 4.5 %collective-permute-start.2 = (bf16[2,144,512]{2,1,0:T(8,128)(2,1)S(1)}, bf16[2,144,512]{2,1,0:T(8,128)(2,1)}, u32[]{:S(2)}, u32[]{:S(2)}) collective-permute-start(bf16[2,144,512]{2,1,0:T(8,128)(2,1)S(1)} %collective-permute-done.refs_2_), channel_id=1, source_target_pairs={{0,32},{4,228},{8,40},{12,236},{16,48},{20,244},{24,56},{28,252},{... | collective-permute-start | bytes 884744 | tf_op jit(solution)/shard_map/ppermute | solution.py:397
  30.2 0.5 collective-permute-start.10
  30.7 0.7 pad_add_fusion.place.refs_2_
  31.3 2.5 %collective-permute-done.2.refs_4_ = bf16[2,144,512]{2,1,0:T(8,128)(2,1)} collective-permute-done((bf16[2,144,512]{2,1,0:T(8,128)(2,1)S(1)}, bf16[2,144,512]{2,1,0:T(8,128)(2,1)}, u32[]{:S(2)}, u32[]{:S(2)}) %collective-permute-start.2) | collective-permute-done | bytes 294944 | tf_op jit(solution)/shard_map/ppermute | solution.py:397
  33.8 3.4 %collective-permute-start.7 = (bf16[2,144,512]{2,1,0:T(8,128)(2,1)}, bf16[2,144,512]{2,1,0:T(8,128)(2,1)}, u32[]{:S(2)}, u32[]{:S(2)}) collective-permute-start(bf16[2,144,512]{2,1,0:T(8,128)(2,1)} %collective-permute-done.2.refs_4_), channel_id=1, source_target_pairs={{0,32},{4,228},{8,40},{12,236},{16,48},{20,244},{24,56},{28,252},{... | collective-permute-start | bytes 884744 | tf_op jit(solution)/shard_map/ppermute | solution.py:397
  37.3 6.1 %gather.1 = (bf16[256,2048]{1,0:T(8,128)(2,1)}, bf16[16,256,64]{2,1,0:T(8,128)(2,1)}, f32[256,128]{1,0:T(8,128)}, bf16[256,256]{1,0:T(8,128)(2,1)}, bf16[256,256...) custom-call(s32[4]{0:T(128)} %pad_add_fusion.place.refs_2_, bf16[64,3200]{1,0:T(8,128)(2,1)} %get-tuple-element.40.p0, ...), custom_call_target="tpu_custom_call" | custom-call | flops 3000000 | bytes 9000000 | tf_op jit(solution)/shard_map/gather/pallas_call | solution.py:458
  43.6 0.7 collective-permute-done.8.refs_5_
  44.3 2.4 %collective-permute-start.13 = (bf16[32,128,128]{2,1,0:T(8,128)(2,1)S(1)}, bf16[32,128,128]{2,1,0:T(8,128)(2,1)S(1)}, u32[]{:S(2)}, u32[]{:S(2)}) collective-permute-start(bf16[32,128,128]{2,1,0:T(8,128)(2,1)S(1)} %bitcast.13), channel_id=1, source_target_pairs={{0,4},{4,0},{8,12},{12,8},{16,20},{20,16},{24,28},{28,24},{32,36},... | collective-permute-start | bytes 3145736 | tf_op jit(solution)/shard_map/ppermute | solution.py:409
  46.7 0.4 collective-permute-start.16
  47.2 1.3 %collective-permute-start.18 = (bf16[2,144,512]{2,1,0:T(8,128)(2,1)}, bf16[2,144,512]{2,1,0:T(8,128)(2,1)S(1)}, u32[]{:S(2)}, u32[]{:S(2)}) collective-permute-start(bf16[2,144,512]{2,1,0:T(8,128)(2,1)} %collective-permute-done.7.refs_0_), channel_id=1, source_target_pairs={{0,32},{4,228},{8,40},{12,236},{16,48},{20,244},{24,56},{28,252},{... | collective-permute-start | bytes 884744 | tf_op jit(solution)/shard_map/ppermute | solution.py:397
  48.5 0.4 collective-permute-done.13.k_swap
  48.9 1.2 %collective-permute-start.14 = (bf16[2,144,512]{2,1,0:T(8,128)(2,1)}, bf16[2,144,512]{2,1,0:T(8,128)(2,1)S(1)}, u32[]{:S(2)}, u32[]{:S(2)}) collective-permute-start(bf16[2,144,512]{2,1,0:T(8,128)(2,1)} %collective-permute-done.8.refs_5_), channel_id=1, source_target_pairs={{0,32},{4,228},{8,40},{12,236},{16,48},{20,244},{24,56},{28,252},{... | collective-permute-start | bytes 884744 | tf_op jit(solution)/shard_map/ppermute | solution.py:397
  50.2 3.2 %queries.1.refs_10_.refs_4_.refs_3_ = bf16[16,256,512]{2,1,0:T(8,128)(2,1)S(1)} custom-call(s32[4]{0:T(128)S(1)} %copy-done.12, bf16[256,2048]{1,0:T(8,128)(2,1)S(1)} %copy-done.3, bf16[64,128,128]{2,1,0:T(8,128)(2,1)S(1)} %all-to-all-done.both.refs_14_, bf16[32,128,128]{2,1,0:T(8,128)(2,1)S(1)} %collective-permute-done.13.k_swap), custom_call_target="tpu_custom_call" | custom-call | flops 3000000 | bytes 9000000 | tf_op jit(solution)/shard_map/queries/pallas_call | solution.py:477
  53.6 5.9 %early_pages.1 = (bf16[16,160,512]{2,1,0:T(8,128)(2,1)S(1)}, f32[160,128]{1,0:T(8,128)S(1)}) custom-call(bf16[2,144,512]{2,1,0:T(8,128)(2,1)S(1)} %copy-done.7, bf16[2,144,512]{2,1,0:T(8,128)(2,1)S(1)} %collective-permute-done.3.refs_1_, bf16[2,144,512]{2,1,0:T(8,128)(2,1)S(1)} %collective-permute-done.refs_2_, ...), custom_call_target="tpu_custom_call" | custom-call | flops 1000000 | bytes 3000000 | tf_op jit(solution)/shard_map/early_pages/pallas_call | solution.py:495
  59.5 0.6 collective-permute-start.19
  60.2 3.2 %mid_pages.1 = (bf16[16,64,512]{2,1,0:T(8,128)(2,1)S(1)}, f32[64,128]{1,0:T(8,128)S(1)}) custom-call(bf16[2,144,512]{2,1,0:T(8,128)(2,1)} %collective-permute-done.7.refs_0_, bf16[2,144,512]{2,1,0:T(8,128)(2,1)S(1)} %collective-permute-done.14.refs_1_, bf16[2,144,512]{2,1,0:T(8,128)(2,1)S(1)} %collective-permute-done.18.refs_2_, ...), custom_call_target="tpu_custom_call" | custom-call | flops 3000000 | bytes 9000000 | tf_op jit(solution)/shard_map/mid_pages/pallas_call | solution.py:495
  63.5 4.5 %late_pages.1 = (bf16[64,2176]{1,0:T(8,128)(2,1)S(1)}, bf16[64,2176]{1,0:T(8,128)(2,1)S(1)}, bf16[64,2176]{1,0:T(8,128)(2,1)S(1)}, bf16[64,2176]{1,0:T(8,128)(2,1)S(1)}) custom-call(bf16[2,144,512]{2,1,0:T(8,128)(2,1)S(1)} %collective-permute-done.17.refs_0_, bf16[2,144,512]{2,1,0:T(8,128)(2,1)S(1)} %collective-permute-done.19.refs_1_, s32[4]{0:T(128)S(1)} %copy-done.12, ...), custom_call_target="tpu_custom_call" | custom-call | flops 7000000 | bytes 21000000 | tf_op jit(solution)/shard_map/late_pages/pallas_call | solution.py:512
  68.0 2.4 %collective-permute-start.23 = (bf16[64,2176]{1,0:T(8,128)(2,1)S(1)}, bf16[64,2176]{1,0:T(8,128)(2,1)S(1)}, u32[]{:S(2)}, u32[]{:S(2)}) collective-permute-start(bf16[64,2176]{1,0:T(8,128)(2,1)S(1)} %get-tuple-element.60), channel_id=1, source_target_pairs={{0,16},{4,20},{8,24},{12,28},{16,0},{20,4},{24,8},{28,12},{32,48},... | collective-permute-start | bytes 835592 | tf_op jit(solution)/shard_map/ppermute | solution.py:401
  70.5 1.2 %collective-permute-start.24 = (bf16[64,2176]{1,0:T(8,128)(2,1)S(1)}, bf16[64,2176]{1,0:T(8,128)(2,1)S(1)}, u32[]{:S(2)}, u32[]{:S(2)}) collective-permute-start(bf16[64,2176]{1,0:T(8,128)(2,1)S(1)} %get-tuple-element.61), channel_id=1, source_target_pairs={{0,8},{4,28},{8,16},{12,4},{16,24},{20,12},{24,0},{28,20},{32,40},... | collective-permute-start | bytes 835592 | tf_op jit(solution)/shard_map/ppermute | solution.py:401
  71.7 11.3 %suffix.1.own = bf16[64,2176]{1,0:T(8,128)(2,1)S(1)} custom-call(s32[4]{0:T(128)S(1)} %copy-done.12, s32[1,64]{1,0:T(1,128)S(1)} %bitcast.11, bf16[64,2048]{1,0:T(8,128)(2,1)S(1)} %copy-done.4, bf16[64,1024]{1,0:T(8,128)(2,1)S(1)} %copy-done.5, bf16[64,64,512]{2,1,0:T(8,128)(2,1)S(1)} %copy-done.1, bf16[64,4096]{1,0:T(8,128)(2,1)S(1)} %copy-done.6, ...), custom_call_target="tpu_custom_call" | custom-call | flops 8000000 | bytes 24000000 | tf_op jit(solution)/shard_map/suffix/pallas_call | solution.py:529
  83.0 0.5 collective-permute-done.24.r3
  83.5 1.7 %combine.1 = bf16[64,2048]{1,0:T(8,128)(2,1)} custom-call(bf16[64,2176]{1,0:T(8,128)(2,1)S(1)} %suffix.1.own, bf16[64,2176]{1,0:T(8,128)(2,1)S(1)} %get-tuple-element.58.r0, bf16[64,2176]{1,0:T(8,128)(2,1)S(1)} %collective-permute-done.22.r1, bf16[64,2176]{1,0:T(8,128)(2,1)S(1)} %collective-permute-done.23.r2, bf16[64,2176]{1,0:T(8,128)(2,1)S(1)} %collective-permute-done.24.r3), custom_call_target="tpu_custom_call" | custom-call | flops 2000000 | bytes 6000000 | tf_op jit(solution)/shard_map/combine/pallas_call | solution.py:548
  (58 shorter events, 0.9 us)
Async XLA Ops:
  4.1 7.1 %copy-start.7 = (bf16[2,144,512]{2,1,0:T(8,128)(2,1)S(1)}, bf16[2,144,512]{2,1,0:T(8,128)(2,1)}, u32[]{:S(2)}) copy-start(bf16[2,144,512]{2,1,0:T(8,128)(2,1)} %get-tuple-element.35.refs_0_) | copy-start | bytes 884740
  4.1 39.3 %all-to-all-start = ((bf16[64,128,128]{2,1,0:T(8,128)(2,1)}), bf16[64,128,128]{2,1,0:T(8,128)(2,1)S(1)}, u32[]{:S(2)}, u32[]{:S(2)}) async-start(bf16[64,128,128]{2,1,0:T(8,128)(2,1)} %get-tuple-element.34), calls=%async_computation | async-start | bytes 4194304 | tf_op jit(solution)/shard_map/all_to_all | solution.py:427
  9.2 3.5 %collective-permute-start.5 = (bf16[64,3200]{1,0:T(8,128)(2,1)}, bf16[64,3200]{1,0:T(8,128)(2,1)S(1)}, u32[]{:S(2)}, u32[]{:S(2)}) collective-permute-start(bf16[64,3200]{1,0:T(8,128)(2,1)} %get-tuple-element.40.p0), channel_id=1, source_target_pairs={{0,4},{4,0},{8,12},{12,8},{16,20},{20,16},{24,28},{28,24},{32,36},... | collective-permute-start | bytes 1228808 | tf_op jit(solution)/shard_map/ppermute | solution.py:409
  11.2 8.7 %collective-permute-start.3 = (bf16[2,144,512]{2,1,0:T(8,128)(2,1)S(1)}, bf16[2,144,512]{2,1,0:T(8,128)(2,1)S(1)}, u32[]{:S(2)}, u32[]{:S(2)}) collective-permute-start(bf16[2,144,512]{2,1,0:T(8,128)(2,1)S(1)} %copy-done.7), channel_id=1, source_target_pairs={{0,4},{4,0},{8,12},{12,8},{16,20},{20,16},{24,28},{28,24},{32,36},... | collective-permute-start | bytes 884744 | tf_op jit(solution)/shard_map/ppermute | solution.py:409
  11.3 12.2 %collective-permute-start.1 = (bf16[64,3200]{1,0:T(8,128)(2,1)}, bf16[64,3200]{1,0:T(8,128)(2,1)}, u32[]{:S(2)}, u32[]{:S(2)}) collective-permute-start(bf16[64,3200]{1,0:T(8,128)(2,1)} %get-tuple-element.40.p0), channel_id=1, source_target_pairs={{0,8},{4,28},{8,16},{12,4},{16,24},{20,12},{24,0},{28,20},{32,40},... | collective-permute-start | bytes 1228808 | tf_op jit(solution)/shard_map/ppermute | solution.py:401
  12.8 11.3 %collective-permute-start.6 = (bf16[64,3200]{1,0:T(8,128)(2,1)S(1)}, bf16[64,3200]{1,0:T(8,128)(2,1)}, u32[]{:S(2)}, u32[]{:S(2)}) collective-permute-start(bf16[64,3200]{1,0:T(8,128)(2,1)S(1)} %collective-permute-done.5), channel_id=1, source_target_pairs={{0,8},{4,28},{8,16},{12,4},{16,24},{20,12},{24,0},{28,20},{32,40},... | collective-permute-start | bytes 1228808 | tf_op jit(solution)/shard_map/ppermute | solution.py:401
  14.3 9.2 %collective-permute-start = (bf16[2,144,512]{2,1,0:T(8,128)(2,1)S(1)}, bf16[2,144,512]{2,1,0:T(8,128)(2,1)S(1)}, u32[]{:S(2)}, u32[]{:S(2)}) collective-permute-start(bf16[2,144,512]{2,1,0:T(8,128)(2,1)S(1)} %copy-done.7), channel_id=1, source_target_pairs={{0,32},{4,228},{8,40},{12,236},{16,48},{20,244},{24,56},{28,252},{... | collective-permute-start | bytes 884744 | tf_op jit(solution)/shard_map/ppermute | solution.py:397
  19.8 10.3 %collective-permute-start.4 = (bf16[2,144,512]{2,1,0:T(8,128)(2,1)S(1)}, bf16[2,144,512]{2,1,0:T(8,128)(2,1)S(1)}, u32[]{:S(2)}, u32[]{:S(2)}) collective-permute-start(bf16[2,144,512]{2,1,0:T(8,128)(2,1)S(1)} %collective-permute-done.3.refs_1_), channel_id=1, source_target_pairs={{0,32},{4,228},{8,40},{12,236},{16,48},{20,244},{24,56},{28,252},{... | collective-permute-start | bytes 884744 | tf_op jit(solution)/shard_map/ppermute | solution.py:397
  23.5 13.8 %collective-permute-start.11 = (bf16[64,3200]{1,0:T(8,128)(2,1)}, bf16[64,3200]{1,0:T(8,128)(2,1)}, u32[]{:S(2)}, u32[]{:S(2)}) collective-permute-start(bf16[64,3200]{1,0:T(8,128)(2,1)} %collective-permute-done.1.p1), channel_id=1, source_target_pairs={{0,8},{4,28},{8,16},{12,4},{16,24},{20,12},{24,0},{28,20},{32,40},... | collective-permute-start | bytes 1228808 | tf_op jit(solution)/shard_map/ppermute | solution.py:401
  24.1 13.2 %collective-permute-start.12 = (bf16[64,3200]{1,0:T(8,128)(2,1)}, bf16[64,3200]{1,0:T(8,128)(2,1)}, u32[]{:S(2)}, u32[]{:S(2)}) collective-permute-start(bf16[64,3200]{1,0:T(8,128)(2,1)} %collective-permute-done.6), channel_id=1, source_target_pairs={{0,4},{4,0},{8,12},{12,8},{16,20},{20,16},{24,28},{28,24},{32,36},... | collective-permute-start | bytes 1228808 | tf_op jit(solution)/shard_map/ppermute | solution.py:409
  25.7 8.1 %collective-permute-start.2 = (bf16[2,144,512]{2,1,0:T(8,128)(2,1)S(1)}, bf16[2,144,512]{2,1,0:T(8,128)(2,1)}, u32[]{:S(2)}, u32[]{:S(2)}) collective-permute-start(bf16[2,144,512]{2,1,0:T(8,128)(2,1)S(1)} %collective-permute-done.refs_2_), channel_id=1, source_target_pairs={{0,32},{4,228},{8,40},{12,236},{16,48},{20,244},{24,56},{28,252},{... | collective-permute-start | bytes 884744 | tf_op jit(solution)/shard_map/ppermute | solution.py:397
  30.1 7.1 %collective-permute-start.9 = (bf16[2,144,512]{2,1,0:T(8,128)(2,1)S(1)}, bf16[2,144,512]{2,1,0:T(8,128)(2,1)}, u32[]{:S(2)}, u32[]{:S(2)}) collective-permute-start(bf16[2,144,512]{2,1,0:T(8,128)(2,1)S(1)} %collective-permute-done.refs_2_), channel_id=1, source_target_pairs={{0,4},{4,0},{8,12},{12,8},{16,20},{20,16},{24,28},{28,24},{32,36},... | collective-permute-start | bytes 884744 | tf_op jit(solution)/shard_map/ppermute | solution.py:409
  30.2 7.1 %collective-permute-start.10 = (bf16[2,144,512]{2,1,0:T(8,128)(2,1)S(1)}, bf16[2,144,512]{2,1,0:T(8,128)(2,1)}, u32[]{:S(2)}, u32[]{:S(2)}) collective-permute-start(bf16[2,144,512]{2,1,0:T(8,128)(2,1)S(1)} %collective-permute-done.4.refs_3_), channel_id=1, source_target_pairs={{0,4},{4,0},{8,12},{12,8},{16,20},{20,16},{24,28},{28,24},{32,36},... | collective-permute-start | bytes 884744 | tf_op jit(solution)/shard_map/ppermute | solution.py:409
  33.8 9.7 %collective-permute-start.7 = (bf16[2,144,512]{2,1,0:T(8,128)(2,1)}, bf16[2,144,512]{2,1,0:T(8,128)(2,1)}, u32[]{:S(2)}, u32[]{:S(2)}) collective-permute-start(bf16[2,144,512]{2,1,0:T(8,128)(2,1)} %collective-permute-done.2.refs_4_), channel_id=1, source_target_pairs={{0,32},{4,228},{8,40},{12,236},{16,48},{20,244},{24,56},{28,252},{... | collective-permute-start | bytes 884744 | tf_op jit(solution)/shard_map/ppermute | solution.py:397
  37.2 7.0 %collective-permute-start.8 = (bf16[2,144,512]{2,1,0:T(8,128)(2,1)S(1)}, bf16[2,144,512]{2,1,0:T(8,128)(2,1)}, u32[]{:S(2)}, u32[]{:S(2)}) collective-permute-start(bf16[2,144,512]{2,1,0:T(8,128)(2,1)S(1)} %collective-permute-done.4.refs_3_), channel_id=1, source_target_pairs={{0,32},{4,228},{8,40},{12,236},{16,48},{20,244},{24,56},{28,252},{... | collective-permute-start | bytes 884744 | tf_op jit(solution)/shard_map/ppermute | solution.py:397
  44.3 4.7 %collective-permute-start.13 = (bf16[32,128,128]{2,1,0:T(8,128)(2,1)S(1)}, bf16[32,128,128]{2,1,0:T(8,128)(2,1)S(1)}, u32[]{:S(2)}, u32[]{:S(2)}) collective-permute-start(bf16[32,128,128]{2,1,0:T(8,128)(2,1)S(1)} %bitcast.13), channel_id=1, source_target_pairs={{0,4},{4,0},{8,12},{12,8},{16,20},{20,16},{24,28},{28,24},{32,36},... | collective-permute-start | bytes 3145736 | tf_op jit(solution)/shard_map/ppermute | solution.py:409
  46.7 16.7 %collective-permute-start.21 = (bf16[32,128,128]{2,1,0:T(8,128)(2,1)S(1)}, bf16[32,128,128]{2,1,0:T(8,128)(2,1)S(1)}, u32[]{:S(2)}, u32[]{:S(2)}) collective-permute-start(bf16[32,128,128]{2,1,0:T(8,128)(2,1)S(1)} %bitcast.12), channel_id=1, source_target_pairs={{0,4},{4,0},{8,12},{12,8},{16,20},{20,16},{24,28},{28,24},{32,36},... | collective-permute-start | bytes 3145736 | tf_op jit(solution)/shard_map/ppermute | solution.py:409
  46.7 6.7 %collective-permute-start.16 = (bf16[2,144,512]{2,1,0:T(8,128)(2,1)}, bf16[2,144,512]{2,1,0:T(8,128)(2,1)S(1)}, u32[]{:S(2)}, u32[]{:S(2)}) collective-permute-start(bf16[2,144,512]{2,1,0:T(8,128)(2,1)} %collective-permute-done.2.refs_4_), channel_id=1, source_target_pairs={{0,4},{4,0},{8,12},{12,8},{16,20},{20,16},{24,28},{28,24},{32,36},... | collective-permute-start | bytes 884744 | tf_op jit(solution)/shard_map/ppermute | solution.py:409
  47.2 6.4 %collective-permute-start.15 = (bf16[2,144,512]{2,1,0:T(8,128)(2,1)}, bf16[2,144,512]{2,1,0:T(8,128)(2,1)S(1)}, u32[]{:S(2)}, u32[]{:S(2)}) collective-permute-start(bf16[2,144,512]{2,1,0:T(8,128)(2,1)} %collective-permute-done.8.refs_5_), channel_id=1, source_target_pairs={{0,4},{4,0},{8,12},{12,8},{16,20},{20,16},{24,28},{28,24},{32,36},... | collective-permute-start | bytes 884744 | tf_op jit(solution)/shard_map/ppermute | solution.py:409
  47.2 12.2 %collective-permute-start.18 = (bf16[2,144,512]{2,1,0:T(8,128)(2,1)}, bf16[2,144,512]{2,1,0:T(8,128)(2,1)S(1)}, u32[]{:S(2)}, u32[]{:S(2)}) collective-permute-start(bf16[2,144,512]{2,1,0:T(8,128)(2,1)} %collective-permute-done.7.refs_0_), channel_id=1, source_target_pairs={{0,32},{4,228},{8,40},{12,236},{16,48},{20,244},{24,56},{28,252},{... | collective-permute-start | bytes 884744 | tf_op jit(solution)/shard_map/ppermute | solution.py:397
  48.9 11.1 %collective-permute-start.14 = (bf16[2,144,512]{2,1,0:T(8,128)(2,1)}, bf16[2,144,512]{2,1,0:T(8,128)(2,1)S(1)}, u32[]{:S(2)}, u32[]{:S(2)}) collective-permute-start(bf16[2,144,512]{2,1,0:T(8,128)(2,1)} %collective-permute-done.8.refs_5_), channel_id=1, source_target_pairs={{0,32},{4,228},{8,40},{12,236},{16,48},{20,244},{24,56},{28,252},{... | collective-permute-start | bytes 884744 | tf_op jit(solution)/shard_map/ppermute | solution.py:397
  53.4 6.8 %collective-permute-start.20 = (bf16[2,144,512]{2,1,0:T(8,128)(2,1)}, bf16[2,144,512]{2,1,0:T(8,128)(2,1)S(1)}, u32[]{:S(2)}, u32[]{:S(2)}) collective-permute-start(bf16[2,144,512]{2,1,0:T(8,128)(2,1)} %collective-permute-done.7.refs_0_), channel_id=1, source_target_pairs={{0,4},{4,0},{8,12},{12,8},{16,20},{20,16},{24,28},{28,24},{32,36},... | collective-permute-start | bytes 884744 | tf_op jit(solution)/shard_map/ppermute | solution.py:409
  59.5 3.9 %collective-permute-start.19 = (bf16[2,144,512]{2,1,0:T(8,128)(2,1)S(1)}, bf16[2,144,512]{2,1,0:T(8,128)(2,1)S(1)}, u32[]{:S(2)}, u32[]{:S(2)}) collective-permute-start(bf16[2,144,512]{2,1,0:T(8,128)(2,1)S(1)} %collective-permute-done.18.refs_2_), channel_id=1, source_target_pairs={{0,4},{4,0},{8,12},{12,8},{16,20},{20,16},{24,28},{28,24},{32,36},... | collective-permute-start | bytes 884744 | tf_op jit(solution)/shard_map/ppermute | solution.py:409
  60.1 3.3 %collective-permute-start.17 = (bf16[2,144,512]{2,1,0:T(8,128)(2,1)S(1)}, bf16[2,144,512]{2,1,0:T(8,128)(2,1)S(1)}, u32[]{:S(2)}, u32[]{:S(2)}) collective-permute-start(bf16[2,144,512]{2,1,0:T(8,128)(2,1)S(1)} %collective-permute-done.14.refs_1_), channel_id=1, source_target_pairs={{0,4},{4,0},{8,12},{12,8},{16,20},{20,16},{24,28},{28,24},{32,36},... | collective-permute-start | bytes 884744 | tf_op jit(solution)/shard_map/ppermute | solution.py:409
  63.4 8.2 %copy-start.1 = (bf16[64,64,512]{2,1,0:T(8,128)(2,1)S(1)}, bf16[64,64,512]{2,1,0:T(8,128)(2,1)}, u32[]{:S(2)}) copy-start(bf16[64,64,512]{2,1,0:T(8,128)(2,1)} %latent_in.3) | copy-start | bytes 12582916
  63.4 8.2 %copy-start.4 = (bf16[64,2048]{1,0:T(8,128)(2,1)S(1)}, bf16[64,2048]{1,0:T(8,128)(2,1)}, u32[]{:S(2)}) copy-start(bf16[64,2048]{1,0:T(8,128)(2,1)} %q_nope_in.1) | copy-start | bytes 786436
  63.4 8.2 %copy-start.5 = (bf16[64,1024]{1,0:T(8,128)(2,1)S(1)}, bf16[64,1024]{1,0:T(8,128)(2,1)}, u32[]{:S(2)}) copy-start(bf16[64,1024]{1,0:T(8,128)(2,1)} %q_rope_in.1) | copy-start | bytes 393220
  63.5 8.2 %copy-start.6 = (bf16[64,4096]{1,0:T(8,128)(2,1)S(1)}, bf16[64,4096]{1,0:T(8,128)(2,1)}, u32[]{:S(2)}) copy-start(bf16[64,4096]{1,0:T(8,128)(2,1)} %rope_in.3) | copy-start | bytes 1572868
  63.5 8.2 %copy-start.13 = (s32[64]{0:T(128)S(1)}, s32[64]{0:T(128)}, u32[]{:S(2)}) copy-start(s32[64]{0:T(128)} %param.21) | copy-start | bytes 772
  68.0 15.0 %collective-permute-start.22 = (bf16[64,2176]{1,0:T(8,128)(2,1)S(1)}, bf16[64,2176]{1,0:T(8,128)(2,1)S(1)}, u32[]{:S(2)}, u32[]{:S(2)}) collective-permute-start(bf16[64,2176]{1,0:T(8,128)(2,1)S(1)} %get-tuple-element.59), channel_id=1, source_target_pairs={{0,24},{4,12},{8,0},{12,20},{16,8},{20,28},{24,16},{28,4},{32,56},... | collective-permute-start | bytes 835592 | tf_op jit(solution)/shard_map/ppermute | solution.py:401
  68.0 14.9 %collective-permute-start.23 = (bf16[64,2176]{1,0:T(8,128)(2,1)S(1)}, bf16[64,2176]{1,0:T(8,128)(2,1)S(1)}, u32[]{:S(2)}, u32[]{:S(2)}) collective-permute-start(bf16[64,2176]{1,0:T(8,128)(2,1)S(1)} %get-tuple-element.60), channel_id=1, source_target_pairs={{0,16},{4,20},{8,24},{12,28},{16,0},{20,4},{24,8},{28,12},{32,48},... | collective-permute-start | bytes 835592 | tf_op jit(solution)/shard_map/ppermute | solution.py:401
  70.5 13.1 %collective-permute-start.24 = (bf16[64,2176]{1,0:T(8,128)(2,1)S(1)}, bf16[64,2176]{1,0:T(8,128)(2,1)S(1)}, u32[]{:S(2)}, u32[]{:S(2)}) collective-permute-start(bf16[64,2176]{1,0:T(8,128)(2,1)S(1)} %get-tuple-element.61), channel_id=1, source_target_pairs={{0,8},{4,28},{8,16},{12,4},{16,24},{20,12},{24,0},{28,20},{32,40},... | collective-permute-start | bytes 835592 | tf_op jit(solution)/shard_map/ppermute | solution.py:401
  (8 other events, 43.1 us)

commit v7 on v6

--- a/solution.py
+++ b/solution.py
@@ -465,13 +465,13 @@
         out_specs=(VMEM,) * 7,
         scratch_shapes=[pltpu.VMEM(square, BF16)],
         compiler_params=params(60),
-        cost_estimate=cost(3),
+        cost_estimate=cost(0.3),
         name="gather",
     )(place, after(pays[0], a_swap[1], b_swap[1]), *pays[1:])
 
     split = both.reshape(NY, HEADS, NOPE, 128)
     k_part, v_part = split[:, : HEADS // 2], split[:, HEADS // 2 :]
-    k_swap = swap(after(k_part.reshape(NY * HEADS // 2, NOPE, 128), a[3], b[2], q_slots))
+    k_swap = swap(after(k_part.reshape(NY * HEADS // 2, NOPE, 128), a[3], q_slots))
     v_swap = swap(v_part.reshape(NY * HEADS // 2, NOPE, 128))
 
     q_lat = pl.pallas_call(
@@ -483,7 +483,7 @@
         compiler_params=params(20),
         cost_estimate=cost(3),
         name="queries",
-    )(place, q_slots, both, k_swap)
+    )(place, after(q_slots, b[2]), both, k_swap)
 
     a.append(ring_z(after(a[3], b[2], a_pay[2])))
     a_swap += [swap(a[2]), swap(a[3])]

time: 85.4 us -> 89.3 us (1.046); the launches traced: 85.2 us -> 88.1 us
  waiting for transfers between devices: 7.13 us -> 10.9 us
    ppermute x7, waiting for transfers between devices: 6.13 us -> 10.6 us  [ring_z(): lax.ppermute(a, 'rows', [(row_of(z, x, c), row_of(z + 1 - 2 * c, x, c)) f...]
    ppermute x7, starting transfers between devices: 16.7 us -> 15.1 us  [ring_z(): lax.ppermute(a, 'rows', [(row_of(z, x, c), row_of(z + 1 - 2 * c, x, c)) f...]
  transfers between devices with their start and end apart: 26 -> 26, of which waited for: 5 -> 4; matrix products, arithmetic and copies ran while one was open for 1% -> 1% of each run, Pallas kernels for 35% -> 34%
where the time goes in v7:
time: 89.3 us; the launch traced here: 88.1 us
  Pallas kernels  39.9 us (45%)
  starting transfers between devices  36.2 us (41%)
  waiting for transfers between devices  10.9 us (12%)
    ppermute x7, starting transfers between devices, ring_z(): lax.ppermute(a, 'rows', [(row_of(z, x, c), row_of(z + 1 - 2 * c, x, c)) f...  15.1 us
    pallas_call x1, Pallas kernels, shards(): pl.pallas_call(suffix_kernel, out_shape=struct(ROWS, RET), in_specs=[SMEM...  11.3 us
    ppermute x7, waiting for transfers between devices, ring_z(): lax.ppermute(a, 'rows', [(row_of(z, x, c), row_of(z + 1 - 2 * c, x, c)) f...  10.6 us
    pallas_call x2, Pallas kernels, attend(): pl.pallas_call(functools.partial(units_kernel, count, base), out_shape=(s...  9.11 us
    ppermute x12, starting transfers between devices, swap(): lax.ppermute(a, 'rows', [(row_of(z, x, c), row_of(z, x, 1 - c)) for z, x,...  8.78 us
    ppermute x6, starting transfers between devices, ring_x(): lax.ppermute(a, 'rows', [(row_of(z, x, c), row_of(z, x + steps * (1 - 2 *...  7.19 us
    pallas_call x1, Pallas kernels, shards(): pl.pallas_call(gather_kernel, out_shape=(struct(SLOTS, QN), struct(HEADS,...  6.09 us
    all_to_all x1, starting transfers between devices, exchange(): return lax.all_to_all(a, 'proj', split_axis=0, concat_axis=0, tiled=True)  5.16 us
  transfers between devices with their start and end apart: 26, of which 4 were waited for; matrix products, arithmetic and copies ran while one was open for 1% of the time, Pallas kernels for 34%

profile of v7, /device:TPU:1, one launch (start us, length us, event | category | flops | bytes accessed | tf_op | source)
XLA Modules:
  0.0 88.1 jit_solution(16864651122065358173)
XLA Ops:
  0.0 4.1 %pack.1 = (bf16[2,144,512]{2,1,0:T(8,128)(2,1)}, bf16[64,3200]{1,0:T(8,128)(2,1)}, bf16[64,128,128]{2,1,0:T(8,128)(2,1)}) custom-call(s32[2,64]{1,0:T(2,128)} %bitcast.14, s32[1,128]{1,0:T(1,128)} %bitcast.15, bf16[2,8192]{1,0:T(2,128)(2,1)} %rope_in.2, bf16[2,128,512]{2,1,0:T(8,128)(2,1)} %latent_in.2, bf16[64,2048]{1,0:T(8,128)(2,1)} %q_nope_in.1, ...), custom_call_target="tpu_custom_call" | custom-call | flops 2000000 | bytes 6000000 | tf_op jit(solution)/shard_map/pack/pallas_call | solution.py:432
  4.1 5.2 %all-to-all-start = ((bf16[64,128,128]{2,1,0:T(8,128)(2,1)}), bf16[64,128,128]{2,1,0:T(8,128)(2,1)S(1)}, u32[]{:S(2)}, u32[]{:S(2)}) async-start(bf16[64,128,128]{2,1,0:T(8,128)(2,1)} %get-tuple-element.35), calls=%async_computation | async-start | bytes 4194304 | tf_op jit(solution)/shard_map/all_to_all | solution.py:427
  9.2 1.9 %collective-permute-start.5 = (bf16[64,3200]{1,0:T(8,128)(2,1)}, bf16[64,3200]{1,0:T(8,128)(2,1)S(1)}, u32[]{:S(2)}, u32[]{:S(2)}) collective-permute-start(bf16[64,3200]{1,0:T(8,128)(2,1)} %get-tuple-element.40.p0), channel_id=1, source_target_pairs={{0,4},{4,0},{8,12},{12,8},{16,20},{20,16},{24,28},{28,24},{32,36},... | collective-permute-start | bytes 1228808 | tf_op jit(solution)/shard_map/ppermute | solution.py:409
  11.3 1.5 %collective-permute-start.1 = (bf16[64,3200]{1,0:T(8,128)(2,1)}, bf16[64,3200]{1,0:T(8,128)(2,1)}, u32[]{:S(2)}, u32[]{:S(2)}) collective-permute-start(bf16[64,3200]{1,0:T(8,128)(2,1)} %get-tuple-element.40.p0), channel_id=1, source_target_pairs={{0,8},{4,28},{8,16},{12,4},{16,24},{20,12},{24,0},{28,20},{32,40},... | collective-permute-start | bytes 1228808 | tf_op jit(solution)/shard_map/ppermute | solution.py:401
  12.8 1.5 %collective-permute-start.6 = (bf16[64,3200]{1,0:T(8,128)(2,1)S(1)}, bf16[64,3200]{1,0:T(8,128)(2,1)}, u32[]{:S(2)}, u32[]{:S(2)}) collective-permute-start(bf16[64,3200]{1,0:T(8,128)(2,1)S(1)} %collective-permute-done.5), channel_id=1, source_target_pairs={{0,8},{4,28},{8,16},{12,4},{16,24},{20,12},{24,0},{28,20},{32,40},... | collective-permute-start | bytes 1228808 | tf_op jit(solution)/shard_map/ppermute | solution.py:401
  14.3 5.6 %collective-permute-start = (bf16[2,144,512]{2,1,0:T(8,128)(2,1)S(1)}, bf16[2,144,512]{2,1,0:T(8,128)(2,1)S(1)}, u32[]{:S(2)}, u32[]{:S(2)}) collective-permute-start(bf16[2,144,512]{2,1,0:T(8,128)(2,1)S(1)} %copy-done.7), channel_id=1, source_target_pairs={{0,32},{4,228},{8,40},{12,236},{16,48},{20,244},{24,56},{28,252},{... | collective-permute-start | bytes 884744 | tf_op jit(solution)/shard_map/ppermute | solution.py:397
  19.8 0.7 collective-permute-start.4
  20.6 2.9 %collective-permute-done.refs_2_ = bf16[2,144,512]{2,1,0:T(8,128)(2,1)S(1)} collective-permute-done((bf16[2,144,512]{2,1,0:T(8,128)(2,1)S(1)}, bf16[2,144,512]{2,1,0:T(8,128)(2,1)S(1)}, u32[]{:S(2)}, u32[]{:S(2)}) %collective-permute-start) | collective-permute-done | bytes 294944 | tf_op jit(solution)/shard_map/ppermute | solution.py:397
  23.5 0.5 collective-permute-start.10
  24.1 1.6 %collective-permute-start.11 = (bf16[64,3200]{1,0:T(8,128)(2,1)}, bf16[64,3200]{1,0:T(8,128)(2,1)}, u32[]{:S(2)}, u32[]{:S(2)}) collective-permute-start(bf16[64,3200]{1,0:T(8,128)(2,1)} %collective-permute-done.6), channel_id=1, source_target_pairs={{0,4},{4,0},{8,12},{12,8},{16,20},{20,16},{24,28},{28,24},{32,36},... | collective-permute-start | bytes 1228808 | tf_op jit(solution)/shard_map/ppermute | solution.py:409
  25.7 4.5 %collective-permute-start.2 = (bf16[2,144,512]{2,1,0:T(8,128)(2,1)S(1)}, bf16[2,144,512]{2,1,0:T(8,128)(2,1)}, u32[]{:S(2)}, u32[]{:S(2)}) collective-permute-start(bf16[2,144,512]{2,1,0:T(8,128)(2,1)S(1)} %collective-permute-done.refs_2_), channel_id=1, source_target_pairs={{0,32},{4,228},{8,40},{12,236},{16,48},{20,244},{24,56},{28,252},{... | collective-permute-start | bytes 884744 | tf_op jit(solution)/shard_map/ppermute | solution.py:397
  30.2 0.5 collective-permute-start.9
  30.7 0.6 pad_add_fusion.place.refs_2_
  31.3 2.5 %collective-permute-done.2.refs_4_ = bf16[2,144,512]{2,1,0:T(8,128)(2,1)} collective-permute-done((bf16[2,144,512]{2,1,0:T(8,128)(2,1)S(1)}, bf16[2,144,512]{2,1,0:T(8,128)(2,1)}, u32[]{:S(2)}, u32[]{:S(2)}) %collective-permute-start.2) | collective-permute-done | bytes 294944 | tf_op jit(solution)/shard_map/ppermute | solution.py:397
  33.8 3.4 %collective-permute-start.7 = (bf16[2,144,512]{2,1,0:T(8,128)(2,1)}, bf16[2,144,512]{2,1,0:T(8,128)(2,1)}, u32[]{:S(2)}, u32[]{:S(2)}) collective-permute-start(bf16[2,144,512]{2,1,0:T(8,128)(2,1)} %collective-permute-done.2.refs_4_), channel_id=1, source_target_pairs={{0,32},{4,228},{8,40},{12,236},{16,48},{20,244},{24,56},{28,252},{... | collective-permute-start | bytes 884744 | tf_op jit(solution)/shard_map/ppermute | solution.py:397
  37.2 6.1 %gather.1 = (bf16[256,2048]{1,0:T(8,128)(2,1)}, bf16[16,256,64]{2,1,0:T(8,128)(2,1)}, f32[256,128]{1,0:T(8,128)}, bf16[256,256]{1,0:T(8,128)(2,1)}, bf16[256,256...) custom-call(s32[4]{0:T(128)} %pad_add_fusion.place.refs_2_, bf16[64,3200]{1,0:T(8,128)(2,1)} %get-tuple-element.40.p0, ...), custom_call_target="tpu_custom_call" | custom-call | flops 300000 | bytes 900000 | tf_op jit(solution)/shard_map/gather/pallas_call | solution.py:458
  43.6 0.5 collective-permute-start.21
  44.1 0.7 collective-permute-start.13
  44.8 5.1 %collective-permute-done.13.refs_5_ = bf16[2,144,512]{2,1,0:T(8,128)(2,1)S(1)} collective-permute-done((bf16[2,144,512]{2,1,0:T(8,128)(2,1)S(1)}, bf16[2,144,512]{2,1,0:T(8,128)(2,1)S(1)}, u32[]{:S(2)}, u32[]{:S(2)}) %collective-permute-start.13) | collective-permute-done | bytes 294944 | tf_op jit(solution)/shard_map/ppermute | solution.py:397
  50.0 2.2 %collective-permute-start.15 = (bf16[2,144,512]{2,1,0:T(8,128)(2,1)S(1)}, bf16[2,144,512]{2,1,0:T(8,128)(2,1)S(1)}, u32[]{:S(2)}, u32[]{:S(2)}) collective-permute-start(bf16[2,144,512]{2,1,0:T(8,128)(2,1)S(1)} %collective-permute-done.13.refs_5_), channel_id=1, source_target_pairs={{0,4},{4,0},{8,12},{12,8},{16,20},{20,16},{24,28},{28,24},{32,36},... | collective-permute-start | bytes 884744 | tf_op jit(solution)/shard_map/ppermute | solution.py:409
  52.3 3.2 %queries.1.refs_10_.refs_4_.refs_3_ = bf16[16,256,512]{2,1,0:T(8,128)(2,1)S(1)} custom-call(s32[4]{0:T(128)S(1)} %copy-done.12, bf16[256,2048]{1,0:T(8,128)(2,1)S(1)} %copy-done.3, bf16[64,128,128]{2,1,0:T(8,128)(2,1)S(1)} %all-to-all-done.both.refs_14_, bf16[32,128,128]{2,1,0:T(8,128)(2,1)S(1)} %collective-permute-done.12.k_swap), custom_call_target="tpu_custom_call" | custom-call | flops 3000000 | bytes 9000000 | tf_op jit(solution)/shard_map/queries/pallas_call | solution.py:477
  55.6 0.4 collective-permute-start.20
  56.0 5.9 %early_pages.1 = (bf16[16,160,512]{2,1,0:T(8,128)(2,1)S(1)}, f32[160,128]{1,0:T(8,128)S(1)}) custom-call(bf16[2,144,512]{2,1,0:T(8,128)(2,1)S(1)} %copy-done.7, bf16[2,144,512]{2,1,0:T(8,128)(2,1)S(1)} %collective-permute-done.3.refs_1_, bf16[2,144,512]{2,1,0:T(8,128)(2,1)S(1)} %collective-permute-done.refs_2_, ...), custom_call_target="tpu_custom_call" | custom-call | flops 1000000 | bytes 3000000 | tf_op jit(solution)/shard_map/early_pages/pallas_call | solution.py:495
  62.0 0.3 collective-permute-start.19
  62.3 1.2 %collective-permute-start.17 = (bf16[2,144,512]{2,1,0:T(8,128)(2,1)S(1)}, bf16[2,144,512]{2,1,0:T(8,128)(2,1)S(1)}, u32[]{:S(2)}, u32[]{:S(2)}) collective-permute-start(bf16[2,144,512]{2,1,0:T(8,128)(2,1)S(1)} %collective-permute-done.14.refs_1_), channel_id=1, source_target_pairs={{0,4},{4,0},{8,12},{12,8},{16,20},{20,16},{24,28},{28,24},{32,36},... | collective-permute-start | bytes 884744 | tf_op jit(solution)/shard_map/ppermute | solution.py:409
  63.5 3.2 %mid_pages.1 = (bf16[16,64,512]{2,1,0:T(8,128)(2,1)S(1)}, f32[64,128]{1,0:T(8,128)S(1)}) custom-call(bf16[2,144,512]{2,1,0:T(8,128)(2,1)} %collective-permute-done.7.refs_0_, bf16[2,144,512]{2,1,0:T(8,128)(2,1)S(1)} %collective-permute-done.14.refs_1_, bf16[2,144,512]{2,1,0:T(8,128)(2,1)S(1)} %collective-permute-done.18.refs_2_, ...), custom_call_target="tpu_custom_call" | custom-call | flops 3000000 | bytes 9000000 | tf_op jit(solution)/shard_map/mid_pages/pallas_call | solution.py:495
  66.8 4.5 %late_pages.1 = (bf16[64,2176]{1,0:T(8,128)(2,1)S(1)}, bf16[64,2176]{1,0:T(8,128)(2,1)S(1)}, bf16[64,2176]{1,0:T(8,128)(2,1)S(1)}, bf16[64,2176]{1,0:T(8,128)(2,1)S(1)}) custom-call(bf16[2,144,512]{2,1,0:T(8,128)(2,1)S(1)} %collective-permute-done.17.refs_0_, bf16[2,144,512]{2,1,0:T(8,128)(2,1)S(1)} %collective-permute-done.19.refs_1_, s32[4]{0:T(128)S(1)} %copy-done.12, ...), custom_call_target="tpu_custom_call" | custom-call | flops 7000000 | bytes 21000000 | tf_op jit(solution)/shard_map/late_pages/pallas_call | solution.py:512
  71.3 2.6 %collective-permute-start.23 = (bf16[64,2176]{1,0:T(8,128)(2,1)S(1)}, bf16[64,2176]{1,0:T(8,128)(2,1)S(1)}, u32[]{:S(2)}, u32[]{:S(2)}) collective-permute-start(bf16[64,2176]{1,0:T(8,128)(2,1)S(1)} %get-tuple-element.62), channel_id=1, source_target_pairs={{0,16},{4,20},{8,24},{12,28},{16,0},{20,4},{24,8},{28,12},{32,48},... | collective-permute-start | bytes 835592 | tf_op jit(solution)/shard_map/ppermute | solution.py:401
  73.9 1.0 %collective-permute-start.24 = (bf16[64,2176]{1,0:T(8,128)(2,1)S(1)}, bf16[64,2176]{1,0:T(8,128)(2,1)S(1)}, u32[]{:S(2)}, u32[]{:S(2)}) collective-permute-start(bf16[64,2176]{1,0:T(8,128)(2,1)S(1)} %get-tuple-element.63), channel_id=1, source_target_pairs={{0,8},{4,28},{8,16},{12,4},{16,24},{20,12},{24,0},{28,20},{32,40},... | collective-permute-start | bytes 835592 | tf_op jit(solution)/shard_map/ppermute | solution.py:401
  74.9 11.3 %suffix.1.own = bf16[64,2176]{1,0:T(8,128)(2,1)S(1)} custom-call(s32[4]{0:T(128)S(1)} %copy-done.12, s32[1,64]{1,0:T(1,128)S(1)} %bitcast.11, bf16[64,2048]{1,0:T(8,128)(2,1)S(1)} %copy-done.4, bf16[64,1024]{1,0:T(8,128)(2,1)S(1)} %copy-done.5, bf16[64,64,512]{2,1,0:T(8,128)(2,1)S(1)} %copy-done.1, bf16[64,4096]{1,0:T(8,128)(2,1)S(1)} %copy-done.6, ...), custom_call_target="tpu_custom_call" | custom-call | flops 8000000 | bytes 24000000 | tf_op jit(solution)/shard_map/suffix/pallas_call | solution.py:529
  86.3 0.2 collective-permute-done.24.r3
  86.5 1.7 %combine.1 = bf16[64,2048]{1,0:T(8,128)(2,1)} custom-call(bf16[64,2176]{1,0:T(8,128)(2,1)S(1)} %suffix.1.own, bf16[64,2176]{1,0:T(8,128)(2,1)S(1)} %get-tuple-element.60.r0, bf16[64,2176]{1,0:T(8,128)(2,1)S(1)} %collective-permute-done.22.r1, bf16[64,2176]{1,0:T(8,128)(2,1)S(1)} %collective-permute-done.23.r2, bf16[64,2176]{1,0:T(8,128)(2,1)S(1)} %collective-permute-done.24.r3), custom_call_target="tpu_custom_call" | custom-call | flops 2000000 | bytes 6000000 | tf_op jit(solution)/shard_map/combine/pallas_call | solution.py:548
  (58 shorter events, 0.7 us)
Async XLA Ops:
  4.1 39.3 %all-to-all-start = ((bf16[64,128,128]{2,1,0:T(8,128)(2,1)}), bf16[64,128,128]{2,1,0:T(8,128)(2,1)S(1)}, u32[]{:S(2)}, u32[]{:S(2)}) async-start(bf16[64,128,128]{2,1,0:T(8,128)(2,1)} %get-tuple-element.35), calls=%async_computation | async-start | bytes 4194304 | tf_op jit(solution)/shard_map/all_to_all | solution.py:427
  9.2 3.5 %collective-permute-start.5 = (bf16[64,3200]{1,0:T(8,128)(2,1)}, bf16[64,3200]{1,0:T(8,128)(2,1)S(1)}, u32[]{:S(2)}, u32[]{:S(2)}) collective-permute-start(bf16[64,3200]{1,0:T(8,128)(2,1)} %get-tuple-element.40.p0), channel_id=1, source_target_pairs={{0,4},{4,0},{8,12},{12,8},{16,20},{20,16},{24,28},{28,24},{32,36},... | collective-permute-start | bytes 1228808 | tf_op jit(solution)/shard_map/ppermute | solution.py:409
  11.2 8.7 %collective-permute-start.3 = (bf16[2,144,512]{2,1,0:T(8,128)(2,1)S(1)}, bf16[2,144,512]{2,1,0:T(8,128)(2,1)S(1)}, u32[]{:S(2)}, u32[]{:S(2)}) collective-permute-start(bf16[2,144,512]{2,1,0:T(8,128)(2,1)S(1)} %copy-done.7), channel_id=1, source_target_pairs={{0,4},{4,0},{8,12},{12,8},{16,20},{20,16},{24,28},{28,24},{32,36},... | collective-permute-start | bytes 884744 | tf_op jit(solution)/shard_map/ppermute | solution.py:409
  11.3 12.2 %collective-permute-start.1 = (bf16[64,3200]{1,0:T(8,128)(2,1)}, bf16[64,3200]{1,0:T(8,128)(2,1)}, u32[]{:S(2)}, u32[]{:S(2)}) collective-permute-start(bf16[64,3200]{1,0:T(8,128)(2,1)} %get-tuple-element.40.p0), channel_id=1, source_target_pairs={{0,8},{4,28},{8,16},{12,4},{16,24},{20,12},{24,0},{28,20},{32,40},... | collective-permute-start | bytes 1228808 | tf_op jit(solution)/shard_map/ppermute | solution.py:401
  12.8 11.3 %collective-permute-start.6 = (bf16[64,3200]{1,0:T(8,128)(2,1)S(1)}, bf16[64,3200]{1,0:T(8,128)(2,1)}, u32[]{:S(2)}, u32[]{:S(2)}) collective-permute-start(bf16[64,3200]{1,0:T(8,128)(2,1)S(1)} %collective-permute-done.5), channel_id=1, source_target_pairs={{0,8},{4,28},{8,16},{12,4},{16,24},{20,12},{24,0},{28,20},{32,40},... | collective-permute-start | bytes 1228808 | tf_op jit(solution)/shard_map/ppermute | solution.py:401
  14.3 9.2 %collective-permute-start = (bf16[2,144,512]{2,1,0:T(8,128)(2,1)S(1)}, bf16[2,144,512]{2,1,0:T(8,128)(2,1)S(1)}, u32[]{:S(2)}, u32[]{:S(2)}) collective-permute-start(bf16[2,144,512]{2,1,0:T(8,128)(2,1)S(1)} %copy-done.7), channel_id=1, source_target_pairs={{0,32},{4,228},{8,40},{12,236},{16,48},{20,244},{24,56},{28,252},{... | collective-permute-start | bytes 884744 | tf_op jit(solution)/shard_map/ppermute | solution.py:397
  19.8 10.3 %collective-permute-start.4 = (bf16[2,144,512]{2,1,0:T(8,128)(2,1)S(1)}, bf16[2,144,512]{2,1,0:T(8,128)(2,1)S(1)}, u32[]{:S(2)}, u32[]{:S(2)}) collective-permute-start(bf16[2,144,512]{2,1,0:T(8,128)(2,1)S(1)} %collective-permute-done.3.refs_1_), channel_id=1, source_target_pairs={{0,32},{4,228},{8,40},{12,236},{16,48},{20,244},{24,56},{28,252},{... | collective-permute-start | bytes 884744 | tf_op jit(solution)/shard_map/ppermute | solution.py:397
  23.5 13.7 %collective-permute-start.10 = (bf16[64,3200]{1,0:T(8,128)(2,1)}, bf16[64,3200]{1,0:T(8,128)(2,1)}, u32[]{:S(2)}, u32[]{:S(2)}) collective-permute-start(bf16[64,3200]{1,0:T(8,128)(2,1)} %collective-permute-done.1.p1), channel_id=1, source_target_pairs={{0,8},{4,28},{8,16},{12,4},{16,24},{20,12},{24,0},{28,20},{32,40},... | collective-permute-start | bytes 1228808 | tf_op jit(solution)/shard_map/ppermute | solution.py:401
  24.1 13.2 %collective-permute-start.11 = (bf16[64,3200]{1,0:T(8,128)(2,1)}, bf16[64,3200]{1,0:T(8,128)(2,1)}, u32[]{:S(2)}, u32[]{:S(2)}) collective-permute-start(bf16[64,3200]{1,0:T(8,128)(2,1)} %collective-permute-done.6), channel_id=1, source_target_pairs={{0,4},{4,0},{8,12},{12,8},{16,20},{20,16},{24,28},{28,24},{32,36},... | collective-permute-start | bytes 1228808 | tf_op jit(solution)/shard_map/ppermute | solution.py:409
  25.7 8.1 %collective-permute-start.2 = (bf16[2,144,512]{2,1,0:T(8,128)(2,1)S(1)}, bf16[2,144,512]{2,1,0:T(8,128)(2,1)}, u32[]{:S(2)}, u32[]{:S(2)}) collective-permute-start(bf16[2,144,512]{2,1,0:T(8,128)(2,1)S(1)} %collective-permute-done.refs_2_), channel_id=1, source_target_pairs={{0,32},{4,228},{8,40},{12,236},{16,48},{20,244},{24,56},{28,252},{... | collective-permute-start | bytes 884744 | tf_op jit(solution)/shard_map/ppermute | solution.py:397
  30.1 7.1 %collective-permute-start.8 = (bf16[2,144,512]{2,1,0:T(8,128)(2,1)S(1)}, bf16[2,144,512]{2,1,0:T(8,128)(2,1)}, u32[]{:S(2)}, u32[]{:S(2)}) collective-permute-start(bf16[2,144,512]{2,1,0:T(8,128)(2,1)S(1)} %collective-permute-done.refs_2_), channel_id=1, source_target_pairs={{0,4},{4,0},{8,12},{12,8},{16,20},{20,16},{24,28},{28,24},{32,36},... | collective-permute-start | bytes 884744 | tf_op jit(solution)/shard_map/ppermute | solution.py:409
  30.2 7.1 %collective-permute-start.9 = (bf16[2,144,512]{2,1,0:T(8,128)(2,1)S(1)}, bf16[2,144,512]{2,1,0:T(8,128)(2,1)}, u32[]{:S(2)}, u32[]{:S(2)}) collective-permute-start(bf16[2,144,512]{2,1,0:T(8,128)(2,1)S(1)} %collective-permute-done.4.refs_3_), channel_id=1, source_target_pairs={{0,4},{4,0},{8,12},{12,8},{16,20},{20,16},{24,28},{28,24},{32,36},... | collective-permute-start | bytes 884744 | tf_op jit(solution)/shard_map/ppermute | solution.py:409
  33.8 9.7 %collective-permute-start.7 = (bf16[2,144,512]{2,1,0:T(8,128)(2,1)}, bf16[2,144,512]{2,1,0:T(8,128)(2,1)}, u32[]{:S(2)}, u32[]{:S(2)}) collective-permute-start(bf16[2,144,512]{2,1,0:T(8,128)(2,1)} %collective-permute-done.2.refs_4_), channel_id=1, source_target_pairs={{0,32},{4,228},{8,40},{12,236},{16,48},{20,244},{24,56},{28,252},{... | collective-permute-start | bytes 884744 | tf_op jit(solution)/shard_map/ppermute | solution.py:397
  43.3 9.0 %copy-start.3 = (bf16[256,2048]{1,0:T(8,128)(2,1)S(1)}, bf16[256,2048]{1,0:T(8,128)(2,1)}, u32[]{:S(2)}) copy-start(bf16[256,2048]{1,0:T(8,128)(2,1)} %get-tuple-element.45.q_nope) | copy-start | bytes 3145732
  43.3 9.0 %copy-start.12 = (s32[4]{0:T(128)S(1)}, s32[4]{0:T(128)}, u32[]{:S(2)}) copy-start(s32[4]{0:T(128)} %pad_add_fusion.place.refs_2_) | copy-start | bytes 52
  43.5 8.7 %collective-permute-start.12 = (bf16[32,128,128]{2,1,0:T(8,128)(2,1)S(1)}, bf16[32,128,128]{2,1,0:T(8,128)(2,1)S(1)}, u32[]{:S(2)}, u32[]{:S(2)}) collective-permute-start(bf16[32,128,128]{2,1,0:T(8,128)(2,1)S(1)} %bitcast.13), channel_id=1, source_target_pairs={{0,4},{4,0},{8,12},{12,8},{16,20},{20,16},{24,28},{28,24},{32,36},... | collective-permute-start | bytes 3145736 | tf_op jit(solution)/shard_map/ppermute | solution.py:409
  43.6 12.4 %copy-start = (bf16[16,256,64]{2,1,0:T(8,128)(2,1)S(1)}, bf16[16,256,64]{2,1,0:T(8,128)(2,1)}, u32[]{:S(2)}) copy-start(bf16[16,256,64]{2,1,0:T(8,128)(2,1)} %get-tuple-element.46.refs_11_.refs_5_.refs_4_) | copy-start | bytes 1572868
  43.6 12.4 %copy-start.2 = (f32[256,128]{1,0:T(8,128)S(1)}, f32[256,128]{1,0:T(8,128)}, u32[]{:S(2)}) copy-start(f32[256,128]{1,0:T(8,128)} %get-tuple-element.57.refs_12_.refs_6_.refs_5_) | copy-start | bytes 393220
  43.6 23.0 %collective-permute-start.21 = (bf16[32,128,128]{2,1,0:T(8,128)(2,1)S(1)}, bf16[32,128,128]{2,1,0:T(8,128)(2,1)S(1)}, u32[]{:S(2)}, u32[]{:S(2)}) collective-permute-start(bf16[32,128,128]{2,1,0:T(8,128)(2,1)S(1)} %bitcast.12), channel_id=1, source_target_pairs={{0,4},{4,0},{8,12},{12,8},{16,20},{20,16},{24,28},{28,24},{32,36},... | collective-permute-start | bytes 3145736 | tf_op jit(solution)/shard_map/ppermute | solution.py:409
  44.1 5.9 %collective-permute-start.13 = (bf16[2,144,512]{2,1,0:T(8,128)(2,1)S(1)}, bf16[2,144,512]{2,1,0:T(8,128)(2,1)S(1)}, u32[]{:S(2)}, u32[]{:S(2)}) collective-permute-start(bf16[2,144,512]{2,1,0:T(8,128)(2,1)S(1)} %collective-permute-done.4.refs_3_), channel_id=1, source_target_pairs={{0,32},{4,228},{8,40},{12,236},{16,48},{20,244},{24,56},{28,252},{... | collective-permute-start | bytes 884744 | tf_op jit(solution)/shard_map/ppermute | solution.py:397
  44.8 10.8 %collective-permute-start.16 = (bf16[2,144,512]{2,1,0:T(8,128)(2,1)}, bf16[2,144,512]{2,1,0:T(8,128)(2,1)S(1)}, u32[]{:S(2)}, u32[]{:S(2)}) collective-permute-start(bf16[2,144,512]{2,1,0:T(8,128)(2,1)} %collective-permute-done.2.refs_4_), channel_id=1, source_target_pairs={{0,4},{4,0},{8,12},{12,8},{16,20},{20,16},{24,28},{28,24},{32,36},... | collective-permute-start | bytes 884744 | tf_op jit(solution)/shard_map/ppermute | solution.py:409
  50.0 6.0 %collective-permute-start.15 = (bf16[2,144,512]{2,1,0:T(8,128)(2,1)S(1)}, bf16[2,144,512]{2,1,0:T(8,128)(2,1)S(1)}, u32[]{:S(2)}, u32[]{:S(2)}) collective-permute-start(bf16[2,144,512]{2,1,0:T(8,128)(2,1)S(1)} %collective-permute-done.13.refs_5_), channel_id=1, source_target_pairs={{0,4},{4,0},{8,12},{12,8},{16,20},{20,16},{24,28},{28,24},{32,36},... | collective-permute-start | bytes 884744 | tf_op jit(solution)/shard_map/ppermute | solution.py:409
  52.2 9.8 %collective-permute-start.18 = (bf16[2,144,512]{2,1,0:T(8,128)(2,1)}, bf16[2,144,512]{2,1,0:T(8,128)(2,1)S(1)}, u32[]{:S(2)}, u32[]{:S(2)}) collective-permute-start(bf16[2,144,512]{2,1,0:T(8,128)(2,1)} %collective-permute-done.7.refs_0_), channel_id=1, source_target_pairs={{0,32},{4,228},{8,40},{12,236},{16,48},{20,244},{24,56},{28,252},{... | collective-permute-start | bytes 884744 | tf_op jit(solution)/shard_map/ppermute | solution.py:397
  52.2 10.1 %collective-permute-start.14 = (bf16[2,144,512]{2,1,0:T(8,128)(2,1)S(1)}, bf16[2,144,512]{2,1,0:T(8,128)(2,1)S(1)}, u32[]{:S(2)}, u32[]{:S(2)}) collective-permute-start(bf16[2,144,512]{2,1,0:T(8,128)(2,1)S(1)} %collective-permute-done.13.refs_5_), channel_id=1, source_target_pairs={{0,32},{4,228},{8,40},{12,236},{16,48},{20,244},{24,56},{28,252},{... | collective-permute-start | bytes 884744 | tf_op jit(solution)/shard_map/ppermute | solution.py:397
  55.6 7.9 %collective-permute-start.20 = (bf16[2,144,512]{2,1,0:T(8,128)(2,1)}, bf16[2,144,512]{2,1,0:T(8,128)(2,1)S(1)}, u32[]{:S(2)}, u32[]{:S(2)}) collective-permute-start(bf16[2,144,512]{2,1,0:T(8,128)(2,1)} %collective-permute-done.7.refs_0_), channel_id=1, source_target_pairs={{0,4},{4,0},{8,12},{12,8},{16,20},{20,16},{24,28},{28,24},{32,36},... | collective-permute-start | bytes 884744 | tf_op jit(solution)/shard_map/ppermute | solution.py:409
  62.0 4.7 %collective-permute-start.19 = (bf16[2,144,512]{2,1,0:T(8,128)(2,1)S(1)}, bf16[2,144,512]{2,1,0:T(8,128)(2,1)S(1)}, u32[]{:S(2)}, u32[]{:S(2)}) collective-permute-start(bf16[2,144,512]{2,1,0:T(8,128)(2,1)S(1)} %collective-permute-done.18.refs_2_), channel_id=1, source_target_pairs={{0,4},{4,0},{8,12},{12,8},{16,20},{20,16},{24,28},{28,24},{32,36},... | collective-permute-start | bytes 884744 | tf_op jit(solution)/shard_map/ppermute | solution.py:409
  62.3 4.4 %collective-permute-start.17 = (bf16[2,144,512]{2,1,0:T(8,128)(2,1)S(1)}, bf16[2,144,512]{2,1,0:T(8,128)(2,1)S(1)}, u32[]{:S(2)}, u32[]{:S(2)}) collective-permute-start(bf16[2,144,512]{2,1,0:T(8,128)(2,1)S(1)} %collective-permute-done.14.refs_1_), channel_id=1, source_target_pairs={{0,4},{4,0},{8,12},{12,8},{16,20},{20,16},{24,28},{28,24},{32,36},... | collective-permute-start | bytes 884744 | tf_op jit(solution)/shard_map/ppermute | solution.py:409
  66.7 8.2 %copy-start.1 = (bf16[64,64,512]{2,1,0:T(8,128)(2,1)S(1)}, bf16[64,64,512]{2,1,0:T(8,128)(2,1)}, u32[]{:S(2)}) copy-start(bf16[64,64,512]{2,1,0:T(8,128)(2,1)} %latent_in.3) | copy-start | bytes 12582916
  66.7 8.2 %copy-start.4 = (bf16[64,2048]{1,0:T(8,128)(2,1)S(1)}, bf16[64,2048]{1,0:T(8,128)(2,1)}, u32[]{:S(2)}) copy-start(bf16[64,2048]{1,0:T(8,128)(2,1)} %q_nope_in.1) | copy-start | bytes 786436
  71.2 15.0 %collective-permute-start.22 = (bf16[64,2176]{1,0:T(8,128)(2,1)S(1)}, bf16[64,2176]{1,0:T(8,128)(2,1)S(1)}, u32[]{:S(2)}, u32[]{:S(2)}) collective-permute-start(bf16[64,2176]{1,0:T(8,128)(2,1)S(1)} %get-tuple-element.61), channel_id=1, source_target_pairs={{0,24},{4,12},{8,0},{12,20},{16,8},{20,28},{24,16},{28,4},{32,56},... | collective-permute-start | bytes 835592 | tf_op jit(solution)/shard_map/ppermute | solution.py:401
  71.3 14.9 %collective-permute-start.23 = (bf16[64,2176]{1,0:T(8,128)(2,1)S(1)}, bf16[64,2176]{1,0:T(8,128)(2,1)S(1)}, u32[]{:S(2)}, u32[]{:S(2)}) collective-permute-start(bf16[64,2176]{1,0:T(8,128)(2,1)S(1)} %get-tuple-element.62), channel_id=1, source_target_pairs={{0,16},{4,20},{8,24},{12,28},{16,0},{20,4},{24,8},{28,12},{32,48},... | collective-permute-start | bytes 835592 | tf_op jit(solution)/shard_map/ppermute | solution.py:401
  73.9 12.6 %collective-permute-start.24 = (bf16[64,2176]{1,0:T(8,128)(2,1)S(1)}, bf16[64,2176]{1,0:T(8,128)(2,1)S(1)}, u32[]{:S(2)}, u32[]{:S(2)}) collective-permute-start(bf16[64,2176]{1,0:T(8,128)(2,1)S(1)} %get-tuple-element.63), channel_id=1, source_target_pairs={{0,8},{4,28},{8,16},{12,4},{16,24},{20,12},{24,0},{28,20},{32,40},... | collective-permute-start | bytes 835592 | tf_op jit(solution)/shard_map/ppermute | solution.py:401
  (8 other events, 50.5 us)
